TPU v7x, 32 devices: a whole 2x2x4 slice. The times are simulated.
32 devices in a mesh: dp: 16 (over z, y, core), mp: 2 (over x).
Axes of the slice: x: 2, y: 2, z: 4, core: 2. Of those that a mesh axis runs over, the one named last changes fastest.
Arguments:
- image_feat: bfloat16 [2048, 1024], P('dp', 'mp'), may hold values from -6 to 6
- image_proj: bfloat16 [1024, 768], P('mp'), may hold values from -1 to 1
- text_feat: bfloat16 [2048, 768], P('dp', 'mp'), may hold values from -6 to 6
- text_proj: bfloat16 [768, 768], P('mp'), may hold values from -1 to 1
- pair_index: int32 [2048], P('dp'), may hold values from 0 to 2047, each once
- logit_scale: float32 [1], replicated, may hold values from 10 to 100
Outputs:
- row_loss: float32 [2048], P('dp')
- col_loss: float32 [2048], P(('dp', 'mp'))
Inputs may be any that keep to these rules, and one draw needn't show every extreme that they name: `pair_index`: each text index appears exactly once.
All inputs are finite; a program needn't handle non-finite values.
Results may differ from a plain program's by a relative error of at most 0.00091.
Values may be sent and summed in bfloat16 or wider, within the bound.
No kernel may reach another device: no remote copies, remote signals or barrier semaphores. Data moves between devices by JAX's collectives and lax.ppermute only.
A program may use at most 64 MiB of HBM per device.

v0:
```python
import jax
import jax.numpy as jnp
from jax import lax
from jax.sharding import PartitionSpec as P


def joined(value, axis, join):
    pieces = jax.tree.map(lambda part: lax.all_gather(part, axis), value)
    head = jax.tree.map(lambda part: part[0], pieces)
    tail = jax.tree.map(lambda part: part[1:], pieces)
    so_far, _ = lax.scan(lambda so_far, slab: (join(so_far, slab), None), head, tail)
    return so_far


def normalize(raw):
    norm_sq = jnp.sum(raw * raw, axis=1, keepdims=True)
    return (raw / jnp.sqrt(norm_sq + 1e-06)).astype(jnp.bfloat16)


def combine_stats(first, second):
    top = jnp.maximum(first[0], second[0])
    total = first[1] * jnp.exp(first[0] - top) + second[1] * jnp.exp(second[0] - top)
    return (top, total, first[2] + second[2])


def on_device(image_feat, image_proj, text_feat, text_proj, pair_index, logit_scale):
    multiplier = logit_scale[0]
    image_part = jnp.dot(image_feat, image_proj, preferred_element_type=jnp.float32)
    image_emb = normalize(lax.psum(image_part, "mp"))
    text_part = jnp.dot(text_feat, text_proj, preferred_element_type=jnp.float32)
    mp_count = lax.axis_size("mp")
    mp_index = lax.axis_index("mp")
    row_count = text_part.shape[0]
    half_rows = row_count // mp_count
    summed = lax.psum(text_part, "mp")
    own_text = lax.dynamic_slice_in_dim(summed, mp_index * half_rows, half_rows, 0)
    text_emb = normalize(own_text)
    dp_count = lax.axis_size("dp")
    piece = lax.all_gather(text_emb, "dp", axis=0, tiled=True)
    row_max = jnp.full((row_count,), -jnp.inf, jnp.float32)
    row_sum = jnp.zeros((row_count,), jnp.float32)
    width_now = piece.shape[0]
    logits = multiplier * lax.dot_general(
        image_emb, piece, (((1,), (1,)), ((), ())), preferred_element_type=jnp.float32
    )
    local_idx = jnp.arange(width_now, dtype=jnp.int32)
    global_idx = local_idx // half_rows * row_count + mp_index * half_rows + local_idx % half_rows
    matched = pair_index[:, None] == global_idx[None, :]
    picked = jnp.where(matched, logits, 0.0)
    new_max = jnp.max(logits, axis=1)
    row_sum = row_sum * jnp.exp(row_max - new_max) + jnp.sum(
        jnp.exp(logits - new_max[:, None]), axis=1
    )
    row_pos = jnp.sum(picked, axis=1)
    block_max = jnp.max(logits, axis=0)
    block_sum = jnp.sum(jnp.exp(logits - block_max[None, :]), axis=0)
    block_pos = jnp.sum(picked, axis=0)
    col_max = block_max
    col_sum = block_sum
    col_pos = block_pos
    row_max, row_sum, row_pos, col_max, col_sum, col_pos = (
        new_max,
        row_sum,
        row_pos,
        col_max,
        col_sum,
        col_pos,
    )
    row_max, row_sum, row_pos = joined((row_max, row_sum, row_pos), "mp", combine_stats)
    row_loss = row_max + jnp.log(row_sum) - row_pos
    shaped_max = col_max.reshape(dp_count, half_rows)
    shaped_sum = col_sum.reshape(dp_count, half_rows)
    shaped_pos = col_pos.reshape(dp_count, half_rows)
    got_max, got_sum, got_pos = (
        lax.all_to_all(shaped_max, "dp", split_axis=0, concat_axis=0, tiled=True),
        lax.all_to_all(shaped_sum, "dp", split_axis=0, concat_axis=0, tiled=True),
        lax.all_to_all(shaped_pos, "dp", split_axis=0, concat_axis=0, tiled=True),
    )
    top = jnp.max(got_max, axis=0)
    total = jnp.sum(got_sum * jnp.exp(got_max - top[None, :]), axis=0)
    positive = jnp.sum(got_pos, axis=0)
    col_loss = top + jnp.log(total) - positive
    return (row_loss, col_loss)


def solution(mesh):
    in_specs = (P("dp", "mp"), P("mp", None), P("dp", "mp"), P("mp", None), P("dp"), P())
    out_specs = (P("dp"), P(("dp", "mp")))
    return jax.shard_map(
        on_device, mesh=mesh, in_specs=in_specs, out_specs=out_specs, check_vma=False
    )
```

profile of v0, /device:TPU:0, one launch (start us, length us, event | category | flops | bytes accessed | tf_op | source)
XLA Modules:
  0.0 141.9 jit_solution(9192998830763414036)
XLA Ops:
  7.2 0.0 copy-start
  7.2 0.0 copy-start.1
  7.2 0.0 all-reduce.3.cloned.1.call-start
  7.2 1.1 copy-done
  8.3 1.9 %fusion.21 = f32[128,768]{1,0:T(8,128)} fusion(bf16[128,512]{1,0:T(8,128)(2,1)} %param.6, bf16[512,768]{1,0:T(8,128)(2,1)S(1)} %copy-done), kind=kOutput, calls=%fused_computation.44 | convolution fusion | flops 100663296 | bytes 1310720 | tf_op jit(solution)/shard_map/dot_general | solution.py:28
  10.2 0.0 copy-done.1
  10.2 1.9 %fusion.22 = f32[128,768]{1,0:T(8,128)} fusion(bf16[128,384]{1,0:T(8,128)(2,1)} %param.8, bf16[384,768]{1,0:T(8,128)(2,1)S(1)} %copy-done.1), kind=kOutput, calls=%fused_computation.45 | convolution fusion | flops 75497472 | bytes 1081344 | tf_op jit(solution)/shard_map/dot_general | solution.py:30
  12.1 0.0 all-reduce.3.cloned.1.call-update
  12.2 0.0 all-gather.7.cloned.1.call-start
  12.2 37.3 %all-reduce.3.cloned.1.call-done = (f32[128,768]{1,0:T(8,128)}, f32[128,768]{1,0:T(8,128)}) async-done(((f32[128,768]{1,0:T(8,128)}, f32[128,768]{1,0:T(8,128)}), (f32[128,768]{1,0:T(8,128)}, f32[128,768]{1,0:T(8,128)})) %all-reduce.3.cloned.1.call-update) | async-done | bytes 786448 | tf_op jit(solution)/shard_map/psum | solution.py:35
  49.5 1.0 multiply_reduce_fusion.1
  50.6 1.7 %divide_convert_fusion.2 = bf16[64,768]{1,0:T(8,128)(2,1)} fusion(f32[128,768]{1,0:T(8,128)} %get-tuple-element.28, s32[]{:T(128)S(6)} %select_n.27, f32[64]{0:T(128)S(1)} %add_sqrt_fusion), kind=kLoop, calls=%fused_computation.8 | loop fusion | flops 98304 | bytes 295172 | tf_op jit(solution)/shard_map/convert_element_type | solution.py:17
  52.2 0.0 all-gather.7.cloned.1.call-update
  52.9 1.1 multiply_reduce_fusion
  54.0 38.1 %all-gather.7.cloned.1.call-done = bf16[1024,768]{1,0:T(8,128)(2,1)} async-done(((bf16[64,768]{1,0:T(8,128)(2,1)}), bf16[1024,768]{1,0:T(8,128)(2,1)}) %all-gather.7.cloned.1.call-update) | async-done | bytes 1572880 | tf_op jit(solution)/shard_map/all_gather | solution.py:39
  92.1 0.0 copy-start.2
  92.1 2.3 %fusion.20 = (f32[128]{0:T(128)S(1)}, f32[128,1024]{1,0:T(8,128)S(1)}) fusion(bf16[1024,768]{1,0:T(8,128)(2,1)} %all-gather.7.cloned.1.call-done, f32[128,768]{1,0:T(8,128)} %get-tuple-element.29, f32[128]{0:T(128)S(1)} %add_sqrt_fusion.1, f32[]{:T(128)} %bitcast.41), kind=kOutput, calls=%fused_computation.43 | convolution fusion | flops 201785216 | bytes 2491396 | tf_op jit(solution)/shard_map/dot_general | solution.py:43
  94.4 0.2 fusion.19
  94.6 0.7 all_to_all.22
  95.3 3.6 %all-to-all-start = ((f32[16,1,64]{2,1,0:T(1,128)}), f32[16,1,64]{2,1,0:T(1,128)S(1)}, u32[]{:S(2)}, u32[]{:S(2)}) async-start(f32[16,1,64]{2,1,0:T(1,128)} %all_to_all.22), calls=%async_computation | async-start | bytes 16384 | tf_op jit(solution)/shard_map/all_to_all | solution.py:75
  98.9 0.0 copy-done.2
  98.9 0.2 fusion
  99.1 0.7 all_to_all.28
  99.8 5.5 %all-to-all-done = f32[16,1,64]{2,1,0:T(1,128)S(1)} async-done(((f32[16,1,64]{2,1,0:T(1,128)}), f32[16,1,64]{2,1,0:T(1,128)S(1)}, u32[]{:S(2)}, u32[]{:S(2)}) %all-to-all-start) | async-done | bytes 4128 | tf_op jit(solution)/shard_map/all_to_all | solution.py:75
  105.3 3.5 %all-to-all-start.2 = ((f32[16,1,64]{2,1,0:T(1,128)}), f32[16,1,64]{2,1,0:T(1,128)S(1)}, u32[]{:S(2)}, u32[]{:S(2)}) async-start(f32[16,1,64]{2,1,0:T(1,128)} %all_to_all.28), calls=%async_computation.2 | async-start | bytes 16384 | tf_op jit(solution)/shard_map/all_to_all | solution.py:77
  108.8 0.7 all_to_all.24
  109.5 4.2 %all-gather.3 = f32[2,1,128]{2,1,0:T(1,128)S(1)} all-gather(f32[1,1,128]{2,1,0:T(1,128)S(1)} %add_bitcast_fusion), channel_id=1, replica_groups=mesh['dp'=16,'mp'=2] {'mp'}, dimensions={0}, use_global_device_ids=true | all-gather | bytes 1536 | tf_op jit(solution)/shard_map/all_gather | solution.py:8
  113.7 4.2 %all-gather.4 = f32[2,1,128]{2,1,0:T(1,128)S(1)} all-gather(f32[1,1,128]{2,1,0:T(1,128)S(1)} %bitcast.46), channel_id=3, replica_groups=mesh['dp'=16,'mp'=2] {'mp'}, dimensions={0}, use_global_device_ids=true | all-gather | bytes 1536 | tf_op jit(solution)/shard_map/all_gather | solution.py:8
  117.9 4.2 %all-gather.2 = f32[2,1,128]{2,1,0:T(1,128)S(1)} all-gather(f32[1,1,128]{2,1,0:T(1,128)S(1)} %bitcast.45), channel_id=2, replica_groups=mesh['dp'=16,'mp'=2] {'mp'}, dimensions={0}, use_global_device_ids=true | all-gather | bytes 1536 | tf_op jit(solution)/shard_map/all_gather | solution.py:8
  122.1 0.0 all-to-all-done.2
  122.1 6.0 %all-to-all-start.1 = ((f32[16,1,64]{2,1,0:T(1,128)}), f32[16,1,64]{2,1,0:T(1,128)S(1)}, u32[]{:S(2)}, u32[]{:S(2)}) async-start(f32[16,1,64]{2,1,0:T(1,128)} %all_to_all.24), calls=%async_computation.1 | async-start | bytes 16384 | tf_op jit(solution)/shard_map/all_to_all | solution.py:76
  128.1 0.5 fusion.14
  128.7 5.8 %all-to-all-done.1 = f32[16,1,64]{2,1,0:T(1,128)S(1)} async-done(((f32[16,1,64]{2,1,0:T(1,128)}), f32[16,1,64]{2,1,0:T(1,128)S(1)}, u32[]{:S(2)}, u32[]{:S(2)}) %all-to-all-start.1) | async-done | bytes 4128 | tf_op jit(solution)/shard_map/all_to_all | solution.py:76
  134.5 0.5 add_subtract_fusion
  (7 shorter events, 0.1 us)
Async XLA Ops:
  7.2 1.1 copy-start
  7.2 3.1 %copy-start.1 = (bf16[384,768]{1,0:T(8,128)(2,1)S(1)}, bf16[384,768]{1,0:T(8,128)(2,1)}, u32[]{:S(2)}) copy-start(bf16[384,768]{1,0:T(8,128)(2,1)} %param.9) | copy-start | bytes 1769476
  7.2 42.3 %all-reduce.3.cloned.1.call-start = ((), (), s32[]{:S(2)}) async-start(), calls=%async_computation.4 | async-start | bytes 1572864 | tf_op jit(solution)/shard_map/psum | solution.py:35
  12.2 79.9 %all-gather.7.cloned.1.call-start = ((), (), s32[]{:S(2)}) async-start(), calls=%async_computation.3 | async-start | bytes 1671168 | tf_op jit(solution)/shard_map/all_gather | solution.py:39
  92.1 6.8 %copy-start.2 = (s32[128]{0:T(128)S(1)}, s32[128]{0:T(128)}, u32[]{:S(2)}) copy-start(s32[128]{0:T(128)} %param.10) | copy-start | bytes 1540
  95.3 10.0 %all-to-all-start = ((f32[16,1,64]{2,1,0:T(1,128)}), f32[16,1,64]{2,1,0:T(1,128)S(1)}, u32[]{:S(2)}, u32[]{:S(2)}) async-start(f32[16,1,64]{2,1,0:T(1,128)} %all_to_all.22), calls=%async_computation | async-start | bytes 16384 | tf_op jit(solution)/shard_map/all_to_all | solution.py:75
  105.3 16.8 %all-to-all-start.2 = ((f32[16,1,64]{2,1,0:T(1,128)}), f32[16,1,64]{2,1,0:T(1,128)S(1)}, u32[]{:S(2)}, u32[]{:S(2)}) async-start(f32[16,1,64]{2,1,0:T(1,128)} %all_to_all.28), calls=%async_computation.2 | async-start | bytes 16384 | tf_op jit(solution)/shard_map/all_to_all | solution.py:77
  122.1 12.4 %all-to-all-start.1 = ((f32[16,1,64]{2,1,0:T(1,128)}), f32[16,1,64]{2,1,0:T(1,128)S(1)}, u32[]{:S(2)}, u32[]{:S(2)}) async-start(f32[16,1,64]{2,1,0:T(1,128)} %all_to_all.24), calls=%async_computation.1 | async-start | bytes 16384 | tf_op jit(solution)/shard_map/all_to_all | solution.py:76
Sparse Core Ops, SparseCore 0:
  12.3 37.1 all-reduce.2
  52.4 39.6 all-gather.6
where the time goes:
time: 142 us
  waiting for transfers between devices  86.7 us (61%)
  between operations  14.8 us (10%)
  starting transfers between devices  13.1 us (9%)
  blocking collectives  12.6 us (9%)
  matrix products  6.11 us (4%)
  other arithmetic  5.44 us (4%)
  local copies, waits for them, and re-layouts  3.09 us (2%)
    all_gather x1, waiting for transfers between devices, on_device(): piece = lax.all_gather(text_emb, 'dp', axis=0, tiled=True)  38.1 us
    psum x1, waiting for transfers between devices, on_device(): summed = lax.psum(text_part, 'mp')  37.3 us
    all_gather x3, blocking collectives, joined(): pieces = jax.tree.map(lambda part: lax.all_gather(part, axis), value)  12.6 us
    all_to_all x1, starting transfers between devices, on_device(): lax.all_to_all(shaped_sum, 'dp', split_axis=0, concat_axis=0, tiled=True)  5.97 us
    all_to_all x1, waiting for transfers between devices, on_device(): lax.all_to_all(shaped_sum, 'dp', split_axis=0, concat_axis=0, tiled=True)  5.81 us
    all_to_all x1, waiting for transfers between devices, on_device(): lax.all_to_all(shaped_max, 'dp', split_axis=0, concat_axis=0, tiled=True)  5.48 us
    all_to_all x1, starting transfers between devices, on_device(): lax.all_to_all(shaped_max, 'dp', split_axis=0, concat_axis=0, tiled=True)  3.6 us
    all_to_all x1, starting transfers between devices, on_device(): lax.all_to_all(shaped_pos, 'dp', split_axis=0, concat_axis=0, tiled=True)  3.49 us
  transfers between devices with their start and end apart: 5, of which 4 were waited for; matrix products, arithmetic and copies ran while one was open for 1% of the time, Pallas kernels for 0%

commit v1 on v0

v1 whole, which is shorter than its diff:
```python
import jax
import jax.numpy as jnp
from jax import lax
from jax.sharding import PartitionSpec as P


def exchange(value, axis, count, stride):
    return lax.ppermute(value, axis, [(i, i ^ stride) for i in range(count)])


def normalize(raw):
    norm_sq = jnp.sum(raw * raw, axis=1, keepdims=True)
    return (raw / jnp.sqrt(norm_sq + 1e-06)).astype(jnp.bfloat16)


def merge(own, other):
    top = jnp.maximum(own[0], other[0])
    total = jnp.exp(own[0] - top) + jnp.exp(other[0] - top)
    return jnp.stack([top + jnp.log(total), own[1] + other[1]])


def strides(low, high):
    out = []
    while low < high:
        out.append(low)
        low *= 2
    return out


def on_device(image_feat, image_proj, text_feat, text_proj, pair_index, logit_scale):
    dp = lax.axis_size("dp")
    mp = lax.axis_size("mp")
    dp_index = lax.axis_index("dp")
    mp_index = lax.axis_index("mp")
    levels = dp.bit_length() - 1
    far = 1 << (levels // 2)
    near = dp // far
    core = min(2, near)
    rows = image_feat.shape[0]
    half = rows // mp

    def text_rows(owner):
        mine = lax.dynamic_slice_in_dim(text_feat, owner * half, half, 0)
        return jnp.dot(mine, text_proj, preferred_element_type=jnp.float32)

    text_raw = None
    got = [
        exchange(text_rows(mp_index ^ step).astype(jnp.float16), "mp", mp, step)
        for step in range(1, mp)
    ]
    text_raw = text_rows(mp_index)
    image_raw = jnp.dot(image_feat, image_proj, preferred_element_type=jnp.float32)
    for step in strides(1, mp):
        image_raw = image_raw + exchange(image_raw.astype(jnp.float16), "mp", mp, step)
    for part in got:
        text_raw = text_raw + part

    pairs = pair_index[None]
    for stride in strides(core, near):
        pairs = jnp.concatenate([pairs, exchange(pairs, "dp", dp, stride)])

    text_emb = normalize(text_raw)
    texts = [text_emb] + [exchange(text_emb, "dp", dp, near * j) for j in range(1, far)]
    image_emb = normalize(image_raw)[None]
    for stride in strides(core, near):
        image_emb = jnp.concatenate([image_emb, exchange(image_emb, "dp", dp, stride)])
    both = [[text] + [exchange(text, "dp", dp, c) for c in range(1, core)] for text in texts]
    text_all = jnp.concatenate([text for c in range(core) for text in [b[c] for b in both]])

    images = image_emb.reshape(-1, image_emb.shape[-1])
    logits = logit_scale[0] * lax.dot_general(
        images, text_all, (((1,), (1,)), ((), ())), preferred_element_type=jnp.float32
    )
    slot = jnp.arange(core * far, dtype=jnp.int32)
    owner = dp_index ^ (near * (slot % far) + slot // far)
    start = owner * rows + mp_index * half
    text_id = (start[:, None] + jnp.arange(half, dtype=jnp.int32)[None]).reshape(-1)
    picked = jnp.where(pairs.reshape(-1, 1) == text_id[None], logits, 0.0)

    row_top = jnp.max(logits, axis=1)
    row_lse = row_top + jnp.log(jnp.sum(jnp.exp(logits - row_top[:, None]), axis=1))
    col_top = jnp.max(logits, axis=0)
    col_lse = col_top + jnp.log(jnp.sum(jnp.exp(logits - col_top[None]), axis=0))
    row = jnp.stack([row_lse, jnp.sum(picked, axis=1)])
    col = jnp.stack([col_lse, jnp.sum(picked, axis=0)])

    for stride in [1] * (core > 1) + [near * s for s in reversed(strides(1, far))]:
        split = col.shape[1] // 2
        col = merge(col[:, :split], exchange(col[:, split:], "dp", dp, stride))
    for stride in reversed(strides(core, near)):
        split = row.shape[1] // 2
        row = merge(row[:, :split], exchange(row[:, split:], "dp", dp, stride))
    for step in strides(1, mp):
        row = merge(row, exchange(row, "mp", mp, step))
    return (row[0] - row[1], col[0] - col[1])


def solution(mesh):
    in_specs = (P("dp", "mp"), P("mp", None), P("dp", "mp"), P("mp", None), P("dp"), P())
    out_specs = (P("dp"), P(("dp", "mp")))
    return jax.shard_map(
        on_device, mesh=mesh, in_specs=in_specs, out_specs=out_specs, check_vma=False
    )
```

time: 142 us -> 36.2 us (0.25)
  waiting for transfers between devices: 86.7 us -> 11 us
  between operations: 14.8 us -> 1.51 us
  blocking collectives: 12.6 us -> 0 us
  starting transfers between devices: 13.1 us -> 18.1 us
  matrix products: 6.11 us -> 2.47 us
  other arithmetic: 5.44 us -> 2.12 us
  local copies, waits for them, and re-layouts: 3.09 us -> 0.79 us
    all_gather x1 -> x0, waiting for transfers between devices: 38.1 us -> none  [on_device(): piece = lax.all_gather(text_emb, 'dp', axis=0, tiled=True)]
    psum x1 -> x0, waiting for transfers between devices: 37.3 us -> none  [on_device(): summed = lax.psum(text_part, 'mp')]
    ppermute x0 -> x16, starting transfers between devices: none -> 18.1 us  [exchange(): return lax.ppermute(value, axis, [(i, i ^ stride) for i in range(count)])]
    all_to_all x3 -> x0, starting transfers between devices: 13.1 us -> none  [the longest x1 5.97 us: on_device(): lax.all_to_all(shaped_sum, 'dp', split_axis=0, concat_axis=0, tiled=True)]
    all_gather x3 -> x0, blocking collectives: 12.6 us -> none  [joined(): pieces = jax.tree.map(lambda part: lax.all_gather(part, axis), value)]
    all_to_all x3 -> x0, waiting for transfers between devices: 11.3 us -> none  [the longest x1 5.81 us: on_device(): lax.all_to_all(shaped_sum, 'dp', split_axis=0, concat_axis=0, tiled=True)]
    ppermute x0 -> x16, waiting for transfers between devices: none -> 11 us  [exchange(): return lax.ppermute(value, axis, [(i, i ^ stride) for i in range(count)])]
    reduce_sum x2 -> x1, other arithmetic: 2.14 us -> 0.13 us  [normalize(): norm_sq = jnp.sum(raw * raw, axis=1, keepdims=True)]
  transfers between devices with their start and end apart: 5 -> 16, of which waited for: 4 -> 7; matrix products, arithmetic and copies ran while one was open for 1% -> 5% of each run, Pallas kernels for 0% -> 0%
where the time goes in v1:
time: 36.2 us; the launch traced here: 36 us
  starting transfers between devices  18.1 us (50%)
  waiting for transfers between devices  11 us (30%)
  matrix products  2.47 us (7%)
  other arithmetic  2.12 us (6%)
  between operations  1.51 us (4%)
  local copies, waits for them, and re-layouts  0.79 us (2%)
    ppermute x16, starting transfers between devices, exchange(): return lax.ppermute(value, axis, [(i, i ^ stride) for i in range(count)])  18.1 us
    ppermute x16, waiting for transfers between devices, exchange(): return lax.ppermute(value, axis, [(i, i ^ stride) for i in range(count)])  11 us
    dot_general x2, matrix products, text_rows(): return jnp.dot(mine, text_proj, preferred_element_type=jnp.float32)  1.71 us
    sub x2, other arithmetic, on_device(): return (row[0] - row[1], col[0] - col[1])  1.08 us
  transfers between devices with their start and end apart: 16, of which 7 were waited for; matrix products, arithmetic and copies ran while one was open for 5% of the time, Pallas kernels for 0%

profile of v1, /device:TPU:0, one launch (start us, length us, event | category | flops | bytes accessed | tf_op | source)
XLA Modules:
  0.0 36.0 jit_solution(8973234874630476177)
XLA Ops:
  0.6 0.0 copy-start
  0.7 0.0 copy-start.2
  0.7 1.4 %convolution_convert_fusion = f16[64,768]{1,0:T(8,128)(2,1)S(1)} fusion(bf16[384,768]{1,0:T(8,128)(2,1)} %param.9, bf16[128,384]{1,0:T(8,128)(2,1)} %param.8, s32[]{:T(128)S(6)} %select_n.31), kind=kOutput, calls=%fused_computation.1 | convolution fusion | flops 37797888 | bytes 737284 | tf_op jit(solution)/shard_map/dot_general | solution.py:44
  2.1 0.0 copy-start.1
  2.1 0.0 copy-start.3
  2.1 3.0 %collective-permute-start.2 = (f16[64,768]{1,0:T(8,128)(2,1)S(1)}, f16[64,768]{1,0:T(8,128)(2,1)S(1)}, u32[]{:S(2)}, u32[]{:S(2)}) collective-permute-start(f16[64,768]{1,0:T(8,128)(2,1)S(1)} %convolution_convert_fusion), channel_id=1, source_target_pairs={{0,1},{1,0},{2,3},{3,2},{4,5},{5,4},{6,7},{7,6},{8,9},{9,8},{10,11... | collective-permute-start | bytes 294920 | tf_op jit(solution)/shard_map/ppermute | solution.py:8
  5.1 0.0 copy-done
  5.1 0.0 copy-done.2
  5.1 0.3 fusion.28
  5.4 0.0 copy-start.4
  5.4 0.1 collective-permute-start
  5.5 0.6 %copy-done.4 = s32[128]{0:T(128)S(1)} copy-done((s32[128]{0:T(128)S(1)}, s32[128]{0:T(128)}, u32[]{:S(2)}) %copy-start.4) | copy-done | bytes 536
  6.0 1.5 %collective-permute-start.10 = (s32[1,128]{1,0:T(1,128)S(1)}, s32[1,128]{1,0:T(1,128)S(1)}, u32[]{:S(2)}, u32[]{:S(2)}) collective-permute-start(s32[1,128]{1,0:T(1,128)S(1)} %bitcast.107), channel_id=1, source_target_pairs={{0,4},{2,6},{4,0},{6,2},{8,12},{10,14},{12,8},{14,10},{16,20},{18,... | collective-permute-start | bytes 1544 | tf_op jit(solution)/shard_map/ppermute | solution.py:8
  7.6 0.1 iota_add_fusion
  8.3 0.1 add.194
  8.4 1.2 %collective-permute-done.10 = s32[1,128]{1,0:T(1,128)S(1)} collective-permute-done((s32[1,128]{1,0:T(1,128)S(1)}, s32[1,128]{1,0:T(1,128)S(1)}, u32[]{:S(2)}, u32[]{:S(2)}) %collective-permute-start.10) | collective-permute-done | bytes 544 | tf_op jit(solution)/shard_map/ppermute | solution.py:8
  9.6 0.0 collective-permute-done.2
  9.6 0.0 copy-done.1
  9.6 0.0 copy-done.3
  9.6 0.3 multiply_reduce_fusion.1
  9.9 0.1 constant_dynamic-update-slice_fusion.7
  10.1 1.6 %collective-permute-start.3 = (bf16[64,768]{1,0:T(8,128)(2,1)S(1)}, bf16[64,768]{1,0:T(8,128)(2,1)S(1)}, u32[]{:S(2)}, u32[]{:S(2)}) collective-permute-start(bf16[64,768]{1,0:T(8,128)(2,1)S(1)} %get-tuple-element.8), channel_id=1, source_target_pairs={{0,8},{2,10},{4,12},{6,14},{8,0},{10,2},{12,4},{14,6},{16,24},{18,... | collective-permute-start | bytes 294920 | tf_op jit(solution)/shard_map/ppermute | solution.py:8
  11.7 2.6 %collective-permute-start.4 = (bf16[64,768]{1,0:T(8,128)(2,1)S(1)}, bf16[64,768]{1,0:T(8,128)(2,1)S(1)}, u32[]{:S(2)}, u32[]{:S(2)}) collective-permute-start(bf16[64,768]{1,0:T(8,128)(2,1)S(1)} %get-tuple-element.8), channel_id=1, source_target_pairs={{0,16},{2,18},{4,20},{6,22},{8,24},{10,26},{12,28},{14,30},{16,0},... | collective-permute-start | bytes 294920 | tf_op jit(solution)/shard_map/ppermute | solution.py:8
  14.3 0.2 collective-permute-start.5
  14.5 0.0 collective-permute-start.6
  14.5 0.0 collective-permute-done
  14.5 0.1 multiply_reduce_fusion
  14.7 0.1 fusion.2
  14.8 1.6 %collective-permute-start.1 = (bf16[1,128,768]{2,1,0:T(8,128)(2,1)S(1)}, bf16[1,128,768]{2,1,0:T(8,128)(2,1)S(1)}, u32[]{:S(2)}, u32[]{:S(2)}) collective-permute-start(bf16[1,128,768]{2,1,0:T(8,128)(2,1)S(1)} %fusion.2), channel_id=1, source_target_pairs={{0,4},{2,6},{4,0},{6,2},{8,12},{10,14},{12,8},{14,10},{16,20},{18,... | collective-permute-start | bytes 589832 | tf_op jit(solution)/shard_map/ppermute | solution.py:8
  16.4 0.0 collective-permute-done.3
  16.4 0.2 collective-permute-start.7
  16.6 4.4 %collective-permute-done.4 = bf16[64,768]{1,0:T(8,128)(2,1)S(1)} collective-permute-done((bf16[64,768]{1,0:T(8,128)(2,1)S(1)}, bf16[64,768]{1,0:T(8,128)(2,1)S(1)}, u32[]{:S(2)}, u32[]{:S(2)}) %collective-permute-start.4) | collective-permute-done | bytes 98336 | tf_op jit(solution)/shard_map/ppermute | solution.py:8
  21.0 0.0 collective-permute-start.8
  21.0 0.0 collective-permute-done.5
  21.0 0.6 %collective-permute-start.9 = (bf16[64,768]{1,0:T(8,128)(2,1)S(1)}, bf16[64,768]{1,0:T(8,128)(2,1)S(1)}, u32[]{:S(2)}, u32[]{:S(2)}) collective-permute-start(bf16[64,768]{1,0:T(8,128)(2,1)S(1)} %collective-permute-done.5), channel_id=1, source_target_pairs={{0,2},{2,0},{4,6},{6,4},{8,10},{10,8},{12,14},{14,12},{16,18},{18,... | collective-permute-start | bytes 294920 | tf_op jit(solution)/shard_map/ppermute | solution.py:8
  21.6 0.0 collective-permute-done.6
  21.6 0.0 collective-permute-done.7
  21.6 0.7 %collective-permute-done.8 = bf16[64,768]{1,0:T(8,128)(2,1)S(1)} collective-permute-done((bf16[64,768]{1,0:T(8,128)(2,1)S(1)}, bf16[64,768]{1,0:T(8,128)(2,1)S(1)}, u32[]{:S(2)}, u32[]{:S(2)}) %collective-permute-start.8) | collective-permute-done | bytes 98336 | tf_op jit(solution)/shard_map/ppermute | solution.py:8
  22.3 0.2 collective-permute-done.9
  22.5 0.0 collective-permute-done.1
  22.6 0.5 %fusion.29 = (f32[256]{0:T(256)S(1)}, f32[256,512]{1,0:T(8,128)S(1)}) fusion(bf16[256,768]{1,0:T(8,128)(2,1)S(1)} %bitcast.97, bf16[512,768]{1,0:T(8,128)(2,1)S(1)} %constant_dynamic-update-slice_fusion, f32[]{:T(128)} %bitcast.96), kind=kOutput, calls=%fused_computation.84 | convolution fusion | flops 201588480 | bytes 1704964 | tf_op jit(solution)/shard_map/dot_general | solution.py:71
  23.1 0.2 fusion.27
  23.3 0.2 fusion
  23.6 1.6 %collective-permute-start.11 = (f32[2,128]{1,0:T(2,128)S(1)}, f32[2,128]{1,0:T(2,128)S(1)}, u32[]{:S(2)}, u32[]{:S(2)}) collective-permute-start(f32[2,128]{1,0:T(2,128)S(1)} %pad_maximum_fusion.3), channel_id=1, source_target_pairs={{0,4},{2,6},{4,0},{6,2},{8,12},{10,14},{12,8},{14,10},{16,20},{18,... | collective-permute-start | bytes 3080 | tf_op jit(solution)/shard_map/ppermute | solution.py:8
  25.2 0.1 collective-permute-start.13
  25.2 2.0 %collective-permute-done.11 = f32[2,128]{1,0:T(2,128)S(1)} collective-permute-done((f32[2,128]{1,0:T(2,128)S(1)}, f32[2,128]{1,0:T(2,128)S(1)}, u32[]{:S(2)}, u32[]{:S(2)}) %collective-permute-start.11) | collective-permute-done | bytes 1056 | tf_op jit(solution)/shard_map/ppermute | solution.py:8
  27.2 0.0 collective-permute-done.13
  27.3 2.5 %collective-permute-start.14 = (f32[2,128]{1,0:T(2,128)S(1)}, f32[2,128]{1,0:T(2,128)S(1)}, u32[]{:S(2)}, u32[]{:S(2)}) collective-permute-start(f32[2,128]{1,0:T(2,128)S(1)} %pad_maximum_fusion.2), channel_id=1, source_target_pairs={{0,16},{2,18},{4,20},{6,22},{8,24},{10,26},{12,28},{14,30},{16,0},... | collective-permute-start | bytes 3080 | tf_op jit(solution)/shard_map/ppermute | solution.py:8
  29.7 1.2 %collective-permute-start.12 = (f32[2,128]{1,0:T(2,128)S(1)}, f32[2,128]{1,0:T(2,128)S(1)}, u32[]{:S(2)}, u32[]{:S(2)}) collective-permute-start(f32[2,128]{1,0:T(2,128)S(1)} %pad_maximum_fusion.4), channel_id=1, source_target_pairs={{0,1},{1,0},{2,3},{3,2},{4,5},{5,4},{6,7},{7,6},{8,9},{9,8},{10,11... | collective-permute-start | bytes 3080 | tf_op jit(solution)/shard_map/ppermute | solution.py:8
  30.9 0.9 %collective-permute-done.14 = f32[2,128]{1,0:T(2,128)S(1)} collective-permute-done((f32[2,128]{1,0:T(2,128)S(1)}, f32[2,128]{1,0:T(2,128)S(1)}, u32[]{:S(2)}, u32[]{:S(2)}) %collective-permute-start.14) | collective-permute-done | bytes 1056 | tf_op jit(solution)/shard_map/ppermute | solution.py:8
  31.8 0.1 slice.113
  31.9 1.4 %collective-permute-start.15 = (f32[2,64]{1,0:T(2,128)S(1)}, f32[2,64]{1,0:T(2,128)S(1)}, u32[]{:S(2)}, u32[]{:S(2)}) collective-permute-start(f32[2,64]{1,0:T(2,128)S(1)} %slice.113), channel_id=1, source_target_pairs={{0,8},{2,10},{4,12},{6,14},{8,0},{10,2},{12,4},{14,6},{16,24},{18,... | collective-permute-start | bytes 1544 | tf_op jit(solution)/shard_map/ppermute | solution.py:8
  33.3 0.0 collective-permute-done.12
  33.3 0.6 %bitcast_subtract_fusion.3 = f32[128]{0:T(128)} fusion(f32[1,128]{1,0:T(1,128)S(1)} %get-tuple-element.14, f32[2,128]{1,0:T(2,128)S(1)} %collective-permute-done.12, f32[1,256]{1,0:T(1,128)S(1)} %bitcast.104, f32[2,128]{1,0:T(2,128)S(1)} %collective-permute-done.11), kind=kLoop, calls=%fused_computation.59 | loop fusion | flops 1536 | bytes 3072 | tf_op jit(solution)/shard_map/sub | solution.py:95
  33.9 1.6 %collective-permute-done.15 = f32[2,64]{1,0:T(2,128)S(1)} collective-permute-done((f32[2,64]{1,0:T(2,128)S(1)}, f32[2,64]{1,0:T(2,128)S(1)}, u32[]{:S(2)}, u32[]{:S(2)}) %collective-permute-start.15) | collective-permute-done | bytes 544 | tf_op jit(solution)/shard_map/ppermute | solution.py:8
  35.5 0.5 %bitcast_subtract_fusion = f32[64]{0:T(128)} fusion(f32[2,64]{1,0:T(2,128)S(1)} %collective-permute-done.15, f32[1,128]{1,0:T(1,128)S(1)} %get-tuple-element.12, f32[1,128]{1,0:T(1,128)S(1)} %get-tuple-element.11), kind=kLoop, calls=%fused_computation.51 | loop fusion | flops 448 | bytes 1280 | tf_op jit(solution)/shard_map/sub | solution.py:95
  (22 shorter events, 0.2 us)
Async XLA Ops:
  0.6 4.5 %copy-start = (bf16[512,768]{1,0:T(8,128)(2,1)S(1)}, bf16[512,768]{1,0:T(8,128)(2,1)}, u32[]{:S(2)}) copy-start(bf16[512,768]{1,0:T(8,128)(2,1)} %param.7) | copy-start | bytes 2359300
  0.7 4.4 %copy-start.2 = (bf16[128,512]{1,0:T(8,128)(2,1)S(1)}, bf16[128,512]{1,0:T(8,128)(2,1)}, u32[]{:S(2)}) copy-start(bf16[128,512]{1,0:T(8,128)(2,1)} %param.6) | copy-start | bytes 393220
  2.1 7.5 %copy-start.1 = (bf16[384,768]{1,0:T(8,128)(2,1)S(1)}, bf16[384,768]{1,0:T(8,128)(2,1)}, u32[]{:S(2)}) copy-start(bf16[384,768]{1,0:T(8,128)(2,1)} %param.9) | copy-start | bytes 1769476
  2.1 7.5 %copy-start.3 = (bf16[128,384]{1,0:T(8,128)(2,1)S(1)}, bf16[128,384]{1,0:T(8,128)(2,1)}, u32[]{:S(2)}) copy-start(bf16[128,384]{1,0:T(8,128)(2,1)} %param.8) | copy-start | bytes 294916
  2.1 7.5 %collective-permute-start.2 = (f16[64,768]{1,0:T(8,128)(2,1)S(1)}, f16[64,768]{1,0:T(8,128)(2,1)S(1)}, u32[]{:S(2)}, u32[]{:S(2)}) collective-permute-start(f16[64,768]{1,0:T(8,128)(2,1)S(1)} %convolution_convert_fusion), channel_id=1, source_target_pairs={{0,1},{1,0},{2,3},{3,2},{4,5},{5,4},{6,7},{7,6},{8,9},{9,8},{10,11... | collective-permute-start | bytes 294920 | tf_op jit(solution)/shard_map/ppermute | solution.py:8
  5.4 0.7 %copy-start.4 = (s32[128]{0:T(128)S(1)}, s32[128]{0:T(128)}, u32[]{:S(2)}) copy-start(s32[128]{0:T(128)} %param.10) | copy-start | bytes 1540
  5.4 9.1 %collective-permute-start = (f16[128,768]{1,0:T(8,128)(2,1)S(1)}, f16[128,768]{1,0:T(8,128)(2,1)S(1)}, u32[]{:S(2)}, u32[]{:S(2)}) collective-permute-start(f16[128,768]{1,0:T(8,128)(2,1)S(1)} %get-tuple-element.15), channel_id=1, source_target_pairs={{0,1},{1,0},{2,3},{3,2},{4,5},{5,4},{6,7},{7,6},{8,9},{9,8},{10,11... | collective-permute-start | bytes 589832 | tf_op jit(solution)/shard_map/ppermute | solution.py:8
  6.0 3.5 %collective-permute-start.10 = (s32[1,128]{1,0:T(1,128)S(1)}, s32[1,128]{1,0:T(1,128)S(1)}, u32[]{:S(2)}, u32[]{:S(2)}) collective-permute-start(s32[1,128]{1,0:T(1,128)S(1)} %bitcast.107), channel_id=1, source_target_pairs={{0,4},{2,6},{4,0},{6,2},{8,12},{10,14},{12,8},{14,10},{16,20},{18,... | collective-permute-start | bytes 1544 | tf_op jit(solution)/shard_map/ppermute | solution.py:8
  10.1 6.3 %collective-permute-start.3 = (bf16[64,768]{1,0:T(8,128)(2,1)S(1)}, bf16[64,768]{1,0:T(8,128)(2,1)S(1)}, u32[]{:S(2)}, u32[]{:S(2)}) collective-permute-start(bf16[64,768]{1,0:T(8,128)(2,1)S(1)} %get-tuple-element.8), channel_id=1, source_target_pairs={{0,8},{2,10},{4,12},{6,14},{8,0},{10,2},{12,4},{14,6},{16,24},{18,... | collective-permute-start | bytes 294920 | tf_op jit(solution)/shard_map/ppermute | solution.py:8
  11.7 9.3 %collective-permute-start.4 = (bf16[64,768]{1,0:T(8,128)(2,1)S(1)}, bf16[64,768]{1,0:T(8,128)(2,1)S(1)}, u32[]{:S(2)}, u32[]{:S(2)}) collective-permute-start(bf16[64,768]{1,0:T(8,128)(2,1)S(1)} %get-tuple-element.8), channel_id=1, source_target_pairs={{0,16},{2,18},{4,20},{6,22},{8,24},{10,26},{12,28},{14,30},{16,0},... | collective-permute-start | bytes 294920 | tf_op jit(solution)/shard_map/ppermute | solution.py:8
  14.3 6.7 %collective-permute-start.5 = (bf16[64,768]{1,0:T(8,128)(2,1)S(1)}, bf16[64,768]{1,0:T(8,128)(2,1)S(1)}, u32[]{:S(2)}, u32[]{:S(2)}) collective-permute-start(bf16[64,768]{1,0:T(8,128)(2,1)S(1)} %get-tuple-element.8), channel_id=1, source_target_pairs={{0,24},{2,26},{4,28},{6,30},{8,16},{10,18},{12,20},{14,22},{16,8},... | collective-permute-start | bytes 294920 | tf_op jit(solution)/shard_map/ppermute | solution.py:8
  14.5 7.1 %collective-permute-start.6 = (bf16[64,768]{1,0:T(8,128)(2,1)S(1)}, bf16[64,768]{1,0:T(8,128)(2,1)S(1)}, u32[]{:S(2)}, u32[]{:S(2)}) collective-permute-start(bf16[64,768]{1,0:T(8,128)(2,1)S(1)} %get-tuple-element.8), channel_id=1, source_target_pairs={{0,2},{2,0},{4,6},{6,4},{8,10},{10,8},{12,14},{14,12},{16,18},{18,... | collective-permute-start | bytes 294920 | tf_op jit(solution)/shard_map/ppermute | solution.py:8
  14.8 7.8 %collective-permute-start.1 = (bf16[1,128,768]{2,1,0:T(8,128)(2,1)S(1)}, bf16[1,128,768]{2,1,0:T(8,128)(2,1)S(1)}, u32[]{:S(2)}, u32[]{:S(2)}) collective-permute-start(bf16[1,128,768]{2,1,0:T(8,128)(2,1)S(1)} %fusion.2), channel_id=1, source_target_pairs={{0,4},{2,6},{4,0},{6,2},{8,12},{10,14},{12,8},{14,10},{16,20},{18,... | collective-permute-start | bytes 589832 | tf_op jit(solution)/shard_map/ppermute | solution.py:8
  16.4 5.2 %collective-permute-start.7 = (bf16[64,768]{1,0:T(8,128)(2,1)S(1)}, bf16[64,768]{1,0:T(8,128)(2,1)S(1)}, u32[]{:S(2)}, u32[]{:S(2)}) collective-permute-start(bf16[64,768]{1,0:T(8,128)(2,1)S(1)} %collective-permute-done.3), channel_id=1, source_target_pairs={{0,2},{2,0},{4,6},{6,4},{8,10},{10,8},{12,14},{14,12},{16,18},{18,... | collective-permute-start | bytes 294920 | tf_op jit(solution)/shard_map/ppermute | solution.py:8
  21.0 1.3 %collective-permute-start.8 = (bf16[64,768]{1,0:T(8,128)(2,1)S(1)}, bf16[64,768]{1,0:T(8,128)(2,1)S(1)}, u32[]{:S(2)}, u32[]{:S(2)}) collective-permute-start(bf16[64,768]{1,0:T(8,128)(2,1)S(1)} %collective-permute-done.4), channel_id=1, source_target_pairs={{0,2},{2,0},{4,6},{6,4},{8,10},{10,8},{12,14},{14,12},{16,18},{18,... | collective-permute-start | bytes 294920 | tf_op jit(solution)/shard_map/ppermute | solution.py:8
  21.0 1.5 %collective-permute-start.9 = (bf16[64,768]{1,0:T(8,128)(2,1)S(1)}, bf16[64,768]{1,0:T(8,128)(2,1)S(1)}, u32[]{:S(2)}, u32[]{:S(2)}) collective-permute-start(bf16[64,768]{1,0:T(8,128)(2,1)S(1)} %collective-permute-done.5), channel_id=1, source_target_pairs={{0,2},{2,0},{4,6},{6,4},{8,10},{10,8},{12,14},{14,12},{16,18},{18,... | collective-permute-start | bytes 294920 | tf_op jit(solution)/shard_map/ppermute | solution.py:8
  23.6 3.6 %collective-permute-start.11 = (f32[2,128]{1,0:T(2,128)S(1)}, f32[2,128]{1,0:T(2,128)S(1)}, u32[]{:S(2)}, u32[]{:S(2)}) collective-permute-start(f32[2,128]{1,0:T(2,128)S(1)} %pad_maximum_fusion.3), channel_id=1, source_target_pairs={{0,4},{2,6},{4,0},{6,2},{8,12},{10,14},{12,8},{14,10},{16,20},{18,... | collective-permute-start | bytes 3080 | tf_op jit(solution)/shard_map/ppermute | solution.py:8
  25.2 2.1 %collective-permute-start.13 = (f32[2,256]{1,0:T(2,128)S(1)}, f32[2,256]{1,0:T(2,128)S(1)}, u32[]{:S(2)}, u32[]{:S(2)}) collective-permute-start(f32[2,256]{1,0:T(2,128)S(1)} %pad_maximum_fusion.1), channel_id=1, source_target_pairs={{0,2},{2,0},{4,6},{6,4},{8,10},{10,8},{12,14},{14,12},{16,18},{18,... | collective-permute-start | bytes 6152 | tf_op jit(solution)/shard_map/ppermute | solution.py:8
  27.3 4.5 %collective-permute-start.14 = (f32[2,128]{1,0:T(2,128)S(1)}, f32[2,128]{1,0:T(2,128)S(1)}, u32[]{:S(2)}, u32[]{:S(2)}) collective-permute-start(f32[2,128]{1,0:T(2,128)S(1)} %pad_maximum_fusion.2), channel_id=1, source_target_pairs={{0,16},{2,18},{4,20},{6,22},{8,24},{10,26},{12,28},{14,30},{16,0},... | collective-permute-start | bytes 3080 | tf_op jit(solution)/shard_map/ppermute | solution.py:8
  29.7 3.6 %collective-permute-start.12 = (f32[2,128]{1,0:T(2,128)S(1)}, f32[2,128]{1,0:T(2,128)S(1)}, u32[]{:S(2)}, u32[]{:S(2)}) collective-permute-start(f32[2,128]{1,0:T(2,128)S(1)} %pad_maximum_fusion.4), channel_id=1, source_target_pairs={{0,1},{1,0},{2,3},{3,2},{4,5},{5,4},{6,7},{7,6},{8,9},{9,8},{10,11... | collective-permute-start | bytes 3080 | tf_op jit(solution)/shard_map/ppermute | solution.py:8
  31.9 3.6 %collective-permute-start.15 = (f32[2,64]{1,0:T(2,128)S(1)}, f32[2,64]{1,0:T(2,128)S(1)}, u32[]{:S(2)}, u32[]{:S(2)}) collective-permute-start(f32[2,64]{1,0:T(2,128)S(1)} %slice.113), channel_id=1, source_target_pairs={{0,8},{2,10},{4,12},{6,14},{8,0},{10,2},{12,4},{14,6},{16,24},{18,... | collective-permute-start | bytes 1544 | tf_op jit(solution)/shard_map/ppermute | solution.py:8

commit v2 on v1

v2 whole, which is shorter than its diff:
```python
import functools

import jax
import jax.numpy as jnp
from jax import lax
from jax.experimental import pallas as pl
from jax.experimental.pallas import tpu as pltpu
from jax.sharding import PartitionSpec as P


def exchange(value, stride, step=0):
    dp, mp = lax.axis_size("dp"), lax.axis_size("mp")
    pairs = [(i * mp + j, (i ^ stride) * mp + (j ^ step)) for i in range(dp) for j in range(mp)]
    return lax.ppermute(value, ("dp", "mp"), pairs)


def normalize(raw):
    norm_sq = jnp.sum(raw * raw, axis=1, keepdims=True)
    return (raw / jnp.sqrt(norm_sq + 1e-06)).astype(jnp.bfloat16)


def join(stats):
    top = functools.reduce(jnp.maximum, [s[0] for s in stats])
    total = sum(jnp.exp(s[0] - top) for s in stats)
    return jnp.stack([top + jnp.log(total), sum(s[1] for s in stats)])


def stats_kernel(n_image, n_text, scale_ref, start_ref, *refs):
    refs = list(refs)
    images = [refs.pop(0) for _ in range(n_image)]
    pairs = [refs.pop(0) for _ in range(n_image)]
    texts = [refs.pop(0) for _ in range(n_text)]
    col_out = [refs.pop(0) for _ in range(len(refs) - n_image)]
    row_out = refs
    rows = images[0].shape[0]
    half = texts[0].shape[0]
    per_out = n_text // len(col_out)
    image = jnp.concatenate([r[...] for r in images], axis=0)
    text = jnp.concatenate([r[...] for r in texts], axis=0)
    logits = scale_ref[0] * lax.dot_general(
        image, text, (((1,), (1,)), ((), ())), preferred_element_type=jnp.float32
    )
    place = lax.broadcasted_iota(jnp.int32, (1, n_text * half), 1)
    ids = place + start_ref[0]
    for k in range(1, n_text):
        ids = jnp.where(place >= k * half, place + (start_ref[k] - k * half), ids)
    pair = jnp.concatenate([jnp.broadcast_to(r[...], (rows, rows)).T for r in pairs], axis=0)
    pair = jnp.concatenate([pair] * (n_text * half // rows), axis=1)
    picked = jnp.where(pair == ids, logits, 0.0)

    top = jnp.max(logits, axis=0, keepdims=True)
    lse = top + jnp.log(jnp.sum(jnp.exp(logits - top), axis=0, keepdims=True))
    positive = jnp.sum(picked, axis=0, keepdims=True)
    for k, out in enumerate(col_out):
        lanes = slice(k * per_out * half, (k + 1) * per_out * half)
        out[0:1, :] = lse[:, lanes]
        out[1:2, :] = positive[:, lanes]

    top = jnp.max(logits, axis=1, keepdims=True)
    lse = top + jnp.log(jnp.sum(jnp.exp(logits - top), axis=1, keepdims=True))
    positive = jnp.sum(picked, axis=1, keepdims=True)
    for k, out in enumerate(row_out):
        block = slice(k * rows, (k + 1) * rows)
        lane = lax.broadcasted_iota(jnp.int32, (rows, rows), 1)
        both = jnp.where(lane == 0, lse[block], positive[block]).T
        out[...] = both[0:2]


def block_stats(scale, starts, images, pairs, texts, n_out):
    rows = images[0].shape[0]
    count = len(texts) * texts[0].shape[0]
    vmem = pl.BlockSpec(memory_space=pltpu.VMEM)
    smem = pl.BlockSpec(memory_space=pltpu.SMEM)
    operands = [*images, *pairs, *texts]
    out = pl.pallas_call(
        functools.partial(stats_kernel, len(images), len(texts)),
        out_shape=[jax.ShapeDtypeStruct((2, count // n_out), jnp.float32)] * n_out
        + [jax.ShapeDtypeStruct((2, rows), jnp.float32)] * len(images),
        in_specs=[smem, smem] + [vmem] * len(operands),
        out_specs=[vmem] * (n_out + len(images)),
        compiler_params=pltpu.CompilerParams(vmem_limit_bytes=48 * 2**20),
        cost_estimate=pl.CostEstimate(
            flops=2 * rows * len(images) * count * images[0].shape[1],
            bytes_accessed=sum(o.size * o.dtype.itemsize for o in operands),
            transcendentals=2 * rows * len(images) * count,
        ),
    )(scale, starts, *operands)
    return out[:n_out], out[n_out:]


def on_device(image_feat, image_proj, text_feat, text_proj, pair_index, logit_scale):
    dp = lax.axis_size("dp")
    mp = lax.axis_size("mp")
    dp_index = lax.axis_index("dp")
    mp_index = lax.axis_index("mp")
    far = 1 << ((dp.bit_length() - 1) // 2)
    near = dp // far
    core = min(2, near)
    rows = image_feat.shape[0]
    half = rows // mp
    width = text_proj.shape[1]
    z_order = list(reversed(range(1, far)))

    def text_rows(owner):
        mine = lax.dynamic_slice_in_dim(text_feat, owner * half, half, 0)
        return jnp.dot(mine, text_proj, preferred_element_type=jnp.float32)

    got = [
        exchange(text_rows(mp_index ^ step).astype(jnp.float16), 0, step)
        for step in range(1, mp)
    ]
    image_raw = jnp.dot(image_feat, image_proj, preferred_element_type=jnp.float32)
    sent = image_raw.astype(jnp.float16)
    for step in range(1, mp):
        image_raw = image_raw + exchange(sent, 0, step)
    text_emb = normalize(sum(got, text_rows(mp_index)))

    texts = {j: exchange(text_emb, near * j) for j in z_order}

    pairs = [pair_index[None]]
    pairs += [exchange(pairs[0], stride) for stride in range(core, near, core)]
    image_emb, *pairs = lax.optimization_barrier((normalize(image_raw), *pairs))
    images = [image_emb] + [exchange(image_emb, stride) for stride in range(core, near, core)]

    texts[0] = text_emb
    late, _ = lax.optimization_barrier((text_emb, texts[z_order[0]]))
    both = [
        text for j in range(far)
        for text in [texts[j]] + [exchange(late if j == 0 else texts[j], c) for c in range(1, core)]
    ]
    owner = jnp.stack([dp_index ^ (near * j + c) for j in range(far) for c in range(core)])
    starts = (owner * rows + mp_index * half).astype(jnp.int32)
    col, row = block_stats(logit_scale, starts, images, pairs, both, far)

    k = far
    col = list(col)
    while k > 1:
        k //= 2
        other = exchange(jnp.concatenate(col[k : 2 * k], axis=1), near * k)
        n = core * half
        col = [join([col[j], other[:, j * n : (j + 1) * n]]) for j in range(k)]
    col = col[0]
    row = list(row)
    k = near // core
    while k > 1:
        k //= 2
        row = [join([row[s], exchange(row[s + k], core * k)]) for s in range(k)]
    row = join([row[0]] + [exchange(row[0], 0, m) for m in range(1, mp)])
    col = join(
        [col[:, :half]]
        + [exchange(col[:, c * half : (c + 1) * half], c) for c in range(1, core)]
    )
    return (row[0] - row[1], col[0] - col[1])


def solution(mesh):
    in_specs = (P("dp", "mp"), P("mp", None), P("dp", "mp"), P("mp", None), P("dp"), P())
    out_specs = (P("dp"), P(("dp", "mp")))
    return jax.shard_map(
        on_device, mesh=mesh, in_specs=in_specs, out_specs=out_specs, check_vma=False
    )
```

time: 36.2 us -> 34.6 us (0.956)
  starting transfers between devices: 18.1 us -> 16.2 us
  Pallas kernels: 0 us -> 1.27 us
  other arithmetic: 2.12 us -> 1.52 us
  matrix products: 2.47 us -> 1.98 us
    ppermute x16, starting transfers between devices: 18.1 us -> 16.2 us  [exchange(): return lax.ppermute(value, ('dp', 'mp'), pairs)]
    pallas_call x0 -> x1, Pallas kernels: none -> 1.27 us  [block_stats(): pl.pallas_call(functools.partial(stats_kernel, len(images), len(texts)),...]
    dot_general x1 -> x0, matrix products: 0.48 us -> none  [on_device(): lax.dot_general(images, text_all, (((1,), (1,)), ((), ())), preferred_ele...]
  transfers between devices with their start and end apart: 16 -> 16, of which waited for: 7 -> 10; matrix products, arithmetic and copies ran while one was open for 5% -> 5% of each run, Pallas kernels for 0% -> 0%
where the time goes in v2:
time: 34.6 us; the launch traced here: 34.4 us
  starting transfers between devices  16.2 us (47%)
  waiting for transfers between devices  11.2 us (32%)
  matrix products  1.98 us (6%)
  other arithmetic  1.52 us (4%)
  between operations  1.44 us (4%)
  Pallas kernels  1.27 us (4%)
  local copies, waits for them, and re-layouts  0.74 us (2%)
    ppermute x16, starting transfers between devices, exchange(): return lax.ppermute(value, ('dp', 'mp'), pairs)  16.2 us
    ppermute x16, waiting for transfers between devices, exchange(): return lax.ppermute(value, ('dp', 'mp'), pairs)  11.2 us
    dot_general x2, matrix products, text_rows(): return jnp.dot(mine, text_proj, preferred_element_type=jnp.float32)  1.71 us
    pallas_call x1, Pallas kernels, block_stats(): pl.pallas_call(functools.partial(stats_kernel, len(images), len(texts)),...  1.27 us
    sub x2, other arithmetic, on_device(): return (row[0] - row[1], col[0] - col[1])  1.08 us
  transfers between devices with their start and end apart: 16, of which 10 were waited for; matrix products, arithmetic and copies ran while one was open for 5% of the time, Pallas kernels for 0%

profile of v2, /device:TPU:0, one launch (start us, length us, event | category | flops | bytes accessed | tf_op | source)
XLA Modules:
  0.0 34.4 jit_solution(9014138323605090474)
XLA Ops:
  0.6 0.0 copy-start
  0.7 0.0 copy-start.3
  0.7 1.4 %convolution_convert_fusion = f16[64,768]{1,0:T(8,128)(2,1)S(1)} fusion(bf16[384,768]{1,0:T(8,128)(2,1)} %param.9, bf16[128,384]{1,0:T(8,128)(2,1)} %param.8, s32[]{:T(128)S(6)} %select_n.7), kind=kOutput, calls=%fused_computation | convolution fusion | flops 37797888 | bytes 737284 | tf_op jit(solution)/shard_map/dot_general | solution.py:106
  2.1 0.0 copy-start.2
  2.1 0.0 copy-start.4
  2.1 3.0 %collective-permute-start.3 = (f16[64,768]{1,0:T(8,128)(2,1)S(1)}, f16[64,768]{1,0:T(8,128)(2,1)S(1)}, u32[]{:S(2)}, u32[]{:S(2)}) collective-permute-start(f16[64,768]{1,0:T(8,128)(2,1)S(1)} %convolution_convert_fusion), channel_id=1, source_target_pairs={{0,1},{1,0},{2,3},{3,2},{4,5},{5,4},{6,7},{7,6},{8,9},{9,8},{10,11... | collective-permute-start | bytes 294920 | tf_op jit(solution)/shard_map/ppermute | solution.py:14
  5.1 0.0 copy-done
  5.1 0.0 copy-done.3
  5.1 0.3 fusion.21
  5.4 0.0 copy-start.1
  5.4 0.1 collective-permute-start
  5.5 0.6 %copy-done.1 = s32[128]{0:T(128)S(1)} copy-done((s32[128]{0:T(128)S(1)}, s32[128]{0:T(128)}, u32[]{:S(2)}) %copy-start.1) | copy-done | bytes 536
  6.0 1.5 %collective-permute-start.1 = (s32[1,128]{1,0:T(1,128)S(1)}, s32[1,128]{1,0:T(1,128)S(1)}, u32[]{:S(2)}, u32[]{:S(2)}) collective-permute-start(s32[1,128]{1,0:T(1,128)S(1)} %bitcast.92), channel_id=1, source_target_pairs={{0,4},{1,5},{2,6},{3,7},{4,0},{5,1},{6,2},{7,3},{8,12},{9,13},{10,... | collective-permute-start | bytes 1544 | tf_op jit(solution)/shard_map/ppermute | solution.py:14
  7.6 0.1 stack.50
  7.6 0.7 %collective-permute-done.3 = f16[64,768]{1,0:T(8,128)(2,1)S(1)} collective-permute-done((f16[64,768]{1,0:T(8,128)(2,1)S(1)}, f16[64,768]{1,0:T(8,128)(2,1)S(1)}, u32[]{:S(2)}, u32[]{:S(2)}) %collective-permute-start.3) | collective-permute-done | bytes 98336 | tf_op jit(solution)/shard_map/ppermute | solution.py:14
  8.3 0.0 copy-done.2
  8.3 0.0 copy-done.4
  8.3 0.3 multiply_reduce_fusion.1
  8.6 0.1 divide_convert_fusion.1.refs_4_
  8.7 4.3 %collective-permute-start.4 = (bf16[64,768]{1,0:T(8,128)(2,1)S(1)}, bf16[64,768]{1,0:T(8,128)(2,1)S(1)}, u32[]{:S(2)}, u32[]{:S(2)}) collective-permute-start(bf16[64,768]{1,0:T(8,128)(2,1)S(1)} %divide_convert_fusion.1.refs_4_), channel_id=1, source_target_pairs={{0,24},{1,25},{2,26},{3,27},{4,28},{5,29},{6,30},{7,31},{8,16},{9,... | collective-permute-start | bytes 294920 | tf_op jit(solution)/shard_map/ppermute | solution.py:14
  13.0 0.0 collective-permute-start.6
  13.0 0.6 %collective-permute-start.8 = (bf16[64,768]{1,0:T(8,128)(2,1)S(1)}, bf16[64,768]{1,0:T(8,128)(2,1)S(1)}, u32[]{:S(2)}, u32[]{:S(2)}) collective-permute-start(bf16[64,768]{1,0:T(8,128)(2,1)S(1)} %divide_convert_fusion.1.refs_4_), channel_id=1, source_target_pairs={{0,16},{1,17},{2,18},{3,19},{4,20},{5,21},{6,22},{7,23},{8,24},{9,... | collective-permute-start | bytes 294920 | tf_op jit(solution)/shard_map/ppermute | solution.py:14
  13.7 0.0 collective-permute-done
  13.7 0.1 multiply_reduce_fusion
  13.8 0.1 divide_convert_fusion.refs_0_
  13.9 0.0 collective-permute-done.1.refs_3_
  13.9 1.7 %collective-permute-start.2 = (bf16[128,768]{1,0:T(8,128)(2,1)S(1)}, bf16[128,768]{1,0:T(8,128)(2,1)S(1)}, u32[]{:S(2)}, u32[]{:S(2)}) collective-permute-start(bf16[128,768]{1,0:T(8,128)(2,1)S(1)} %divide_convert_fusion.refs_0_), channel_id=1, source_target_pairs={{0,4},{1,5},{2,6},{3,7},{4,0},{5,1},{6,2},{7,3},{8,12},{9,13},{10,... | collective-permute-start | bytes 589832 | tf_op jit(solution)/shard_map/ppermute | solution.py:14
  15.7 0.2 collective-permute-done.4.refs_10_
  15.9 0.0 collective-permute-start.5
  15.9 0.5 %collective-permute-start.10 = (bf16[64,768]{1,0:T(8,128)(2,1)S(1)}, bf16[64,768]{1,0:T(8,128)(2,1)S(1)}, u32[]{:S(2)}, u32[]{:S(2)}) collective-permute-start(bf16[64,768]{1,0:T(8,128)(2,1)S(1)} %collective-permute-done.4.refs_10_), channel_id=1, source_target_pairs={{0,2},{1,3},{2,0},{3,1},{4,6},{5,7},{6,4},{7,5},{8,10},{9,11},{10,... | collective-permute-start | bytes 294920 | tf_op jit(solution)/shard_map/ppermute | solution.py:14
  16.4 2.7 %collective-permute-done.6.refs_6_ = bf16[64,768]{1,0:T(8,128)(2,1)S(1)} collective-permute-done((bf16[64,768]{1,0:T(8,128)(2,1)S(1)}, bf16[64,768]{1,0:T(8,128)(2,1)S(1)}, u32[]{:S(2)}, u32[]{:S(2)}) %collective-permute-start.6) | collective-permute-done | bytes 98336 | tf_op jit(solution)/shard_map/ppermute | solution.py:14
  19.1 0.0 collective-permute-start.7
  19.1 1.2 %collective-permute-done.8.refs_8_ = bf16[64,768]{1,0:T(8,128)(2,1)S(1)} collective-permute-done((bf16[64,768]{1,0:T(8,128)(2,1)S(1)}, bf16[64,768]{1,0:T(8,128)(2,1)S(1)}, u32[]{:S(2)}, u32[]{:S(2)}) %collective-permute-start.8) | collective-permute-done | bytes 98336 | tf_op jit(solution)/shard_map/ppermute | solution.py:14
  20.4 0.0 collective-permute-start.9
  21.0 0.0 collective-permute-done.5.refs_5_
  21.0 0.0 collective-permute-done.7.refs_7_
  21.0 0.6 %collective-permute-done.9.refs_9_ = bf16[64,768]{1,0:T(8,128)(2,1)S(1)} collective-permute-done((bf16[64,768]{1,0:T(8,128)(2,1)S(1)}, bf16[64,768]{1,0:T(8,128)(2,1)S(1)}, u32[]{:S(2)}, u32[]{:S(2)}) %collective-permute-start.9) | collective-permute-done | bytes 98336 | tf_op jit(solution)/shard_map/ppermute | solution.py:14
  21.7 0.0 collective-permute-done.10.refs_11_
  21.7 0.0 collective-permute-done.2.refs_1_
  21.7 1.3 %shard_map.77 = (f32[2,128]{1,0:T(2,128)S(1)}, f32[2,128]{1,0:T(2,128)S(1)}, f32[2,128]{1,0:T(2,128)S(1)}, f32[2,128]{1,0:T(2,128)S(1)}, f32[2,128]{1,0:T(2,128)S(1)}, /*index=5*/f32[2,128]{1,0:T(2,128)S(1)}) custom-call(f32[1]{0:T(128)S(6)} %copy.8.scale_ref, s32[8]{0:T(128)S(1)} %multiply_add_fusion.start_ref, ...), custom_call_target="tpu_custom_call" | custom-call | flops 201326592 | bytes 1180672 | tf_op jit(solution)/shard_map/pallas_call | solution.py:75
  22.9 1.5 %collective-permute-start.11 = (f32[2,128]{1,0:T(2,128)S(1)}, f32[2,128]{1,0:T(2,128)S(1)}, u32[]{:S(2)}, u32[]{:S(2)}) collective-permute-start(f32[2,128]{1,0:T(2,128)S(1)} %get-tuple-element.17), channel_id=1, source_target_pairs={{0,4},{1,5},{2,6},{3,7},{4,0},{5,1},{6,2},{7,3},{8,12},{9,13},{10,... | collective-permute-start | bytes 3080 | tf_op jit(solution)/shard_map/ppermute | solution.py:14
  24.5 0.6 %collective-permute-start.13 = (f32[2,256]{1,0:T(2,128)S(1)}, f32[2,256]{1,0:T(2,128)S(1)}, u32[]{:S(2)}, u32[]{:S(2)}) collective-permute-start(f32[2,256]{1,0:T(2,128)S(1)} %pad_maximum_fusion), channel_id=1, source_target_pairs={{0,16},{1,17},{2,18},{3,19},{4,20},{5,21},{6,22},{7,23},{8,24},{9,... | collective-permute-start | bytes 6152 | tf_op jit(solution)/shard_map/ppermute | solution.py:14
  25.1 1.4 %collective-permute-done.11 = f32[2,128]{1,0:T(2,128)S(1)} collective-permute-done((f32[2,128]{1,0:T(2,128)S(1)}, f32[2,128]{1,0:T(2,128)S(1)}, u32[]{:S(2)}, u32[]{:S(2)}) %collective-permute-start.11) | collective-permute-done | bytes 1056 | tf_op jit(solution)/shard_map/ppermute | solution.py:14
  26.6 2.4 %collective-permute-done.13 = f32[2,256]{1,0:T(2,128)S(1)} collective-permute-done((f32[2,256]{1,0:T(2,128)S(1)}, f32[2,256]{1,0:T(2,128)S(1)}, u32[]{:S(2)}, u32[]{:S(2)}) %collective-permute-start.13) | collective-permute-done | bytes 2080 | tf_op jit(solution)/shard_map/ppermute | solution.py:14
  29.0 0.4 %collective-permute-start.14 = (f32[2,128]{1,0:T(2,128)S(1)}, f32[2,128]{1,0:T(2,128)S(1)}, u32[]{:S(2)}, u32[]{:S(2)}) collective-permute-start(f32[2,128]{1,0:T(2,128)S(1)} %pad_maximum_fusion.2), channel_id=1, source_target_pairs={{0,8},{1,9},{2,10},{3,11},{4,12},{5,13},{6,14},{7,15},{8,0},{9,1},... | collective-permute-start | bytes 3080 | tf_op jit(solution)/shard_map/ppermute | solution.py:14
  29.4 1.9 %collective-permute-start.12 = (f32[2,128]{1,0:T(2,128)S(1)}, f32[2,128]{1,0:T(2,128)S(1)}, u32[]{:S(2)}, u32[]{:S(2)}) collective-permute-start(f32[2,128]{1,0:T(2,128)S(1)} %pad_maximum_fusion.1), channel_id=1, source_target_pairs={{0,1},{1,0},{2,3},{3,2},{4,5},{5,4},{6,7},{7,6},{8,9},{9,8},{10,11... | collective-permute-start | bytes 3080 | tf_op jit(solution)/shard_map/ppermute | solution.py:14
  31.2 1.4 %collective-permute-done.14 = f32[2,128]{1,0:T(2,128)S(1)} collective-permute-done((f32[2,128]{1,0:T(2,128)S(1)}, f32[2,128]{1,0:T(2,128)S(1)}, u32[]{:S(2)}, u32[]{:S(2)}) %collective-permute-start.14) | collective-permute-done | bytes 1056 | tf_op jit(solution)/shard_map/ppermute | solution.py:14
  32.7 0.1 slice.101
  32.7 0.0 collective-permute-start.15
  32.7 0.2 collective-permute-done.12
  32.9 0.6 %bitcast_subtract_fusion.3 = f32[128]{0:T(128)} fusion(f32[1,128]{1,0:T(1,128)S(1)} %get-tuple-element.27, f32[2,128]{1,0:T(2,128)S(1)} %collective-permute-done.12, f32[2,128]{1,0:T(2,128)S(1)} %collective-permute-done.11, f32[2,128]{1,0:T(2,128)S(1)} %get-tuple-element.16), kind=kLoop, calls=%fused_computation.25 | loop fusion | flops 1536 | bytes 3072 | tf_op jit(solution)/shard_map/sub | solution.py:153
  33.5 0.4 %collective-permute-done.15 = f32[2,64]{1,0:T(2,128)S(1)} collective-permute-done((f32[2,64]{1,0:T(2,128)S(1)}, f32[2,64]{1,0:T(2,128)S(1)}, u32[]{:S(2)}, u32[]{:S(2)}) %collective-permute-start.15) | collective-permute-done | bytes 544 | tf_op jit(solution)/shard_map/ppermute | solution.py:14
  33.9 0.5 %bitcast_subtract_fusion = f32[64]{0:T(128)} fusion(f32[2,64]{1,0:T(2,128)S(1)} %collective-permute-done.15, f32[1,128]{1,0:T(1,128)S(1)} %get-tuple-element.23, f32[1,128]{1,0:T(1,128)S(1)} %get-tuple-element.22), kind=kLoop, calls=%fused_computation.17 | loop fusion | flops 448 | bytes 1280 | tf_op jit(solution)/shard_map/sub | solution.py:153
  (10 shorter events, 0.1 us)
Async XLA Ops:
  0.6 4.5 %copy-start = (bf16[512,768]{1,0:T(8,128)(2,1)S(1)}, bf16[512,768]{1,0:T(8,128)(2,1)}, u32[]{:S(2)}) copy-start(bf16[512,768]{1,0:T(8,128)(2,1)} %param.7) | copy-start | bytes 2359300
  0.7 4.4 %copy-start.3 = (bf16[128,512]{1,0:T(8,128)(2,1)S(1)}, bf16[128,512]{1,0:T(8,128)(2,1)}, u32[]{:S(2)}) copy-start(bf16[128,512]{1,0:T(8,128)(2,1)} %param.6) | copy-start | bytes 393220
  2.1 6.2 %copy-start.2 = (bf16[384,768]{1,0:T(8,128)(2,1)S(1)}, bf16[384,768]{1,0:T(8,128)(2,1)}, u32[]{:S(2)}) copy-start(bf16[384,768]{1,0:T(8,128)(2,1)} %param.9) | copy-start | bytes 1769476
  2.1 6.2 %copy-start.4 = (bf16[128,384]{1,0:T(8,128)(2,1)S(1)}, bf16[128,384]{1,0:T(8,128)(2,1)}, u32[]{:S(2)}) copy-start(bf16[128,384]{1,0:T(8,128)(2,1)} %param.8) | copy-start | bytes 294916
  2.1 6.2 %collective-permute-start.3 = (f16[64,768]{1,0:T(8,128)(2,1)S(1)}, f16[64,768]{1,0:T(8,128)(2,1)S(1)}, u32[]{:S(2)}, u32[]{:S(2)}) collective-permute-start(f16[64,768]{1,0:T(8,128)(2,1)S(1)} %convolution_convert_fusion), channel_id=1, source_target_pairs={{0,1},{1,0},{2,3},{3,2},{4,5},{5,4},{6,7},{7,6},{8,9},{9,8},{10,11... | collective-permute-start | bytes 294920 | tf_op jit(solution)/shard_map/ppermute | solution.py:14
  5.4 0.7 %copy-start.1 = (s32[128]{0:T(128)S(1)}, s32[128]{0:T(128)}, u32[]{:S(2)}) copy-start(s32[128]{0:T(128)} %param.10) | copy-start | bytes 1540
  5.4 8.3 %collective-permute-start = (f16[128,768]{1,0:T(8,128)(2,1)S(1)}, f16[128,768]{1,0:T(8,128)(2,1)S(1)}, u32[]{:S(2)}, u32[]{:S(2)}) collective-permute-start(f16[128,768]{1,0:T(8,128)(2,1)S(1)} %get-tuple-element.28), channel_id=1, source_target_pairs={{0,1},{1,0},{2,3},{3,2},{4,5},{5,4},{6,7},{7,6},{8,9},{9,8},{10,11... | collective-permute-start | bytes 589832 | tf_op jit(solution)/shard_map/ppermute | solution.py:14
  6.0 7.9 %collective-permute-start.1 = (s32[1,128]{1,0:T(1,128)S(1)}, s32[1,128]{1,0:T(1,128)S(1)}, u32[]{:S(2)}, u32[]{:S(2)}) collective-permute-start(s32[1,128]{1,0:T(1,128)S(1)} %bitcast.92), channel_id=1, source_target_pairs={{0,4},{1,5},{2,6},{3,7},{4,0},{5,1},{6,2},{7,3},{8,12},{9,13},{10,... | collective-permute-start | bytes 1544 | tf_op jit(solution)/shard_map/ppermute | solution.py:14
  8.7 7.2 %collective-permute-start.4 = (bf16[64,768]{1,0:T(8,128)(2,1)S(1)}, bf16[64,768]{1,0:T(8,128)(2,1)S(1)}, u32[]{:S(2)}, u32[]{:S(2)}) collective-permute-start(bf16[64,768]{1,0:T(8,128)(2,1)S(1)} %divide_convert_fusion.1.refs_4_), channel_id=1, source_target_pairs={{0,24},{1,25},{2,26},{3,27},{4,28},{5,29},{6,30},{7,31},{8,16},{9,... | collective-permute-start | bytes 294920 | tf_op jit(solution)/shard_map/ppermute | solution.py:14
  13.0 6.1 %collective-permute-start.6 = (bf16[64,768]{1,0:T(8,128)(2,1)S(1)}, bf16[64,768]{1,0:T(8,128)(2,1)S(1)}, u32[]{:S(2)}, u32[]{:S(2)}) collective-permute-start(bf16[64,768]{1,0:T(8,128)(2,1)S(1)} %divide_convert_fusion.1.refs_4_), channel_id=1, source_target_pairs={{0,8},{1,9},{2,10},{3,11},{4,12},{5,13},{6,14},{7,15},{8,0},{9,1},... | collective-permute-start | bytes 294920 | tf_op jit(solution)/shard_map/ppermute | solution.py:14
  13.0 7.3 %collective-permute-start.8 = (bf16[64,768]{1,0:T(8,128)(2,1)S(1)}, bf16[64,768]{1,0:T(8,128)(2,1)S(1)}, u32[]{:S(2)}, u32[]{:S(2)}) collective-permute-start(bf16[64,768]{1,0:T(8,128)(2,1)S(1)} %divide_convert_fusion.1.refs_4_), channel_id=1, source_target_pairs={{0,16},{1,17},{2,18},{3,19},{4,20},{5,21},{6,22},{7,23},{8,24},{9,... | collective-permute-start | bytes 294920 | tf_op jit(solution)/shard_map/ppermute | solution.py:14
  13.9 7.7 %collective-permute-start.2 = (bf16[128,768]{1,0:T(8,128)(2,1)S(1)}, bf16[128,768]{1,0:T(8,128)(2,1)S(1)}, u32[]{:S(2)}, u32[]{:S(2)}) collective-permute-start(bf16[128,768]{1,0:T(8,128)(2,1)S(1)} %divide_convert_fusion.refs_0_), channel_id=1, source_target_pairs={{0,4},{1,5},{2,6},{3,7},{4,0},{5,1},{6,2},{7,3},{8,12},{9,13},{10,... | collective-permute-start | bytes 589832 | tf_op jit(solution)/shard_map/ppermute | solution.py:14
  15.9 5.1 %collective-permute-start.5 = (bf16[64,768]{1,0:T(8,128)(2,1)S(1)}, bf16[64,768]{1,0:T(8,128)(2,1)S(1)}, u32[]{:S(2)}, u32[]{:S(2)}) collective-permute-start(bf16[64,768]{1,0:T(8,128)(2,1)S(1)} %divide_convert_fusion.1.refs_4_), channel_id=1, source_target_pairs={{0,2},{1,3},{2,0},{3,1},{4,6},{5,7},{6,4},{7,5},{8,10},{9,11},{10,... | collective-permute-start | bytes 294920 | tf_op jit(solution)/shard_map/ppermute | solution.py:14
  15.9 5.8 %collective-permute-start.10 = (bf16[64,768]{1,0:T(8,128)(2,1)S(1)}, bf16[64,768]{1,0:T(8,128)(2,1)S(1)}, u32[]{:S(2)}, u32[]{:S(2)}) collective-permute-start(bf16[64,768]{1,0:T(8,128)(2,1)S(1)} %collective-permute-done.4.refs_10_), channel_id=1, source_target_pairs={{0,2},{1,3},{2,0},{3,1},{4,6},{5,7},{6,4},{7,5},{8,10},{9,11},{10,... | collective-permute-start | bytes 294920 | tf_op jit(solution)/shard_map/ppermute | solution.py:14
  19.1 1.9 %collective-permute-start.7 = (bf16[64,768]{1,0:T(8,128)(2,1)S(1)}, bf16[64,768]{1,0:T(8,128)(2,1)S(1)}, u32[]{:S(2)}, u32[]{:S(2)}) collective-permute-start(bf16[64,768]{1,0:T(8,128)(2,1)S(1)} %collective-permute-done.6.refs_6_), channel_id=1, source_target_pairs={{0,2},{1,3},{2,0},{3,1},{4,6},{5,7},{6,4},{7,5},{8,10},{9,11},{10,... | collective-permute-start | bytes 294920 | tf_op jit(solution)/shard_map/ppermute | solution.py:14
  20.4 1.3 %collective-permute-start.9 = (bf16[64,768]{1,0:T(8,128)(2,1)S(1)}, bf16[64,768]{1,0:T(8,128)(2,1)S(1)}, u32[]{:S(2)}, u32[]{:S(2)}) collective-permute-start(bf16[64,768]{1,0:T(8,128)(2,1)S(1)} %collective-permute-done.8.refs_8_), channel_id=1, source_target_pairs={{0,2},{1,3},{2,0},{3,1},{4,6},{5,7},{6,4},{7,5},{8,10},{9,11},{10,... | collective-permute-start | bytes 294920 | tf_op jit(solution)/shard_map/ppermute | solution.py:14
  22.9 3.6 %collective-permute-start.11 = (f32[2,128]{1,0:T(2,128)S(1)}, f32[2,128]{1,0:T(2,128)S(1)}, u32[]{:S(2)}, u32[]{:S(2)}) collective-permute-start(f32[2,128]{1,0:T(2,128)S(1)} %get-tuple-element.17), channel_id=1, source_target_pairs={{0,4},{1,5},{2,6},{3,7},{4,0},{5,1},{6,2},{7,3},{8,12},{9,13},{10,... | collective-permute-start | bytes 3080 | tf_op jit(solution)/shard_map/ppermute | solution.py:14
  24.5 4.5 %collective-permute-start.13 = (f32[2,256]{1,0:T(2,128)S(1)}, f32[2,256]{1,0:T(2,128)S(1)}, u32[]{:S(2)}, u32[]{:S(2)}) collective-permute-start(f32[2,256]{1,0:T(2,128)S(1)} %pad_maximum_fusion), channel_id=1, source_target_pairs={{0,16},{1,17},{2,18},{3,19},{4,20},{5,21},{6,22},{7,23},{8,24},{9,... | collective-permute-start | bytes 6152 | tf_op jit(solution)/shard_map/ppermute | solution.py:14
  29.0 3.6 %collective-permute-start.14 = (f32[2,128]{1,0:T(2,128)S(1)}, f32[2,128]{1,0:T(2,128)S(1)}, u32[]{:S(2)}, u32[]{:S(2)}) collective-permute-start(f32[2,128]{1,0:T(2,128)S(1)} %pad_maximum_fusion.2), channel_id=1, source_target_pairs={{0,8},{1,9},{2,10},{3,11},{4,12},{5,13},{6,14},{7,15},{8,0},{9,1},... | collective-permute-start | bytes 3080 | tf_op jit(solution)/shard_map/ppermute | solution.py:14
  29.4 3.6 %collective-permute-start.12 = (f32[2,128]{1,0:T(2,128)S(1)}, f32[2,128]{1,0:T(2,128)S(1)}, u32[]{:S(2)}, u32[]{:S(2)}) collective-permute-start(f32[2,128]{1,0:T(2,128)S(1)} %pad_maximum_fusion.1), channel_id=1, source_target_pairs={{0,1},{1,0},{2,3},{3,2},{4,5},{5,4},{6,7},{7,6},{8,9},{9,8},{10,11... | collective-permute-start | bytes 3080 | tf_op jit(solution)/shard_map/ppermute | solution.py:14
  32.7 1.1 %collective-permute-start.15 = (f32[2,64]{1,0:T(2,128)S(1)}, f32[2,64]{1,0:T(2,128)S(1)}, u32[]{:S(2)}, u32[]{:S(2)}) collective-permute-start(f32[2,64]{1,0:T(2,128)S(1)} %slice.101), channel_id=1, source_target_pairs={{0,2},{1,3},{2,0},{3,1},{4,6},{5,7},{6,4},{7,5},{8,10},{9,11},{10,... | collective-permute-start | bytes 1544 | tf_op jit(solution)/shard_map/ppermute | solution.py:14

commit v3 on v2

--- a/solution.py
+++ b/solution.py
@@ -25,11 +25,12 @@
     return jnp.stack([top + jnp.log(total), sum(s[1] for s in stats)])
 
 
-def stats_kernel(n_image, n_text, scale_ref, start_ref, *refs):
+def stats_kernel(n_image, n_text, scale_ref, id_ref, *refs):
     refs = list(refs)
+    texts = [refs.pop(0)]
     images = [refs.pop(0) for _ in range(n_image)]
     pairs = [refs.pop(0) for _ in range(n_image)]
-    texts = [refs.pop(0) for _ in range(n_text)]
+    texts += [refs.pop(0) for _ in range(n_text - 1)]
     col_out = [refs.pop(0) for _ in range(len(refs) - n_image)]
     row_out = refs
     rows = images[0].shape[0]
@@ -37,13 +38,10 @@
     per_out = n_text // len(col_out)
     image = jnp.concatenate([r[...] for r in images], axis=0)
     text = jnp.concatenate([r[...] for r in texts], axis=0)
-    logits = scale_ref[0] * lax.dot_general(
+    logits = scale_ref[0:1, 0:1] * lax.dot_general(
         image, text, (((1,), (1,)), ((), ())), preferred_element_type=jnp.float32
     )
-    place = lax.broadcasted_iota(jnp.int32, (1, n_text * half), 1)
-    ids = place + start_ref[0]
-    for k in range(1, n_text):
-        ids = jnp.where(place >= k * half, place + (start_ref[k] - k * half), ids)
+    ids = id_ref[...]
     pair = jnp.concatenate([jnp.broadcast_to(r[...], (rows, rows)).T for r in pairs], axis=0)
     pair = jnp.concatenate([pair] * (n_text * half // rows), axis=1)
     picked = jnp.where(pair == ids, logits, 0.0)
@@ -66,17 +64,16 @@
         out[...] = both[0:2]
 
 
-def block_stats(scale, starts, images, pairs, texts, n_out):
+def block_stats(scale, ids, images, pairs, texts, n_out):
     rows = images[0].shape[0]
     count = len(texts) * texts[0].shape[0]
     vmem = pl.BlockSpec(memory_space=pltpu.VMEM)
-    smem = pl.BlockSpec(memory_space=pltpu.SMEM)
-    operands = [*images, *pairs, *texts]
+    operands = [scale, ids, texts[0], *images, *pairs, *texts[1:]]
     out = pl.pallas_call(
         functools.partial(stats_kernel, len(images), len(texts)),
         out_shape=[jax.ShapeDtypeStruct((2, count // n_out), jnp.float32)] * n_out
         + [jax.ShapeDtypeStruct((2, rows), jnp.float32)] * len(images),
-        in_specs=[smem, smem] + [vmem] * len(operands),
+        in_specs=[vmem] * len(operands),
         out_specs=[vmem] * (n_out + len(images)),
         compiler_params=pltpu.CompilerParams(vmem_limit_bytes=48 * 2**20),
         cost_estimate=pl.CostEstimate(
@@ -84,7 +81,7 @@
             bytes_accessed=sum(o.size * o.dtype.itemsize for o in operands),
             transcendentals=2 * rows * len(images) * count,
         ),
-    )(scale, starts, *operands)
+    )(*operands)
     return out[:n_out], out[n_out:]
 
 
@@ -113,7 +110,7 @@
     sent = image_raw.astype(jnp.float16)
     for step in range(1, mp):
         image_raw = image_raw + exchange(sent, 0, step)
-    text_emb = normalize(sum(got, text_rows(mp_index)))
+    text_emb = normalize(sum(got, lax.optimization_barrier(text_rows(mp_index))))
 
     texts = {j: exchange(text_emb, near * j) for j in z_order}
 
@@ -123,14 +120,16 @@
     images = [image_emb] + [exchange(image_emb, stride) for stride in range(core, near, core)]
 
     texts[0] = text_emb
-    late, _ = lax.optimization_barrier((text_emb, texts[z_order[0]]))
+    late, _ = lax.optimization_barrier((text_emb, texts[z_order[1]]))
     both = [
         text for j in range(far)
         for text in [texts[j]] + [exchange(late if j == 0 else texts[j], c) for c in range(1, core)]
     ]
     owner = jnp.stack([dp_index ^ (near * j + c) for j in range(far) for c in range(core)])
     starts = (owner * rows + mp_index * half).astype(jnp.int32)
-    col, row = block_stats(logit_scale, starts, images, pairs, both, far)
+    ids = (starts[:, None] + jnp.arange(half, dtype=jnp.int32)[None]).reshape(1, -1)
+    scale = jnp.broadcast_to(logit_scale[None], (1, rows))
+    col, row = block_stats(scale, ids, images, pairs, both, far)
 
     k = far
     col = list(col)

time: 34.6 us -> 33.5 us (0.968)
  waiting for transfers between devices: 11.2 us -> 9.45 us
  starting transfers between devices: 16.2 us -> 17.3 us
  Pallas kernels: 1.27 us -> 0.73 us
    ppermute x16, waiting for transfers between devices: 11.2 us -> 9.45 us  [exchange(): return lax.ppermute(value, ('dp', 'mp'), pairs)]
    ppermute x16, starting transfers between devices: 16.2 us -> 17.3 us  [exchange(): return lax.ppermute(value, ('dp', 'mp'), pairs)]
    pallas_call x1, Pallas kernels: 1.27 us -> 0.73 us  [block_stats(): pl.pallas_call(functools.partial(stats_kernel, len(images), len(texts)),...]
  transfers between devices with their start and end apart: 16 -> 16, of which waited for: 10 -> 9; matrix products, arithmetic and copies ran while one was open for 5% -> 6% of each run, Pallas kernels for 0% -> 0%
where the time goes in v3:
time: 33.5 us; the launch traced here: 33.3 us
  starting transfers between devices  17.3 us (52%)
  waiting for transfers between devices  9.45 us (28%)
  matrix products  1.88 us (6%)
  other arithmetic  1.74 us (5%)
  between operations  1.44 us (4%)
  local copies, waits for them, and re-layouts  0.82 us (2%)
  Pallas kernels  0.73 us (2%)
    ppermute x16, starting transfers between devices, exchange(): return lax.ppermute(value, ('dp', 'mp'), pairs)  17.3 us
    ppermute x16, waiting for transfers between devices, exchange(): return lax.ppermute(value, ('dp', 'mp'), pairs)  9.45 us
    dot_general x2, matrix products, text_rows(): return jnp.dot(mine, text_proj, preferred_element_type=jnp.float32)  1.61 us
    sub x2, other arithmetic, on_device(): return (row[0] - row[1], col[0] - col[1])  1.08 us
    pallas_call x1, Pallas kernels, block_stats(): pl.pallas_call(functools.partial(stats_kernel, len(images), len(texts)),...  0.73 us
  transfers between devices with their start and end apart: 16, of which 9 were waited for; matrix products, arithmetic and copies ran while one was open for 6% of the time, Pallas kernels for 0%

profile of v3, /device:TPU:0, one launch (start us, length us, event | category | flops | bytes accessed | tf_op | source)
XLA Modules:
  0.0 33.3 jit_solution(5101988141745918473)
XLA Ops:
  0.6 0.0 copy-start
  0.7 0.0 copy-start.3
  0.7 1.4 %convolution_convert_fusion = f16[64,768]{1,0:T(8,128)(2,1)S(1)} fusion(bf16[384,768]{1,0:T(8,128)(2,1)} %param.9, bf16[128,384]{1,0:T(8,128)(2,1)} %param.8, s32[]{:T(128)S(6)} %select_n.7), kind=kOutput, calls=%fused_computation | convolution fusion | flops 37797888 | bytes 737284 | tf_op jit(solution)/shard_map/dot_general | solution.py:103
  2.1 0.0 copy-start.2
  2.1 0.0 copy-start.4
  2.1 3.0 %collective-permute-start = (f16[64,768]{1,0:T(8,128)(2,1)S(1)}, f16[64,768]{1,0:T(8,128)(2,1)S(1)}, u32[]{:S(2)}, u32[]{:S(2)}) collective-permute-start(f16[64,768]{1,0:T(8,128)(2,1)S(1)} %convolution_convert_fusion), channel_id=1, source_target_pairs={{0,1},{1,0},{2,3},{3,2},{4,5},{5,4},{6,7},{7,6},{8,9},{9,8},{10,11... | collective-permute-start | bytes 294920 | tf_op jit(solution)/shard_map/ppermute | solution.py:14
  5.1 0.0 copy-done
  5.1 0.0 copy-done.3
  5.1 0.3 fusion.21
  5.4 0.0 copy-start.1
  5.4 0.1 collective-permute-start.1
  5.5 0.6 %copy-done.1 = s32[128]{0:T(128)S(1)} copy-done((s32[128]{0:T(128)S(1)}, s32[128]{0:T(128)}, u32[]{:S(2)}) %copy-start.1) | copy-done | bytes 536
  6.0 1.5 %collective-permute-start.2 = (s32[1,128]{1,0:T(1,128)S(1)}, s32[1,128]{1,0:T(1,128)S(1)}, u32[]{:S(2)}, u32[]{:S(2)}) collective-permute-start(s32[1,128]{1,0:T(1,128)S(1)} %bitcast.94), channel_id=1, source_target_pairs={{0,4},{1,5},{2,6},{3,7},{4,0},{5,1},{6,2},{7,3},{8,12},{9,13},{10,... | collective-permute-start | bytes 1544 | tf_op jit(solution)/shard_map/ppermute | solution.py:14
  7.6 0.0 copy-done.2
  7.6 0.0 copy-done.4
  7.6 0.2 fusion.1
  7.8 0.1 stack.50
  7.9 0.4 %collective-permute-done = f16[64,768]{1,0:T(8,128)(2,1)S(1)} collective-permute-done((f16[64,768]{1,0:T(8,128)(2,1)S(1)}, f16[64,768]{1,0:T(8,128)(2,1)S(1)}, u32[]{:S(2)}, u32[]{:S(2)}) %collective-permute-start) | collective-permute-done | bytes 98336 | tf_op jit(solution)/shard_map/ppermute | solution.py:14
  8.3 0.1 multiply_reduce_fusion.1
  8.4 0.1 divide_convert_fusion.1.refs_0_
  8.5 3.3 %collective-permute-start.4 = (bf16[64,768]{1,0:T(8,128)(2,1)S(1)}, bf16[64,768]{1,0:T(8,128)(2,1)S(1)}, u32[]{:S(2)}, u32[]{:S(2)}) collective-permute-start(bf16[64,768]{1,0:T(8,128)(2,1)S(1)} %divide_convert_fusion.1.refs_0_), channel_id=1, source_target_pairs={{0,16},{1,17},{2,18},{3,19},{4,20},{5,21},{6,22},{7,23},{8,24},{9,... | collective-permute-start | bytes 294920 | tf_op jit(solution)/shard_map/ppermute | solution.py:14
  11.8 1.6 %collective-permute-start.6 = (bf16[64,768]{1,0:T(8,128)(2,1)S(1)}, bf16[64,768]{1,0:T(8,128)(2,1)S(1)}, u32[]{:S(2)}, u32[]{:S(2)}) collective-permute-start(bf16[64,768]{1,0:T(8,128)(2,1)S(1)} %divide_convert_fusion.1.refs_0_), channel_id=1, source_target_pairs={{0,8},{1,9},{2,10},{3,11},{4,12},{5,13},{6,14},{7,15},{8,0},{9,1},... | collective-permute-start | bytes 294920 | tf_op jit(solution)/shard_map/ppermute | solution.py:14
  13.4 0.0 collective-permute-start.9
  13.4 0.0 collective-permute-done.1
  13.4 0.1 multiply_reduce_fusion
  13.5 0.1 divide_convert_fusion.refs_1_
  13.7 0.0 collective-permute-done.2.refs_4_
  13.7 1.8 %collective-permute-start.3 = (bf16[128,768]{1,0:T(8,128)(2,1)S(1)}, bf16[128,768]{1,0:T(8,128)(2,1)S(1)}, u32[]{:S(2)}, u32[]{:S(2)}) collective-permute-start(bf16[128,768]{1,0:T(8,128)(2,1)S(1)} %divide_convert_fusion.refs_1_), channel_id=1, source_target_pairs={{0,4},{1,5},{2,6},{3,7},{4,0},{5,1},{6,2},{7,3},{8,12},{9,13},{10,... | collective-permute-start | bytes 589832 | tf_op jit(solution)/shard_map/ppermute | solution.py:14
  15.5 1.6 %collective-permute-done.4.refs_8_ = bf16[64,768]{1,0:T(8,128)(2,1)S(1)} collective-permute-done((bf16[64,768]{1,0:T(8,128)(2,1)S(1)}, bf16[64,768]{1,0:T(8,128)(2,1)S(1)}, u32[]{:S(2)}, u32[]{:S(2)}) %collective-permute-start.4) | collective-permute-done | bytes 98336 | tf_op jit(solution)/shard_map/ppermute | solution.py:14
  17.1 0.0 collective-permute-start.5
  17.1 0.5 %collective-permute-start.8 = (bf16[64,768]{1,0:T(8,128)(2,1)S(1)}, bf16[64,768]{1,0:T(8,128)(2,1)S(1)}, u32[]{:S(2)}, u32[]{:S(2)}) collective-permute-start(bf16[64,768]{1,0:T(8,128)(2,1)S(1)} %collective-permute-done.4.refs_8_), channel_id=1, source_target_pairs={{0,2},{1,3},{2,0},{3,1},{4,6},{5,7},{6,4},{7,5},{8,10},{9,11},{10,... | collective-permute-start | bytes 294920 | tf_op jit(solution)/shard_map/ppermute | solution.py:14
  17.6 0.1 collective-permute-done.6.refs_6_
  17.7 0.0 collective-permute-start.7
  17.7 2.1 %collective-permute-done.9.refs_10_ = bf16[64,768]{1,0:T(8,128)(2,1)S(1)} collective-permute-done((bf16[64,768]{1,0:T(8,128)(2,1)S(1)}, bf16[64,768]{1,0:T(8,128)(2,1)S(1)}, u32[]{:S(2)}, u32[]{:S(2)}) %collective-permute-start.9) | collective-permute-done | bytes 98336 | tf_op jit(solution)/shard_map/ppermute | solution.py:14
  19.8 0.0 collective-permute-start.10
  19.8 0.1 iota_add_fusion
  20.5 0.1 add.149.id_ref
  20.6 0.0 collective-permute-done.5.refs_5_
  20.6 0.0 collective-permute-done.7.refs_7_
  20.6 0.0 collective-permute-done.8.refs_9_
  20.6 0.5 %collective-permute-done.10.refs_11_ = bf16[64,768]{1,0:T(8,128)(2,1)S(1)} collective-permute-done((bf16[64,768]{1,0:T(8,128)(2,1)S(1)}, bf16[64,768]{1,0:T(8,128)(2,1)S(1)}, u32[]{:S(2)}, u32[]{:S(2)}) %collective-permute-start.10) | collective-permute-done | bytes 98336 | tf_op jit(solution)/shard_map/ppermute | solution.py:14
  21.1 0.0 collective-permute-done.3.refs_2_
  21.1 0.7 %shard_map.77 = (f32[2,128]{1,0:T(2,128)S(1)}, f32[2,128]{1,0:T(2,128)S(1)}, f32[2,128]{1,0:T(2,128)S(1)}, f32[2,128]{1,0:T(2,128)S(1)}, f32[2,128]{1,0:T(2,128)S(1)}, /*index=5*/f32[2,128]{1,0:T(2,128)S(1)}) custom-call(f32[1,128]{1,0:T(1,128)S(1)} %broadcast_in_dim.7.scale_ref, s32[1,512]{1,0:T(1,128)S(1)} %add.149.id_ref, ...), custom_call_target="tpu_custom_call" | custom-call | flops 201326592 | bytes 1183232 | tf_op jit(solution)/shard_map/pallas_call | solution.py:72
  21.8 1.6 %collective-permute-start.11 = (f32[2,128]{1,0:T(2,128)S(1)}, f32[2,128]{1,0:T(2,128)S(1)}, u32[]{:S(2)}, u32[]{:S(2)}) collective-permute-start(f32[2,128]{1,0:T(2,128)S(1)} %get-tuple-element.17), channel_id=1, source_target_pairs={{0,4},{1,5},{2,6},{3,7},{4,0},{5,1},{6,2},{7,3},{8,12},{9,13},{10,... | collective-permute-start | bytes 3080 | tf_op jit(solution)/shard_map/ppermute | solution.py:14
  23.4 1.9 %collective-permute-start.13 = (f32[2,256]{1,0:T(2,128)S(1)}, f32[2,256]{1,0:T(2,128)S(1)}, u32[]{:S(2)}, u32[]{:S(2)}) collective-permute-start(f32[2,256]{1,0:T(2,128)S(1)} %pad_maximum_fusion), channel_id=1, source_target_pairs={{0,16},{1,17},{2,18},{3,19},{4,20},{5,21},{6,22},{7,23},{8,24},{9,... | collective-permute-start | bytes 6152 | tf_op jit(solution)/shard_map/ppermute | solution.py:14
  25.3 0.1 collective-permute-done.11
  25.5 2.4 %collective-permute-done.13 = f32[2,256]{1,0:T(2,128)S(1)} collective-permute-done((f32[2,256]{1,0:T(2,128)S(1)}, f32[2,256]{1,0:T(2,128)S(1)}, u32[]{:S(2)}, u32[]{:S(2)}) %collective-permute-start.13) | collective-permute-done | bytes 2080 | tf_op jit(solution)/shard_map/ppermute | solution.py:14
  27.9 0.1 collective-permute-start.14
  28.1 1.9 %collective-permute-start.12 = (f32[2,128]{1,0:T(2,128)S(1)}, f32[2,128]{1,0:T(2,128)S(1)}, u32[]{:S(2)}, u32[]{:S(2)}) collective-permute-start(f32[2,128]{1,0:T(2,128)S(1)} %pad_maximum_fusion.1), channel_id=1, source_target_pairs={{0,1},{1,0},{2,3},{3,2},{4,5},{5,4},{6,7},{7,6},{8,9},{9,8},{10,11... | collective-permute-start | bytes 3080 | tf_op jit(solution)/shard_map/ppermute | solution.py:14
  29.9 1.6 %collective-permute-done.14 = f32[2,128]{1,0:T(2,128)S(1)} collective-permute-done((f32[2,128]{1,0:T(2,128)S(1)}, f32[2,128]{1,0:T(2,128)S(1)}, u32[]{:S(2)}, u32[]{:S(2)}) %collective-permute-start.14) | collective-permute-done | bytes 1056 | tf_op jit(solution)/shard_map/ppermute | solution.py:14
  31.6 0.1 slice.101
  31.7 0.0 collective-permute-start.15
  31.7 0.0 collective-permute-done.12
  31.7 0.6 %bitcast_subtract_fusion.3 = f32[128]{0:T(128)} fusion(f32[1,128]{1,0:T(1,128)S(1)} %get-tuple-element.27, f32[2,128]{1,0:T(2,128)S(1)} %collective-permute-done.12, f32[2,128]{1,0:T(2,128)S(1)} %collective-permute-done.11, f32[2,128]{1,0:T(2,128)S(1)} %get-tuple-element.16), kind=kLoop, calls=%fused_computation.26 | loop fusion | flops 1536 | bytes 3072 | tf_op jit(solution)/shard_map/sub | solution.py:152
  32.2 0.6 %collective-permute-done.15 = f32[2,64]{1,0:T(2,128)S(1)} collective-permute-done((f32[2,64]{1,0:T(2,128)S(1)}, f32[2,64]{1,0:T(2,128)S(1)}, u32[]{:S(2)}, u32[]{:S(2)}) %collective-permute-start.15) | collective-permute-done | bytes 544 | tf_op jit(solution)/shard_map/ppermute | solution.py:14
  32.8 0.5 %bitcast_subtract_fusion = f32[64]{0:T(128)} fusion(f32[2,64]{1,0:T(2,128)S(1)} %collective-permute-done.15, f32[1,128]{1,0:T(1,128)S(1)} %get-tuple-element.23, f32[1,128]{1,0:T(1,128)S(1)} %get-tuple-element.22), kind=kLoop, calls=%fused_computation.18 | loop fusion | flops 448 | bytes 1280 | tf_op jit(solution)/shard_map/sub | solution.py:152
  (11 shorter events, 0.1 us)
Async XLA Ops:
  0.6 4.5 %copy-start = (bf16[512,768]{1,0:T(8,128)(2,1)S(1)}, bf16[512,768]{1,0:T(8,128)(2,1)}, u32[]{:S(2)}) copy-start(bf16[512,768]{1,0:T(8,128)(2,1)} %param.7) | copy-start | bytes 2359300
  0.7 4.4 %copy-start.3 = (bf16[128,512]{1,0:T(8,128)(2,1)S(1)}, bf16[128,512]{1,0:T(8,128)(2,1)}, u32[]{:S(2)}) copy-start(bf16[128,512]{1,0:T(8,128)(2,1)} %param.6) | copy-start | bytes 393220
  2.1 5.5 %copy-start.2 = (bf16[384,768]{1,0:T(8,128)(2,1)S(1)}, bf16[384,768]{1,0:T(8,128)(2,1)}, u32[]{:S(2)}) copy-start(bf16[384,768]{1,0:T(8,128)(2,1)} %param.9) | copy-start | bytes 1769476
  2.1 5.5 %copy-start.4 = (bf16[128,384]{1,0:T(8,128)(2,1)S(1)}, bf16[128,384]{1,0:T(8,128)(2,1)}, u32[]{:S(2)}) copy-start(bf16[128,384]{1,0:T(8,128)(2,1)} %param.8) | copy-start | bytes 294916
  2.1 6.2 %collective-permute-start = (f16[64,768]{1,0:T(8,128)(2,1)S(1)}, f16[64,768]{1,0:T(8,128)(2,1)S(1)}, u32[]{:S(2)}, u32[]{:S(2)}) collective-permute-start(f16[64,768]{1,0:T(8,128)(2,1)S(1)} %convolution_convert_fusion), channel_id=1, source_target_pairs={{0,1},{1,0},{2,3},{3,2},{4,5},{5,4},{6,7},{7,6},{8,9},{9,8},{10,11... | collective-permute-start | bytes 294920 | tf_op jit(solution)/shard_map/ppermute | solution.py:14
  5.4 0.7 %copy-start.1 = (s32[128]{0:T(128)S(1)}, s32[128]{0:T(128)}, u32[]{:S(2)}) copy-start(s32[128]{0:T(128)} %param.10) | copy-start | bytes 1540
  5.4 8.0 %collective-permute-start.1 = (f16[128,768]{1,0:T(8,128)(2,1)S(1)}, f16[128,768]{1,0:T(8,128)(2,1)S(1)}, u32[]{:S(2)}, u32[]{:S(2)}) collective-permute-start(f16[128,768]{1,0:T(8,128)(2,1)S(1)} %get-tuple-element.28), channel_id=1, source_target_pairs={{0,1},{1,0},{2,3},{3,2},{4,5},{5,4},{6,7},{7,6},{8,9},{9,8},{10,11... | collective-permute-start | bytes 589832 | tf_op jit(solution)/shard_map/ppermute | solution.py:14
  6.0 7.6 %collective-permute-start.2 = (s32[1,128]{1,0:T(1,128)S(1)}, s32[1,128]{1,0:T(1,128)S(1)}, u32[]{:S(2)}, u32[]{:S(2)}) collective-permute-start(s32[1,128]{1,0:T(1,128)S(1)} %bitcast.94), channel_id=1, source_target_pairs={{0,4},{1,5},{2,6},{3,7},{4,0},{5,1},{6,2},{7,3},{8,12},{9,13},{10,... | collective-permute-start | bytes 1544 | tf_op jit(solution)/shard_map/ppermute | solution.py:14
  8.5 8.6 %collective-permute-start.4 = (bf16[64,768]{1,0:T(8,128)(2,1)S(1)}, bf16[64,768]{1,0:T(8,128)(2,1)S(1)}, u32[]{:S(2)}, u32[]{:S(2)}) collective-permute-start(bf16[64,768]{1,0:T(8,128)(2,1)S(1)} %divide_convert_fusion.1.refs_0_), channel_id=1, source_target_pairs={{0,16},{1,17},{2,18},{3,19},{4,20},{5,21},{6,22},{7,23},{8,24},{9,... | collective-permute-start | bytes 294920 | tf_op jit(solution)/shard_map/ppermute | solution.py:14
  11.8 5.9 %collective-permute-start.6 = (bf16[64,768]{1,0:T(8,128)(2,1)S(1)}, bf16[64,768]{1,0:T(8,128)(2,1)S(1)}, u32[]{:S(2)}, u32[]{:S(2)}) collective-permute-start(bf16[64,768]{1,0:T(8,128)(2,1)S(1)} %divide_convert_fusion.1.refs_0_), channel_id=1, source_target_pairs={{0,8},{1,9},{2,10},{3,11},{4,12},{5,13},{6,14},{7,15},{8,0},{9,1},... | collective-permute-start | bytes 294920 | tf_op jit(solution)/shard_map/ppermute | solution.py:14
  13.4 6.4 %collective-permute-start.9 = (bf16[64,768]{1,0:T(8,128)(2,1)S(1)}, bf16[64,768]{1,0:T(8,128)(2,1)S(1)}, u32[]{:S(2)}, u32[]{:S(2)}) collective-permute-start(bf16[64,768]{1,0:T(8,128)(2,1)S(1)} %divide_convert_fusion.1.refs_0_), channel_id=1, source_target_pairs={{0,24},{1,25},{2,26},{3,27},{4,28},{5,29},{6,30},{7,31},{8,16},{9,... | collective-permute-start | bytes 294920 | tf_op jit(solution)/shard_map/ppermute | solution.py:14
  13.7 7.4 %collective-permute-start.3 = (bf16[128,768]{1,0:T(8,128)(2,1)S(1)}, bf16[128,768]{1,0:T(8,128)(2,1)S(1)}, u32[]{:S(2)}, u32[]{:S(2)}) collective-permute-start(bf16[128,768]{1,0:T(8,128)(2,1)S(1)} %divide_convert_fusion.refs_1_), channel_id=1, source_target_pairs={{0,4},{1,5},{2,6},{3,7},{4,0},{5,1},{6,2},{7,3},{8,12},{9,13},{10,... | collective-permute-start | bytes 589832 | tf_op jit(solution)/shard_map/ppermute | solution.py:14
  17.1 3.5 %collective-permute-start.5 = (bf16[64,768]{1,0:T(8,128)(2,1)S(1)}, bf16[64,768]{1,0:T(8,128)(2,1)S(1)}, u32[]{:S(2)}, u32[]{:S(2)}) collective-permute-start(bf16[64,768]{1,0:T(8,128)(2,1)S(1)} %divide_convert_fusion.1.refs_0_), channel_id=1, source_target_pairs={{0,2},{1,3},{2,0},{3,1},{4,6},{5,7},{6,4},{7,5},{8,10},{9,11},{10,... | collective-permute-start | bytes 294920 | tf_op jit(solution)/shard_map/ppermute | solution.py:14
  17.1 3.5 %collective-permute-start.8 = (bf16[64,768]{1,0:T(8,128)(2,1)S(1)}, bf16[64,768]{1,0:T(8,128)(2,1)S(1)}, u32[]{:S(2)}, u32[]{:S(2)}) collective-permute-start(bf16[64,768]{1,0:T(8,128)(2,1)S(1)} %collective-permute-done.4.refs_8_), channel_id=1, source_target_pairs={{0,2},{1,3},{2,0},{3,1},{4,6},{5,7},{6,4},{7,5},{8,10},{9,11},{10,... | collective-permute-start | bytes 294920 | tf_op jit(solution)/shard_map/ppermute | solution.py:14
  17.7 2.9 %collective-permute-start.7 = (bf16[64,768]{1,0:T(8,128)(2,1)S(1)}, bf16[64,768]{1,0:T(8,128)(2,1)S(1)}, u32[]{:S(2)}, u32[]{:S(2)}) collective-permute-start(bf16[64,768]{1,0:T(8,128)(2,1)S(1)} %collective-permute-done.6.refs_6_), channel_id=1, source_target_pairs={{0,2},{1,3},{2,0},{3,1},{4,6},{5,7},{6,4},{7,5},{8,10},{9,11},{10,... | collective-permute-start | bytes 294920 | tf_op jit(solution)/shard_map/ppermute | solution.py:14
  19.8 1.3 %collective-permute-start.10 = (bf16[64,768]{1,0:T(8,128)(2,1)S(1)}, bf16[64,768]{1,0:T(8,128)(2,1)S(1)}, u32[]{:S(2)}, u32[]{:S(2)}) collective-permute-start(bf16[64,768]{1,0:T(8,128)(2,1)S(1)} %collective-permute-done.9.refs_10_), channel_id=1, source_target_pairs={{0,2},{1,3},{2,0},{3,1},{4,6},{5,7},{6,4},{7,5},{8,10},{9,11},{10,... | collective-permute-start | bytes 294920 | tf_op jit(solution)/shard_map/ppermute | solution.py:14
  21.8 3.6 %collective-permute-start.11 = (f32[2,128]{1,0:T(2,128)S(1)}, f32[2,128]{1,0:T(2,128)S(1)}, u32[]{:S(2)}, u32[]{:S(2)}) collective-permute-start(f32[2,128]{1,0:T(2,128)S(1)} %get-tuple-element.17), channel_id=1, source_target_pairs={{0,4},{1,5},{2,6},{3,7},{4,0},{5,1},{6,2},{7,3},{8,12},{9,13},{10,... | collective-permute-start | bytes 3080 | tf_op jit(solution)/shard_map/ppermute | solution.py:14
  23.4 4.5 %collective-permute-start.13 = (f32[2,256]{1,0:T(2,128)S(1)}, f32[2,256]{1,0:T(2,128)S(1)}, u32[]{:S(2)}, u32[]{:S(2)}) collective-permute-start(f32[2,256]{1,0:T(2,128)S(1)} %pad_maximum_fusion), channel_id=1, source_target_pairs={{0,16},{1,17},{2,18},{3,19},{4,20},{5,21},{6,22},{7,23},{8,24},{9,... | collective-permute-start | bytes 6152 | tf_op jit(solution)/shard_map/ppermute | solution.py:14
  27.9 3.6 %collective-permute-start.14 = (f32[2,128]{1,0:T(2,128)S(1)}, f32[2,128]{1,0:T(2,128)S(1)}, u32[]{:S(2)}, u32[]{:S(2)}) collective-permute-start(f32[2,128]{1,0:T(2,128)S(1)} %pad_maximum_fusion.2), channel_id=1, source_target_pairs={{0,8},{1,9},{2,10},{3,11},{4,12},{5,13},{6,14},{7,15},{8,0},{9,1},... | collective-permute-start | bytes 3080 | tf_op jit(solution)/shard_map/ppermute | solution.py:14
  28.1 3.6 %collective-permute-start.12 = (f32[2,128]{1,0:T(2,128)S(1)}, f32[2,128]{1,0:T(2,128)S(1)}, u32[]{:S(2)}, u32[]{:S(2)}) collective-permute-start(f32[2,128]{1,0:T(2,128)S(1)} %pad_maximum_fusion.1), channel_id=1, source_target_pairs={{0,1},{1,0},{2,3},{3,2},{4,5},{5,4},{6,7},{7,6},{8,9},{9,8},{10,11... | collective-permute-start | bytes 3080 | tf_op jit(solution)/shard_map/ppermute | solution.py:14
  31.7 1.1 %collective-permute-start.15 = (f32[2,64]{1,0:T(2,128)S(1)}, f32[2,64]{1,0:T(2,128)S(1)}, u32[]{:S(2)}, u32[]{:S(2)}) collective-permute-start(f32[2,64]{1,0:T(2,128)S(1)} %slice.101), channel_id=1, source_target_pairs={{0,2},{1,3},{2,0},{3,1},{4,6},{5,7},{6,4},{7,5},{8,10},{9,11},{10,... | collective-permute-start | bytes 1544 | tf_op jit(solution)/shard_map/ppermute | solution.py:14

commit v4 on v3

--- a/solution.py
+++ b/solution.py
@@ -25,17 +25,16 @@
     return jnp.stack([top + jnp.log(total), sum(s[1] for s in stats)])
 
 
-def stats_kernel(n_image, n_text, scale_ref, id_ref, *refs):
+def stats_kernel(n_image, places, n_col, scale_ref, id_ref, *refs):
     refs = list(refs)
     texts = [refs.pop(0)]
     images = [refs.pop(0) for _ in range(n_image)]
     pairs = [refs.pop(0) for _ in range(n_image)]
-    texts += [refs.pop(0) for _ in range(n_text - 1)]
-    col_out = [refs.pop(0) for _ in range(len(refs) - n_image)]
-    row_out = refs
+    texts += [refs.pop(0) for _ in places[1:]]
+    texts = [text for _, text in sorted(zip(places, texts), key=lambda pair: pair[0])]
+    col_out, row_out = refs[:n_col], refs[n_col:]
     rows = images[0].shape[0]
     half = texts[0].shape[0]
-    per_out = n_text // len(col_out)
     image = jnp.concatenate([r[...] for r in images], axis=0)
     text = jnp.concatenate([r[...] for r in texts], axis=0)
     logits = scale_ref[0:1, 0:1] * lax.dot_general(
@@ -43,38 +42,45 @@
     )
     ids = id_ref[...]
     pair = jnp.concatenate([jnp.broadcast_to(r[...], (rows, rows)).T for r in pairs], axis=0)
-    pair = jnp.concatenate([pair] * (n_text * half // rows), axis=1)
+    pair = jnp.concatenate([pair] * (len(texts) * half // rows), axis=1)
     picked = jnp.where(pair == ids, logits, 0.0)
 
     top = jnp.max(logits, axis=0, keepdims=True)
     lse = top + jnp.log(jnp.sum(jnp.exp(logits - top), axis=0, keepdims=True))
     positive = jnp.sum(picked, axis=0, keepdims=True)
-    for k, out in enumerate(col_out):
-        lanes = slice(k * per_out * half, (k + 1) * per_out * half)
-        out[0:1, :] = lse[:, lanes]
-        out[1:2, :] = positive[:, lanes]
+    write(col_out, lse, positive)
 
     top = jnp.max(logits, axis=1, keepdims=True)
     lse = top + jnp.log(jnp.sum(jnp.exp(logits - top), axis=1, keepdims=True))
     positive = jnp.sum(picked, axis=1, keepdims=True)
-    for k, out in enumerate(row_out):
-        block = slice(k * rows, (k + 1) * rows)
-        lane = lax.broadcasted_iota(jnp.int32, (rows, rows), 1)
-        both = jnp.where(lane == 0, lse[block], positive[block]).T
-        out[...] = both[0:2]
+    lane = lax.broadcasted_iota(jnp.int32, (image.shape[0], rows), 1)
+    both = jnp.where(lane == 0, lse, positive).T
+    write(row_out, both[0:1], both[1:2])
 
 
-def block_stats(scale, ids, images, pairs, texts, n_out):
+def write(outs, lse, positive):
+    count = lse.shape[1] // len(outs)
+    for k, out in enumerate(outs):
+        out[0:1, :] = lse[:, k * count : (k + 1) * count]
+        out[1:2, :] = positive[:, k * count : (k + 1) * count]
+
+
+def pieces(count, n):
+    return [jax.ShapeDtypeStruct((2, count // n), jnp.float32)] * n
+
+
+def block_stats(scale, ids, images, pairs, texts, places):
     rows = images[0].shape[0]
     count = len(texts) * texts[0].shape[0]
     vmem = pl.BlockSpec(memory_space=pltpu.VMEM)
     operands = [scale, ids, texts[0], *images, *pairs, *texts[1:]]
+    col = pieces(count, min(2, len(texts)))
+    row = pieces(rows * len(images), min(2, len(images)))
     out = pl.pallas_call(
-        functools.partial(stats_kernel, len(images), len(texts)),
-        out_shape=[jax.ShapeDtypeStruct((2, count // n_out), jnp.float32)] * n_out
-        + [jax.ShapeDtypeStruct((2, rows), jnp.float32)] * len(images),
+        functools.partial(stats_kernel, len(images), places, len(col)),
+        out_shape=col + row,
         in_specs=[vmem] * len(operands),
-        out_specs=[vmem] * (n_out + len(images)),
+        out_specs=[vmem] * len(col + row),
         compiler_params=pltpu.CompilerParams(vmem_limit_bytes=48 * 2**20),
         cost_estimate=pl.CostEstimate(
             flops=2 * rows * len(images) * count * images[0].shape[1],
@@ -82,7 +88,42 @@
             transcendentals=2 * rows * len(images) * count,
         ),
     )(*operands)
-    return out[:n_out], out[n_out:]
+    return out[: len(col)], out[len(col) :]
+
+
+def joined(parts):
+    top = functools.reduce(jnp.maximum, [p[0:1, :] for p in parts])
+    total = sum(jnp.exp(p[0:1, :] - top) for p in parts)
+    return top + jnp.log(total), sum(p[1:2, :] for p in parts)
+
+
+def join_kernel(counts, splits, *refs):
+    refs = list(refs)
+    groups = [[refs.pop(0) for _ in range(n)] for n in counts]
+    for parts, n in zip(groups, splits):
+        lse, positive = joined(parts)
+        if n:
+            write([refs.pop(0) for _ in range(n)], lse, positive)
+        else:
+            refs.pop(0)[...] = lse - positive
+
+
+def join(groups, splits):
+    vmem = pl.BlockSpec(memory_space=pltpu.VMEM)
+    parts = [part for group in groups for part in group]
+    shapes = [
+        pieces(g[0].shape[1], n) if n else [jax.ShapeDtypeStruct((1, g[0].shape[1]), jnp.float32)]
+        for g, n in zip(groups, splits)
+    ]
+    flat = [s for shape in shapes for s in shape]
+    out = list(pl.pallas_call(
+        functools.partial(join_kernel, [len(g) for g in groups], splits),
+        out_shape=flat,
+        in_specs=[vmem] * len(parts),
+        out_specs=[vmem] * len(flat),
+        compiler_params=pltpu.CompilerParams(vmem_limit_bytes=4 * 2**20),
+    )(*parts))
+    return [[out.pop(0) for _ in shape] for shape in shapes]
 
 
 def on_device(image_feat, image_proj, text_feat, text_proj, pair_index, logit_scale):
@@ -121,35 +162,29 @@
 
     texts[0] = text_emb
     late, _ = lax.optimization_barrier((text_emb, texts[z_order[1]]))
-    both = [
-        text for j in range(far)
-        for text in [texts[j]] + [exchange(late if j == 0 else texts[j], c) for c in range(1, core)]
-    ]
-    owner = jnp.stack([dp_index ^ (near * j + c) for j in range(far) for c in range(core)])
+    blocks = {(0, j): texts[j] for j in range(far)}
+    for c in range(1, core):
+        blocks.update({(c, j): exchange(texts[j] if j else late, c) for j in range(far)})
+    z_names = sorted(z_order, key=lambda j: (j != far // 2, -j))
+    order = [(0, 0)] + [(c, j) for j in z_names for c in range(core)] + [(c, 0) for c in range(1, core)]
+    owner = jnp.stack([dp_index ^ (near * j + c) for c in range(core) for j in range(far)])
     starts = (owner * rows + mp_index * half).astype(jnp.int32)
     ids = (starts[:, None] + jnp.arange(half, dtype=jnp.int32)[None]).reshape(1, -1)
     scale = jnp.broadcast_to(logit_scale[None], (1, rows))
-    col, row = block_stats(scale, ids, images, pairs, both, far)
+    col, row = block_stats(
+        scale, ids, images, pairs, [blocks[k] for k in order], [c * far + j for c, j in order]
+    )
 
-    k = far
-    col = list(col)
-    while k > 1:
-        k //= 2
-        other = exchange(jnp.concatenate(col[k : 2 * k], axis=1), near * k)
-        n = core * half
-        col = [join([col[j], other[:, j * n : (j + 1) * n]]) for j in range(k)]
-    col = col[0]
-    row = list(row)
-    k = near // core
-    while k > 1:
-        k //= 2
-        row = [join([row[s], exchange(row[s + k], core * k)]) for s in range(k)]
-    row = join([row[0]] + [exchange(row[0], 0, m) for m in range(1, mp)])
-    col = join(
-        [col[:, :half]]
-        + [exchange(col[:, c * half : (c + 1) * half], c) for c in range(1, core)]
-    )
-    return (row[0] - row[1], col[0] - col[1])
+    col_steps = [1] * (core > 1) + [near << k for k in reversed(range(far.bit_length() - 1))]
+    row_steps = [core << k for k in reversed(range((near // core).bit_length() - 1))]
+    while len(col_steps) > 1:
+        ((*col,),) = join([[col[0], exchange(col[1], col_steps.pop(0))]], [2])
+    while row_steps:
+        ((*row,),) = join([[row[0], exchange(row[1], row_steps.pop(0))]], [2 if row_steps else 1])
+    row = [row[0]] + [exchange(row[0], 0, m) for m in range(1, mp)]
+    col = [col[0], exchange(col[1], col_steps.pop(0))]
+    (col_loss,), (row_loss,) = join([col, row], [0, 0])
+    return (row_loss.reshape(-1), col_loss.reshape(-1))
 
 
 def solution(mesh):

time: 33.5 us -> 32 us (0.955)
  waiting for transfers between devices: 9.45 us -> 6.74 us
  starting transfers between devices: 17.3 us -> 19.2 us
  other arithmetic: 1.74 us -> 0.58 us
  Pallas kernels: 0.73 us -> 1.37 us
    ppermute x16, waiting for transfers between devices: 9.45 us -> 6.74 us  [exchange(): return lax.ppermute(value, ('dp', 'mp'), pairs)]
    ppermute x16, starting transfers between devices: 17.3 us -> 19.2 us  [exchange(): return lax.ppermute(value, ('dp', 'mp'), pairs)]
    sub x2 -> x0, other arithmetic: 1.08 us -> none  [on_device(): return (row[0] - row[1], col[0] - col[1])]
    pallas_call x1 -> x5, Pallas kernels: 0.73 us -> 1.37 us  [the longest x1 0.73 us: block_stats(): pl.pallas_call(functools.partial(stats_kernel, len(images), places, len(c...]
  transfers between devices with their start and end apart: 16 -> 16, of which waited for: 9 -> 7; matrix products, arithmetic and copies ran while one was open for 6% -> 4% of each run, Pallas kernels for 0% -> 0%
where the time goes in v4:
time: 32 us; the launch traced here: 31.9 us
  starting transfers between devices  19.2 us (60%)
  waiting for transfers between devices  6.74 us (21%)
  matrix products  1.88 us (6%)
  between operations  1.4 us (4%)
  Pallas kernels  1.37 us (4%)
  local copies, waits for them, and re-layouts  0.75 us (2%)
  other arithmetic  0.58 us (2%)
    ppermute x16, starting transfers between devices, exchange(): return lax.ppermute(value, ('dp', 'mp'), pairs)  19.2 us
    ppermute x16, waiting for transfers between devices, exchange(): return lax.ppermute(value, ('dp', 'mp'), pairs)  6.74 us
    dot_general x2, matrix products, text_rows(): return jnp.dot(mine, text_proj, preferred_element_type=jnp.float32)  1.61 us
    pallas_call x1, Pallas kernels, block_stats(): pl.pallas_call(functools.partial(stats_kernel, len(images), places, len(c...  0.73 us
    pallas_call x4, Pallas kernels, join(): pl.pallas_call(functools.partial(join_kernel, [len(g) for g in groups], s...  0.64 us
  transfers between devices with their start and end apart: 16, of which 7 were waited for; matrix products, arithmetic and copies ran while one was open for 4% of the time, Pallas kernels for 0%

profile of v4, /device:TPU:0, one launch (start us, length us, event | category | flops | bytes accessed | tf_op | source)
XLA Modules:
  0.0 31.9 jit_solution(9931599507854040361)
XLA Ops:
  0.6 0.0 copy-start
  0.7 0.0 copy-start.3
  0.7 1.4 %convolution_convert_fusion = f16[64,768]{1,0:T(8,128)(2,1)S(1)} fusion(bf16[384,768]{1,0:T(8,128)(2,1)} %param.9, bf16[128,384]{1,0:T(8,128)(2,1)} %param.8, s32[]{:T(128)S(6)} %select_n.7), kind=kOutput, calls=%fused_computation | convolution fusion | flops 37797888 | bytes 737284 | tf_op jit(solution)/shard_map/dot_general | solution.py:144
  2.1 0.0 copy-start.2
  2.1 0.0 copy-start.4
  2.1 3.0 %collective-permute-start = (f16[64,768]{1,0:T(8,128)(2,1)S(1)}, f16[64,768]{1,0:T(8,128)(2,1)S(1)}, u32[]{:S(2)}, u32[]{:S(2)}) collective-permute-start(f16[64,768]{1,0:T(8,128)(2,1)S(1)} %convolution_convert_fusion), channel_id=1, source_target_pairs={{0,1},{1,0},{2,3},{3,2},{4,5},{5,4},{6,7},{7,6},{8,9},{9,8},{10,11... | collective-permute-start | bytes 294920 | tf_op jit(solution)/shard_map/ppermute | solution.py:14
  5.1 0.0 copy-done
  5.1 0.0 copy-done.3
  5.1 0.3 fusion.5
  5.4 0.0 copy-start.1
  5.4 0.1 collective-permute-start.1
  5.5 0.6 %copy-done.1 = s32[128]{0:T(128)S(1)} copy-done((s32[128]{0:T(128)S(1)}, s32[128]{0:T(128)}, u32[]{:S(2)}) %copy-start.1) | copy-done | bytes 536
  6.0 1.5 %collective-permute-start.2 = (s32[1,128]{1,0:T(1,128)S(1)}, s32[1,128]{1,0:T(1,128)S(1)}, u32[]{:S(2)}, u32[]{:S(2)}) collective-permute-start(s32[1,128]{1,0:T(1,128)S(1)} %bitcast.17), channel_id=1, source_target_pairs={{0,4},{1,5},{2,6},{3,7},{4,0},{5,1},{6,2},{7,3},{8,12},{9,13},{10,... | collective-permute-start | bytes 1544 | tf_op jit(solution)/shard_map/ppermute | solution.py:14
  7.6 0.0 copy-done.2
  7.6 0.0 copy-done.4
  7.6 0.2 fusion.1
  7.8 0.1 stack.35
  7.9 0.4 %collective-permute-done = f16[64,768]{1,0:T(8,128)(2,1)S(1)} collective-permute-done((f16[64,768]{1,0:T(8,128)(2,1)S(1)}, f16[64,768]{1,0:T(8,128)(2,1)S(1)}, u32[]{:S(2)}, u32[]{:S(2)}) %collective-permute-start) | collective-permute-done | bytes 98336 | tf_op jit(solution)/shard_map/ppermute | solution.py:14
  8.3 0.1 multiply_reduce_fusion.1
  8.4 0.1 divide_convert_fusion.1.refs_0_
  8.5 3.3 %collective-permute-start.4 = (bf16[64,768]{1,0:T(8,128)(2,1)S(1)}, bf16[64,768]{1,0:T(8,128)(2,1)S(1)}, u32[]{:S(2)}, u32[]{:S(2)}) collective-permute-start(bf16[64,768]{1,0:T(8,128)(2,1)S(1)} %divide_convert_fusion.1.refs_0_), channel_id=1, source_target_pairs={{0,16},{1,17},{2,18},{3,19},{4,20},{5,21},{6,22},{7,23},{8,24},{9,... | collective-permute-start | bytes 294920 | tf_op jit(solution)/shard_map/ppermute | solution.py:14
  11.8 1.3 %collective-permute-start.6 = (bf16[64,768]{1,0:T(8,128)(2,1)S(1)}, bf16[64,768]{1,0:T(8,128)(2,1)S(1)}, u32[]{:S(2)}, u32[]{:S(2)}) collective-permute-start(bf16[64,768]{1,0:T(8,128)(2,1)S(1)} %divide_convert_fusion.1.refs_0_), channel_id=1, source_target_pairs={{0,24},{1,25},{2,26},{3,27},{4,28},{5,29},{6,30},{7,31},{8,16},{9,... | collective-permute-start | bytes 294920 | tf_op jit(solution)/shard_map/ppermute | solution.py:14
  13.2 0.2 collective-permute-start.8
  13.4 0.0 collective-permute-done.1
  13.4 0.1 multiply_reduce_fusion
  13.5 0.1 divide_convert_fusion.refs_1_
  13.7 0.0 collective-permute-done.2.refs_4_
  13.7 1.6 %collective-permute-start.3 = (bf16[128,768]{1,0:T(8,128)(2,1)S(1)}, bf16[128,768]{1,0:T(8,128)(2,1)S(1)}, u32[]{:S(2)}, u32[]{:S(2)}) collective-permute-start(bf16[128,768]{1,0:T(8,128)(2,1)S(1)} %divide_convert_fusion.refs_1_), channel_id=1, source_target_pairs={{0,4},{1,5},{2,6},{3,7},{4,0},{5,1},{6,2},{7,3},{8,12},{9,13},{10,... | collective-permute-start | bytes 589832 | tf_op jit(solution)/shard_map/ppermute | solution.py:14
  15.3 3.4 %collective-permute-done.4.refs_5_ = bf16[64,768]{1,0:T(8,128)(2,1)S(1)} collective-permute-done((bf16[64,768]{1,0:T(8,128)(2,1)S(1)}, bf16[64,768]{1,0:T(8,128)(2,1)S(1)}, u32[]{:S(2)}, u32[]{:S(2)}) %collective-permute-start.4) | collective-permute-done | bytes 98336 | tf_op jit(solution)/shard_map/ppermute | solution.py:14
  18.6 0.0 collective-permute-start.10
  18.6 0.5 %collective-permute-start.5 = (bf16[64,768]{1,0:T(8,128)(2,1)S(1)}, bf16[64,768]{1,0:T(8,128)(2,1)S(1)}, u32[]{:S(2)}, u32[]{:S(2)}) collective-permute-start(bf16[64,768]{1,0:T(8,128)(2,1)S(1)} %collective-permute-done.4.refs_5_), channel_id=1, source_target_pairs={{0,2},{1,3},{2,0},{3,1},{4,6},{5,7},{6,4},{7,5},{8,10},{9,11},{10,... | collective-permute-start | bytes 294920 | tf_op jit(solution)/shard_map/ppermute | solution.py:14
  19.1 0.0 collective-permute-done.6.refs_7_
  19.1 0.0 collective-permute-start.7
  19.1 0.1 collective-permute-done.8.refs_9_
  19.2 0.4 %collective-permute-start.9 = (bf16[64,768]{1,0:T(8,128)(2,1)S(1)}, bf16[64,768]{1,0:T(8,128)(2,1)S(1)}, u32[]{:S(2)}, u32[]{:S(2)}) collective-permute-start(bf16[64,768]{1,0:T(8,128)(2,1)S(1)} %collective-permute-done.8.refs_9_), channel_id=1, source_target_pairs={{0,2},{1,3},{2,0},{3,1},{4,6},{5,7},{6,4},{7,5},{8,10},{9,11},{10,... | collective-permute-start | bytes 294920 | tf_op jit(solution)/shard_map/ppermute | solution.py:14
  19.6 0.1 iota_add_fusion
  20.4 0.1 add.72.id_ref
  20.4 0.0 collective-permute-done.5.refs_6_
  20.4 0.0 collective-permute-done.7.refs_8_
  20.4 0.1 collective-permute-done.9.refs_10_
  20.6 0.0 collective-permute-done.10.refs_11_
  20.6 0.0 collective-permute-done.3.refs_2_
  20.6 0.7 %shard_map.77 = (f32[2,256]{1,0:T(2,128)S(1)}, f32[2,256]{1,0:T(2,128)S(1)}, f32[2,128]{1,0:T(2,128)S(1)}, f32[2,128]{1,0:T(2,128)S(1)}) custom-call(f32[1,128]{1,0:T(1,128)S(1)} %broadcast_in_dim.7.scale_ref, s32[1,512]{1,0:T(1,128)S(1)} %add.72.id_ref, bf16[64,768]{1,0:T(8,128)(2,1)S(1)} %divide_convert_fusion.1.refs_0_, ...), custom_call_target="tpu_custom_call" | custom-call | flops 201326592 | bytes 1183232 | tf_op jit(solution)/shard_map/pallas_call | solution.py:79
  21.3 0.4 %collective-permute-start.11 = (f32[2,256]{1,0:T(2,128)S(1)}, f32[2,256]{1,0:T(2,128)S(1)}, u32[]{:S(2)}, u32[]{:S(2)}) collective-permute-start(f32[2,256]{1,0:T(2,128)S(1)} %get-tuple-element.21), channel_id=1, source_target_pairs={{0,2},{1,3},{2,0},{3,1},{4,6},{5,7},{6,4},{7,5},{8,10},{9,11},{10,... | collective-permute-start | bytes 6152 | tf_op jit(solution)/shard_map/ppermute | solution.py:14
  21.7 1.4 %collective-permute-start.14 = (f32[2,128]{1,0:T(2,128)S(1)}, f32[2,128]{1,0:T(2,128)S(1)}, u32[]{:S(2)}, u32[]{:S(2)}) collective-permute-start(f32[2,128]{1,0:T(2,128)S(1)} %get-tuple-element.27), channel_id=1, source_target_pairs={{0,4},{1,5},{2,6},{3,7},{4,0},{5,1},{6,2},{7,3},{8,12},{9,13},{10,... | collective-permute-start | bytes 3080 | tf_op jit(solution)/shard_map/ppermute | solution.py:14
  23.1 0.0 collective-permute-done.11.refs_1_
  23.1 2.8 %collective-permute-start.12 = (f32[2,128]{1,0:T(2,128)S(1)}, f32[2,128]{1,0:T(2,128)S(1)}, u32[]{:S(2)}, u32[]{:S(2)}) collective-permute-start(f32[2,128]{1,0:T(2,128)S(1)} %get-tuple-element.23), channel_id=1, source_target_pairs={{0,16},{1,17},{2,18},{3,19},{4,20},{5,21},{6,22},{7,23},{8,24},{9,... | collective-permute-start | bytes 3080 | tf_op jit(solution)/shard_map/ppermute | solution.py:14
  25.9 0.0 collective-permute-done.14.refs_1_
  25.9 1.6 %collective-permute-start.15 = (f32[2,128]{1,0:T(2,128)S(1)}, f32[2,128]{1,0:T(2,128)S(1)}, u32[]{:S(2)}, u32[]{:S(2)}) collective-permute-start(f32[2,128]{1,0:T(2,128)S(1)} %shard_map.80.refs_2_), channel_id=1, source_target_pairs={{0,1},{1,0},{2,3},{3,2},{4,5},{5,4},{6,7},{7,6},{8,9},{9,8},{10,11... | collective-permute-start | bytes 3080 | tf_op jit(solution)/shard_map/ppermute | solution.py:14
  27.5 0.2 collective-permute-done.12.refs_1_
  27.7 0.1 shard_map.79
  27.8 1.0 %collective-permute-start.13 = (f32[2,64]{1,0:T(2,128)S(1)}, f32[2,64]{1,0:T(2,128)S(1)}, u32[]{:S(2)}, u32[]{:S(2)}) collective-permute-start(f32[2,64]{1,0:T(2,128)S(1)} %get-tuple-element.25), channel_id=1, source_target_pairs={{0,8},{1,9},{2,10},{3,11},{4,12},{5,13},{6,14},{7,15},{8,0},{9,1},... | collective-permute-start | bytes 1544 | tf_op jit(solution)/shard_map/ppermute | solution.py:14
  28.8 0.8 %collective-permute-done.15.refs_3_ = f32[2,128]{1,0:T(2,128)S(1)} collective-permute-done((f32[2,128]{1,0:T(2,128)S(1)}, f32[2,128]{1,0:T(2,128)S(1)}, u32[]{:S(2)}, u32[]{:S(2)}) %collective-permute-start.15) | collective-permute-done | bytes 1056 | tf_op jit(solution)/shard_map/ppermute | solution.py:14
  29.6 1.8 %collective-permute-done.13.refs_1_ = f32[2,64]{1,0:T(2,128)S(1)} collective-permute-done((f32[2,64]{1,0:T(2,128)S(1)}, f32[2,64]{1,0:T(2,128)S(1)}, u32[]{:S(2)}, u32[]{:S(2)}) %collective-permute-start.13) | collective-permute-done | bytes 544 | tf_op jit(solution)/shard_map/ppermute | solution.py:14
  31.3 0.5 %shard_map.81 = (f32[1,64]{1,0:T(1,128)}, f32[1,128]{1,0:T(1,128)}) custom-call(f32[2,64]{1,0:T(2,128)S(1)} %get-tuple-element.24.refs_0_, f32[2,64]{1,0:T(2,128)S(1)} %collective-permute-done.13.refs_1_, f32[2,128]{1,0:T(2,128)S(1)} %shard_map.80.refs_2_, f32[2,128]{1,0:T(2,128)S(1)} %collective-permute-done.15.refs_3_), custom_call_target="tpu_custom_call" | custom-call | tf_op jit(solution)/shard_map/pallas_call | solution.py:119
  (6 shorter events, 0.1 us)
Async XLA Ops:
  0.6 4.5 %copy-start = (bf16[512,768]{1,0:T(8,128)(2,1)S(1)}, bf16[512,768]{1,0:T(8,128)(2,1)}, u32[]{:S(2)}) copy-start(bf16[512,768]{1,0:T(8,128)(2,1)} %param.7) | copy-start | bytes 2359300
  0.7 4.4 %copy-start.3 = (bf16[128,512]{1,0:T(8,128)(2,1)S(1)}, bf16[128,512]{1,0:T(8,128)(2,1)}, u32[]{:S(2)}) copy-start(bf16[128,512]{1,0:T(8,128)(2,1)} %param.6) | copy-start | bytes 393220
  2.1 5.5 %copy-start.2 = (bf16[384,768]{1,0:T(8,128)(2,1)S(1)}, bf16[384,768]{1,0:T(8,128)(2,1)}, u32[]{:S(2)}) copy-start(bf16[384,768]{1,0:T(8,128)(2,1)} %param.9) | copy-start | bytes 1769476
  2.1 5.5 %copy-start.4 = (bf16[128,384]{1,0:T(8,128)(2,1)S(1)}, bf16[128,384]{1,0:T(8,128)(2,1)}, u32[]{:S(2)}) copy-start(bf16[128,384]{1,0:T(8,128)(2,1)} %param.8) | copy-start | bytes 294916
  2.1 6.2 %collective-permute-start = (f16[64,768]{1,0:T(8,128)(2,1)S(1)}, f16[64,768]{1,0:T(8,128)(2,1)S(1)}, u32[]{:S(2)}, u32[]{:S(2)}) collective-permute-start(f16[64,768]{1,0:T(8,128)(2,1)S(1)} %convolution_convert_fusion), channel_id=1, source_target_pairs={{0,1},{1,0},{2,3},{3,2},{4,5},{5,4},{6,7},{7,6},{8,9},{9,8},{10,11... | collective-permute-start | bytes 294920 | tf_op jit(solution)/shard_map/ppermute | solution.py:14
  5.4 0.7 %copy-start.1 = (s32[128]{0:T(128)S(1)}, s32[128]{0:T(128)}, u32[]{:S(2)}) copy-start(s32[128]{0:T(128)} %param.10) | copy-start | bytes 1540
  5.4 8.0 %collective-permute-start.1 = (f16[128,768]{1,0:T(8,128)(2,1)S(1)}, f16[128,768]{1,0:T(8,128)(2,1)S(1)}, u32[]{:S(2)}, u32[]{:S(2)}) collective-permute-start(f16[128,768]{1,0:T(8,128)(2,1)S(1)} %get-tuple-element.30), channel_id=1, source_target_pairs={{0,1},{1,0},{2,3},{3,2},{4,5},{5,4},{6,7},{7,6},{8,9},{9,8},{10,11... | collective-permute-start | bytes 589832 | tf_op jit(solution)/shard_map/ppermute | solution.py:14
  6.0 7.6 %collective-permute-start.2 = (s32[1,128]{1,0:T(1,128)S(1)}, s32[1,128]{1,0:T(1,128)S(1)}, u32[]{:S(2)}, u32[]{:S(2)}) collective-permute-start(s32[1,128]{1,0:T(1,128)S(1)} %bitcast.17), channel_id=1, source_target_pairs={{0,4},{1,5},{2,6},{3,7},{4,0},{5,1},{6,2},{7,3},{8,12},{9,13},{10,... | collective-permute-start | bytes 1544 | tf_op jit(solution)/shard_map/ppermute | solution.py:14
  8.5 10.1 %collective-permute-start.4 = (bf16[64,768]{1,0:T(8,128)(2,1)S(1)}, bf16[64,768]{1,0:T(8,128)(2,1)S(1)}, u32[]{:S(2)}, u32[]{:S(2)}) collective-permute-start(bf16[64,768]{1,0:T(8,128)(2,1)S(1)} %divide_convert_fusion.1.refs_0_), channel_id=1, source_target_pairs={{0,16},{1,17},{2,18},{3,19},{4,20},{5,21},{6,22},{7,23},{8,24},{9,... | collective-permute-start | bytes 294920 | tf_op jit(solution)/shard_map/ppermute | solution.py:14
  11.8 7.3 %collective-permute-start.6 = (bf16[64,768]{1,0:T(8,128)(2,1)S(1)}, bf16[64,768]{1,0:T(8,128)(2,1)S(1)}, u32[]{:S(2)}, u32[]{:S(2)}) collective-permute-start(bf16[64,768]{1,0:T(8,128)(2,1)S(1)} %divide_convert_fusion.1.refs_0_), channel_id=1, source_target_pairs={{0,24},{1,25},{2,26},{3,27},{4,28},{5,29},{6,30},{7,31},{8,16},{9,... | collective-permute-start | bytes 294920 | tf_op jit(solution)/shard_map/ppermute | solution.py:14
  13.2 6.1 %collective-permute-start.8 = (bf16[64,768]{1,0:T(8,128)(2,1)S(1)}, bf16[64,768]{1,0:T(8,128)(2,1)S(1)}, u32[]{:S(2)}, u32[]{:S(2)}) collective-permute-start(bf16[64,768]{1,0:T(8,128)(2,1)S(1)} %divide_convert_fusion.1.refs_0_), channel_id=1, source_target_pairs={{0,8},{1,9},{2,10},{3,11},{4,12},{5,13},{6,14},{7,15},{8,0},{9,1},... | collective-permute-start | bytes 294920 | tf_op jit(solution)/shard_map/ppermute | solution.py:14
  13.7 6.9 %collective-permute-start.3 = (bf16[128,768]{1,0:T(8,128)(2,1)S(1)}, bf16[128,768]{1,0:T(8,128)(2,1)S(1)}, u32[]{:S(2)}, u32[]{:S(2)}) collective-permute-start(bf16[128,768]{1,0:T(8,128)(2,1)S(1)} %divide_convert_fusion.refs_1_), channel_id=1, source_target_pairs={{0,4},{1,5},{2,6},{3,7},{4,0},{5,1},{6,2},{7,3},{8,12},{9,13},{10,... | collective-permute-start | bytes 589832 | tf_op jit(solution)/shard_map/ppermute | solution.py:14
  18.6 2.0 %collective-permute-start.10 = (bf16[64,768]{1,0:T(8,128)(2,1)S(1)}, bf16[64,768]{1,0:T(8,128)(2,1)S(1)}, u32[]{:S(2)}, u32[]{:S(2)}) collective-permute-start(bf16[64,768]{1,0:T(8,128)(2,1)S(1)} %divide_convert_fusion.1.refs_0_), channel_id=1, source_target_pairs={{0,2},{1,3},{2,0},{3,1},{4,6},{5,7},{6,4},{7,5},{8,10},{9,11},{10,... | collective-permute-start | bytes 294920 | tf_op jit(solution)/shard_map/ppermute | solution.py:14
  18.6 1.8 %collective-permute-start.5 = (bf16[64,768]{1,0:T(8,128)(2,1)S(1)}, bf16[64,768]{1,0:T(8,128)(2,1)S(1)}, u32[]{:S(2)}, u32[]{:S(2)}) collective-permute-start(bf16[64,768]{1,0:T(8,128)(2,1)S(1)} %collective-permute-done.4.refs_5_), channel_id=1, source_target_pairs={{0,2},{1,3},{2,0},{3,1},{4,6},{5,7},{6,4},{7,5},{8,10},{9,11},{10,... | collective-permute-start | bytes 294920 | tf_op jit(solution)/shard_map/ppermute | solution.py:14
  19.1 1.3 %collective-permute-start.7 = (bf16[64,768]{1,0:T(8,128)(2,1)S(1)}, bf16[64,768]{1,0:T(8,128)(2,1)S(1)}, u32[]{:S(2)}, u32[]{:S(2)}) collective-permute-start(bf16[64,768]{1,0:T(8,128)(2,1)S(1)} %collective-permute-done.6.refs_7_), channel_id=1, source_target_pairs={{0,2},{1,3},{2,0},{3,1},{4,6},{5,7},{6,4},{7,5},{8,10},{9,11},{10,... | collective-permute-start | bytes 294920 | tf_op jit(solution)/shard_map/ppermute | solution.py:14
  19.2 1.4 %collective-permute-start.9 = (bf16[64,768]{1,0:T(8,128)(2,1)S(1)}, bf16[64,768]{1,0:T(8,128)(2,1)S(1)}, u32[]{:S(2)}, u32[]{:S(2)}) collective-permute-start(bf16[64,768]{1,0:T(8,128)(2,1)S(1)} %collective-permute-done.8.refs_9_), channel_id=1, source_target_pairs={{0,2},{1,3},{2,0},{3,1},{4,6},{5,7},{6,4},{7,5},{8,10},{9,11},{10,... | collective-permute-start | bytes 294920 | tf_op jit(solution)/shard_map/ppermute | solution.py:14
  21.3 1.8 %collective-permute-start.11 = (f32[2,256]{1,0:T(2,128)S(1)}, f32[2,256]{1,0:T(2,128)S(1)}, u32[]{:S(2)}, u32[]{:S(2)}) collective-permute-start(f32[2,256]{1,0:T(2,128)S(1)} %get-tuple-element.21), channel_id=1, source_target_pairs={{0,2},{1,3},{2,0},{3,1},{4,6},{5,7},{6,4},{7,5},{8,10},{9,11},{10,... | collective-permute-start | bytes 6152 | tf_op jit(solution)/shard_map/ppermute | solution.py:14
  21.7 4.2 %collective-permute-start.14 = (f32[2,128]{1,0:T(2,128)S(1)}, f32[2,128]{1,0:T(2,128)S(1)}, u32[]{:S(2)}, u32[]{:S(2)}) collective-permute-start(f32[2,128]{1,0:T(2,128)S(1)} %get-tuple-element.27), channel_id=1, source_target_pairs={{0,4},{1,5},{2,6},{3,7},{4,0},{5,1},{6,2},{7,3},{8,12},{9,13},{10,... | collective-permute-start | bytes 3080 | tf_op jit(solution)/shard_map/ppermute | solution.py:14
  23.1 4.5 %collective-permute-start.12 = (f32[2,128]{1,0:T(2,128)S(1)}, f32[2,128]{1,0:T(2,128)S(1)}, u32[]{:S(2)}, u32[]{:S(2)}) collective-permute-start(f32[2,128]{1,0:T(2,128)S(1)} %get-tuple-element.23), channel_id=1, source_target_pairs={{0,16},{1,17},{2,18},{3,19},{4,20},{5,21},{6,22},{7,23},{8,24},{9,... | collective-permute-start | bytes 3080 | tf_op jit(solution)/shard_map/ppermute | solution.py:14
  25.9 3.6 %collective-permute-start.15 = (f32[2,128]{1,0:T(2,128)S(1)}, f32[2,128]{1,0:T(2,128)S(1)}, u32[]{:S(2)}, u32[]{:S(2)}) collective-permute-start(f32[2,128]{1,0:T(2,128)S(1)} %shard_map.80.refs_2_), channel_id=1, source_target_pairs={{0,1},{1,0},{2,3},{3,2},{4,5},{5,4},{6,7},{7,6},{8,9},{9,8},{10,11... | collective-permute-start | bytes 3080 | tf_op jit(solution)/shard_map/ppermute | solution.py:14
  27.8 3.6 %collective-permute-start.13 = (f32[2,64]{1,0:T(2,128)S(1)}, f32[2,64]{1,0:T(2,128)S(1)}, u32[]{:S(2)}, u32[]{:S(2)}) collective-permute-start(f32[2,64]{1,0:T(2,128)S(1)} %get-tuple-element.25), channel_id=1, source_target_pairs={{0,8},{1,9},{2,10},{3,11},{4,12},{5,13},{6,14},{7,15},{8,0},{9,1},... | collective-permute-start | bytes 1544 | tf_op jit(solution)/shard_map/ppermute | solution.py:14

commit v5 on v4

--- a/solution.py
+++ b/solution.py
@@ -31,12 +31,15 @@
     images = [refs.pop(0) for _ in range(n_image)]
     pairs = [refs.pop(0) for _ in range(n_image)]
     texts += [refs.pop(0) for _ in places[1:]]
-    texts = [text for _, text in sorted(zip(places, texts), key=lambda pair: pair[0])]
+    half = texts[0].shape[0]
+    blocks = {}
+    for held, text in zip(places, texts):
+        blocks.update({place: text[n * half : (n + 1) * half, :] for n, place in enumerate(held)})
+    texts = [blocks[place] for place in sorted(blocks)]
     col_out, row_out = refs[:n_col], refs[n_col:]
     rows = images[0].shape[0]
-    half = texts[0].shape[0]
     image = jnp.concatenate([r[...] for r in images], axis=0)
-    text = jnp.concatenate([r[...] for r in texts], axis=0)
+    text = jnp.concatenate(texts, axis=0)
     logits = scale_ref[0:1, 0:1] * lax.dot_general(
         image, text, (((1,), (1,)), ((), ())), preferred_element_type=jnp.float32
     )
@@ -71,10 +74,10 @@
 
 def block_stats(scale, ids, images, pairs, texts, places):
     rows = images[0].shape[0]
-    count = len(texts) * texts[0].shape[0]
+    count = sum(text.shape[0] for text in texts)
     vmem = pl.BlockSpec(memory_space=pltpu.VMEM)
     operands = [scale, ids, texts[0], *images, *pairs, *texts[1:]]
-    col = pieces(count, min(2, len(texts)))
+    col = pieces(count, 2)
     row = pieces(rows * len(images), min(2, len(images)))
     out = pl.pallas_call(
         functools.partial(stats_kernel, len(images), places, len(col)),
@@ -161,18 +164,20 @@
     images = [image_emb] + [exchange(image_emb, stride) for stride in range(core, near, core)]
 
     texts[0] = text_emb
-    late, _ = lax.optimization_barrier((text_emb, texts[z_order[1]]))
-    blocks = {(0, j): texts[j] for j in range(far)}
-    for c in range(1, core):
-        blocks.update({(c, j): exchange(texts[j] if j else late, c) for j in range(far)})
-    z_names = sorted(z_order, key=lambda j: (j != far // 2, -j))
-    order = [(0, 0)] + [(c, j) for j in z_names for c in range(core)] + [(c, 0) for c in range(1, core)]
+    z_names = sorted(z_order, key=lambda j: -j)
+    shards = [(texts[0], [(0, 0)])]
+    for n, j in enumerate(z_names):
+        shards.append((texts[j], [(0, j)]))
+        held = [0, j] if n == len(z_names) - 1 else [j]
+        joint = jnp.concatenate([texts[i] for i in held]) if len(held) > 1 else texts[j]
+        shards += [(exchange(joint, c), [(c, i) for i in held]) for c in range(1, core)]
     owner = jnp.stack([dp_index ^ (near * j + c) for c in range(core) for j in range(far)])
     starts = (owner * rows + mp_index * half).astype(jnp.int32)
     ids = (starts[:, None] + jnp.arange(half, dtype=jnp.int32)[None]).reshape(1, -1)
     scale = jnp.broadcast_to(logit_scale[None], (1, rows))
     col, row = block_stats(
-        scale, ids, images, pairs, [blocks[k] for k in order], [c * far + j for c, j in order]
+        scale, ids, images, pairs, [shard for shard, _ in shards],
+        [[c * far + j for c, j in held] for _, held in shards],
     )
 
     col_steps = [1] * (core > 1) + [near << k for k in reversed(range(far.bit_length() - 1))]

time: 32 us -> 32 us (level)
  starting transfers between devices: 19.2 us -> 17.4 us
  waiting for transfers between devices: 6.74 us -> 8.46 us
    ppermute x16 -> x15, starting transfers between devices: 19.2 us -> 17.4 us  [exchange(): return lax.ppermute(value, ('dp', 'mp'), pairs)]
    ppermute x16 -> x15, waiting for transfers between devices: 6.74 us -> 8.46 us  [exchange(): return lax.ppermute(value, ('dp', 'mp'), pairs)]
  transfers between devices with their start and end apart: 16 -> 15, of which waited for: 7 -> 8; matrix products, arithmetic and copies ran while one was open for 4% -> 4% of each run, Pallas kernels for 0% -> 0%
where the time goes in v5:
time: 32 us; the launch traced here: 31.8 us
  starting transfers between devices  17.4 us (54%)
  waiting for transfers between devices  8.46 us (26%)
  matrix products  1.88 us (6%)
  between operations  1.42 us (4%)
  Pallas kernels  1.37 us (4%)
  local copies, waits for them, and re-layouts  0.75 us (2%)
  other arithmetic  0.57 us (2%)
    ppermute x15, starting transfers between devices, exchange(): return lax.ppermute(value, ('dp', 'mp'), pairs)  17.4 us
    ppermute x15, waiting for transfers between devices, exchange(): return lax.ppermute(value, ('dp', 'mp'), pairs)  8.46 us
    dot_general x2, matrix products, text_rows(): return jnp.dot(mine, text_proj, preferred_element_type=jnp.float32)  1.61 us
    pallas_call x1, Pallas kernels, block_stats(): pl.pallas_call(functools.partial(stats_kernel, len(images), places, len(c...  0.73 us
    pallas_call x4, Pallas kernels, join(): pl.pallas_call(functools.partial(join_kernel, [len(g) for g in groups], s...  0.64 us
  transfers between devices with their start and end apart: 15, of which 8 were waited for; matrix products, arithmetic and copies ran while one was open for 4% of the time, Pallas kernels for 0%

profile of v5, /device:TPU:0, one launch (start us, length us, event | category | flops | bytes accessed | tf_op | source)
XLA Modules:
  0.0 31.8 jit_solution(7925494144706273954)
XLA Ops:
  0.6 0.0 copy-start
  0.7 0.0 copy-start.3
  0.7 1.4 %convolution_convert_fusion = f16[64,768]{1,0:T(8,128)(2,1)S(1)} fusion(bf16[384,768]{1,0:T(8,128)(2,1)} %param.9, bf16[128,384]{1,0:T(8,128)(2,1)} %param.8, s32[]{:T(128)S(6)} %select_n.7), kind=kOutput, calls=%fused_computation | convolution fusion | flops 37797888 | bytes 737284 | tf_op jit(solution)/shard_map/dot_general | solution.py:147
  2.1 0.0 copy-start.2
  2.1 0.0 copy-start.4
  2.1 3.0 %collective-permute-start = (f16[64,768]{1,0:T(8,128)(2,1)S(1)}, f16[64,768]{1,0:T(8,128)(2,1)S(1)}, u32[]{:S(2)}, u32[]{:S(2)}) collective-permute-start(f16[64,768]{1,0:T(8,128)(2,1)S(1)} %convolution_convert_fusion), channel_id=1, source_target_pairs={{0,1},{1,0},{2,3},{3,2},{4,5},{5,4},{6,7},{7,6},{8,9},{9,8},{10,11... | collective-permute-start | bytes 294920 | tf_op jit(solution)/shard_map/ppermute | solution.py:14
  5.1 0.0 copy-done
  5.1 0.0 copy-done.3
  5.1 0.3 fusion.5
  5.4 0.0 copy-start.1
  5.4 0.1 collective-permute-start.1
  5.5 0.6 %copy-done.1 = s32[128]{0:T(128)S(1)} copy-done((s32[128]{0:T(128)S(1)}, s32[128]{0:T(128)}, u32[]{:S(2)}) %copy-start.1) | copy-done | bytes 536
  6.0 1.5 %collective-permute-start.2 = (s32[1,128]{1,0:T(1,128)S(1)}, s32[1,128]{1,0:T(1,128)S(1)}, u32[]{:S(2)}, u32[]{:S(2)}) collective-permute-start(s32[1,128]{1,0:T(1,128)S(1)} %bitcast.17), channel_id=1, source_target_pairs={{0,4},{1,5},{2,6},{3,7},{4,0},{5,1},{6,2},{7,3},{8,12},{9,13},{10,... | collective-permute-start | bytes 1544 | tf_op jit(solution)/shard_map/ppermute | solution.py:14
  7.6 0.0 copy-done.2
  7.6 0.0 copy-done.4
  7.6 0.2 fusion.1
  7.8 0.1 stack.35
  7.9 0.4 %collective-permute-done = f16[64,768]{1,0:T(8,128)(2,1)S(1)} collective-permute-done((f16[64,768]{1,0:T(8,128)(2,1)S(1)}, f16[64,768]{1,0:T(8,128)(2,1)S(1)}, u32[]{:S(2)}, u32[]{:S(2)}) %collective-permute-start) | collective-permute-done | bytes 98336 | tf_op jit(solution)/shard_map/ppermute | solution.py:14
  8.3 0.1 multiply_reduce_fusion.1
  8.4 0.1 divide_convert_fusion.1.refs_0_
  8.5 4.3 %collective-permute-start.4 = (bf16[64,768]{1,0:T(8,128)(2,1)S(1)}, bf16[64,768]{1,0:T(8,128)(2,1)S(1)}, u32[]{:S(2)}, u32[]{:S(2)}) collective-permute-start(bf16[64,768]{1,0:T(8,128)(2,1)S(1)} %divide_convert_fusion.1.refs_0_), channel_id=1, source_target_pairs={{0,24},{1,25},{2,26},{3,27},{4,28},{5,29},{6,30},{7,31},{8,16},{9,... | collective-permute-start | bytes 294920 | tf_op jit(solution)/shard_map/ppermute | solution.py:14
  12.8 0.0 collective-permute-start.6
  12.8 0.6 %collective-permute-start.8 = (bf16[64,768]{1,0:T(8,128)(2,1)S(1)}, bf16[64,768]{1,0:T(8,128)(2,1)S(1)}, u32[]{:S(2)}, u32[]{:S(2)}) collective-permute-start(bf16[64,768]{1,0:T(8,128)(2,1)S(1)} %divide_convert_fusion.1.refs_0_), channel_id=1, source_target_pairs={{0,8},{1,9},{2,10},{3,11},{4,12},{5,13},{6,14},{7,15},{8,0},{9,1},... | collective-permute-start | bytes 294920 | tf_op jit(solution)/shard_map/ppermute | solution.py:14
  13.5 0.0 collective-permute-done.1
  13.5 0.1 multiply_reduce_fusion
  13.6 0.1 divide_convert_fusion.refs_1_
  13.7 0.0 collective-permute-done.2.refs_4_
  13.7 1.7 %collective-permute-start.3 = (bf16[128,768]{1,0:T(8,128)(2,1)S(1)}, bf16[128,768]{1,0:T(8,128)(2,1)S(1)}, u32[]{:S(2)}, u32[]{:S(2)}) collective-permute-start(bf16[128,768]{1,0:T(8,128)(2,1)S(1)} %divide_convert_fusion.refs_1_), channel_id=1, source_target_pairs={{0,4},{1,5},{2,6},{3,7},{4,0},{5,1},{6,2},{7,3},{8,12},{9,13},{10,... | collective-permute-start | bytes 589832 | tf_op jit(solution)/shard_map/ppermute | solution.py:14
  15.5 2.1 %collective-permute-done.8.refs_9_ = bf16[64,768]{1,0:T(8,128)(2,1)S(1)} collective-permute-done((bf16[64,768]{1,0:T(8,128)(2,1)S(1)}, bf16[64,768]{1,0:T(8,128)(2,1)S(1)}, u32[]{:S(2)}, u32[]{:S(2)}) %collective-permute-start.8) | collective-permute-done | bytes 98336 | tf_op jit(solution)/shard_map/ppermute | solution.py:14
  17.6 0.1 collective-permute-start.9
  17.7 0.0 collective-permute-done.4.refs_5_
  17.7 0.5 %collective-permute-start.5 = (bf16[64,768]{1,0:T(8,128)(2,1)S(1)}, bf16[64,768]{1,0:T(8,128)(2,1)S(1)}, u32[]{:S(2)}, u32[]{:S(2)}) collective-permute-start(bf16[64,768]{1,0:T(8,128)(2,1)S(1)} %collective-permute-done.4.refs_5_), channel_id=1, source_target_pairs={{0,2},{1,3},{2,0},{3,1},{4,6},{5,7},{6,4},{7,5},{8,10},{9,11},{10,... | collective-permute-start | bytes 294920 | tf_op jit(solution)/shard_map/ppermute | solution.py:14
  18.2 1.4 %collective-permute-done.6.refs_7_ = bf16[64,768]{1,0:T(8,128)(2,1)S(1)} collective-permute-done((bf16[64,768]{1,0:T(8,128)(2,1)S(1)}, bf16[64,768]{1,0:T(8,128)(2,1)S(1)}, u32[]{:S(2)}, u32[]{:S(2)}) %collective-permute-start.6) | collective-permute-done | bytes 98336 | tf_op jit(solution)/shard_map/ppermute | solution.py:14
  19.6 0.0 collective-permute-start.7
  19.6 0.1 iota_add_fusion
  20.3 0.1 add.72.id_ref
  20.4 0.0 collective-permute-done.5.refs_6_
  20.4 0.5 %collective-permute-done.7.refs_8_ = bf16[64,768]{1,0:T(8,128)(2,1)S(1)} collective-permute-done((bf16[64,768]{1,0:T(8,128)(2,1)S(1)}, bf16[64,768]{1,0:T(8,128)(2,1)S(1)}, u32[]{:S(2)}, u32[]{:S(2)}) %collective-permute-start.7) | collective-permute-done | bytes 98336 | tf_op jit(solution)/shard_map/ppermute | solution.py:14
  20.9 0.0 collective-permute-done.3.refs_2_
  20.9 0.0 collective-permute-done.9.refs_10_
  20.9 0.7 %shard_map.77 = (f32[2,256]{1,0:T(2,128)S(1)}, f32[2,256]{1,0:T(2,128)S(1)}, f32[2,128]{1,0:T(2,128)S(1)}, f32[2,128]{1,0:T(2,128)S(1)}) custom-call(f32[1,128]{1,0:T(1,128)S(1)} %broadcast_in_dim.7.scale_ref, s32[1,512]{1,0:T(1,128)S(1)} %add.72.id_ref, bf16[64,768]{1,0:T(8,128)(2,1)S(1)} %divide_convert_fusion.1.refs_0_, ...), custom_call_target="tpu_custom_call" | custom-call | flops 201326592 | bytes 1183232 | tf_op jit(solution)/shard_map/pallas_call | solution.py:82
  21.6 0.2 collective-permute-start.10
  21.8 1.3 %collective-permute-start.13 = (f32[2,128]{1,0:T(2,128)S(1)}, f32[2,128]{1,0:T(2,128)S(1)}, u32[]{:S(2)}, u32[]{:S(2)}) collective-permute-start(f32[2,128]{1,0:T(2,128)S(1)} %get-tuple-element.25), channel_id=1, source_target_pairs={{0,4},{1,5},{2,6},{3,7},{4,0},{5,1},{6,2},{7,3},{8,12},{9,13},{10,... | collective-permute-start | bytes 3080 | tf_op jit(solution)/shard_map/ppermute | solution.py:14
  23.1 0.0 collective-permute-done.10.refs_1_
  23.1 1.7 %collective-permute-start.11 = (f32[2,128]{1,0:T(2,128)S(1)}, f32[2,128]{1,0:T(2,128)S(1)}, u32[]{:S(2)}, u32[]{:S(2)}) collective-permute-start(f32[2,128]{1,0:T(2,128)S(1)} %get-tuple-element.21), channel_id=1, source_target_pairs={{0,16},{1,17},{2,18},{3,19},{4,20},{5,21},{6,22},{7,23},{8,24},{9,... | collective-permute-start | bytes 3080 | tf_op jit(solution)/shard_map/ppermute | solution.py:14
  24.8 0.6 %collective-permute-done.13.refs_1_ = f32[2,128]{1,0:T(2,128)S(1)} collective-permute-done((f32[2,128]{1,0:T(2,128)S(1)}, f32[2,128]{1,0:T(2,128)S(1)}, u32[]{:S(2)}, u32[]{:S(2)}) %collective-permute-start.13) | collective-permute-done | bytes 1056 | tf_op jit(solution)/shard_map/ppermute | solution.py:14
  25.4 1.3 %collective-permute-start.14 = (f32[2,128]{1,0:T(2,128)S(1)}, f32[2,128]{1,0:T(2,128)S(1)}, u32[]{:S(2)}, u32[]{:S(2)}) collective-permute-start(f32[2,128]{1,0:T(2,128)S(1)} %shard_map.80.refs_2_), channel_id=1, source_target_pairs={{0,1},{1,0},{2,3},{3,2},{4,5},{5,4},{6,7},{7,6},{8,9},{9,8},{10,11... | collective-permute-start | bytes 3080 | tf_op jit(solution)/shard_map/ppermute | solution.py:14
  26.7 0.9 %collective-permute-done.11.refs_1_ = f32[2,128]{1,0:T(2,128)S(1)} collective-permute-done((f32[2,128]{1,0:T(2,128)S(1)}, f32[2,128]{1,0:T(2,128)S(1)}, u32[]{:S(2)}, u32[]{:S(2)}) %collective-permute-start.11) | collective-permute-done | bytes 1056 | tf_op jit(solution)/shard_map/ppermute | solution.py:14
  27.6 0.1 shard_map.79
  27.7 1.1 %collective-permute-start.12 = (f32[2,64]{1,0:T(2,128)S(1)}, f32[2,64]{1,0:T(2,128)S(1)}, u32[]{:S(2)}, u32[]{:S(2)}) collective-permute-start(f32[2,64]{1,0:T(2,128)S(1)} %get-tuple-element.23), channel_id=1, source_target_pairs={{0,8},{1,9},{2,10},{3,11},{4,12},{5,13},{6,14},{7,15},{8,0},{9,1},... | collective-permute-start | bytes 1544 | tf_op jit(solution)/shard_map/ppermute | solution.py:14
  28.8 0.2 collective-permute-done.14.refs_3_
  29.1 2.2 %collective-permute-done.12.refs_1_ = f32[2,64]{1,0:T(2,128)S(1)} collective-permute-done((f32[2,64]{1,0:T(2,128)S(1)}, f32[2,64]{1,0:T(2,128)S(1)}, u32[]{:S(2)}, u32[]{:S(2)}) %collective-permute-start.12) | collective-permute-done | bytes 544 | tf_op jit(solution)/shard_map/ppermute | solution.py:14
  31.3 0.5 %shard_map.81 = (f32[1,64]{1,0:T(1,128)}, f32[1,128]{1,0:T(1,128)}) custom-call(f32[2,64]{1,0:T(2,128)S(1)} %get-tuple-element.22.refs_0_, f32[2,64]{1,0:T(2,128)S(1)} %collective-permute-done.12.refs_1_, f32[2,128]{1,0:T(2,128)S(1)} %shard_map.80.refs_2_, f32[2,128]{1,0:T(2,128)S(1)} %collective-permute-done.14.refs_3_), custom_call_target="tpu_custom_call" | custom-call | tf_op jit(solution)/shard_map/pallas_call | solution.py:122
  (7 shorter events, 0.1 us)
Async XLA Ops:
  0.6 4.5 %copy-start = (bf16[512,768]{1,0:T(8,128)(2,1)S(1)}, bf16[512,768]{1,0:T(8,128)(2,1)}, u32[]{:S(2)}) copy-start(bf16[512,768]{1,0:T(8,128)(2,1)} %param.7) | copy-start | bytes 2359300
  0.7 4.4 %copy-start.3 = (bf16[128,512]{1,0:T(8,128)(2,1)S(1)}, bf16[128,512]{1,0:T(8,128)(2,1)}, u32[]{:S(2)}) copy-start(bf16[128,512]{1,0:T(8,128)(2,1)} %param.6) | copy-start | bytes 393220
  2.1 5.5 %copy-start.2 = (bf16[384,768]{1,0:T(8,128)(2,1)S(1)}, bf16[384,768]{1,0:T(8,128)(2,1)}, u32[]{:S(2)}) copy-start(bf16[384,768]{1,0:T(8,128)(2,1)} %param.9) | copy-start | bytes 1769476
  2.1 5.5 %copy-start.4 = (bf16[128,384]{1,0:T(8,128)(2,1)S(1)}, bf16[128,384]{1,0:T(8,128)(2,1)}, u32[]{:S(2)}) copy-start(bf16[128,384]{1,0:T(8,128)(2,1)} %param.8) | copy-start | bytes 294916
  2.1 6.2 %collective-permute-start = (f16[64,768]{1,0:T(8,128)(2,1)S(1)}, f16[64,768]{1,0:T(8,128)(2,1)S(1)}, u32[]{:S(2)}, u32[]{:S(2)}) collective-permute-start(f16[64,768]{1,0:T(8,128)(2,1)S(1)} %convolution_convert_fusion), channel_id=1, source_target_pairs={{0,1},{1,0},{2,3},{3,2},{4,5},{5,4},{6,7},{7,6},{8,9},{9,8},{10,11... | collective-permute-start | bytes 294920 | tf_op jit(solution)/shard_map/ppermute | solution.py:14
  5.4 0.7 %copy-start.1 = (s32[128]{0:T(128)S(1)}, s32[128]{0:T(128)}, u32[]{:S(2)}) copy-start(s32[128]{0:T(128)} %param.10) | copy-start | bytes 1540
  5.4 8.1 %collective-permute-start.1 = (f16[128,768]{1,0:T(8,128)(2,1)S(1)}, f16[128,768]{1,0:T(8,128)(2,1)S(1)}, u32[]{:S(2)}, u32[]{:S(2)}) collective-permute-start(f16[128,768]{1,0:T(8,128)(2,1)S(1)} %get-tuple-element.28), channel_id=1, source_target_pairs={{0,1},{1,0},{2,3},{3,2},{4,5},{5,4},{6,7},{7,6},{8,9},{9,8},{10,11... | collective-permute-start | bytes 589832 | tf_op jit(solution)/shard_map/ppermute | solution.py:14
  6.0 7.7 %collective-permute-start.2 = (s32[1,128]{1,0:T(1,128)S(1)}, s32[1,128]{1,0:T(1,128)S(1)}, u32[]{:S(2)}, u32[]{:S(2)}) collective-permute-start(s32[1,128]{1,0:T(1,128)S(1)} %bitcast.17), channel_id=1, source_target_pairs={{0,4},{1,5},{2,6},{3,7},{4,0},{5,1},{6,2},{7,3},{8,12},{9,13},{10,... | collective-permute-start | bytes 1544 | tf_op jit(solution)/shard_map/ppermute | solution.py:14
  8.5 9.2 %collective-permute-start.4 = (bf16[64,768]{1,0:T(8,128)(2,1)S(1)}, bf16[64,768]{1,0:T(8,128)(2,1)S(1)}, u32[]{:S(2)}, u32[]{:S(2)}) collective-permute-start(bf16[64,768]{1,0:T(8,128)(2,1)S(1)} %divide_convert_fusion.1.refs_0_), channel_id=1, source_target_pairs={{0,24},{1,25},{2,26},{3,27},{4,28},{5,29},{6,30},{7,31},{8,16},{9,... | collective-permute-start | bytes 294920 | tf_op jit(solution)/shard_map/ppermute | solution.py:14
  12.8 6.8 %collective-permute-start.6 = (bf16[64,768]{1,0:T(8,128)(2,1)S(1)}, bf16[64,768]{1,0:T(8,128)(2,1)S(1)}, u32[]{:S(2)}, u32[]{:S(2)}) collective-permute-start(bf16[64,768]{1,0:T(8,128)(2,1)S(1)} %divide_convert_fusion.1.refs_0_), channel_id=1, source_target_pairs={{0,16},{1,17},{2,18},{3,19},{4,20},{5,21},{6,22},{7,23},{8,24},{9,... | collective-permute-start | bytes 294920 | tf_op jit(solution)/shard_map/ppermute | solution.py:14
  12.8 4.8 %collective-permute-start.8 = (bf16[64,768]{1,0:T(8,128)(2,1)S(1)}, bf16[64,768]{1,0:T(8,128)(2,1)S(1)}, u32[]{:S(2)}, u32[]{:S(2)}) collective-permute-start(bf16[64,768]{1,0:T(8,128)(2,1)S(1)} %divide_convert_fusion.1.refs_0_), channel_id=1, source_target_pairs={{0,8},{1,9},{2,10},{3,11},{4,12},{5,13},{6,14},{7,15},{8,0},{9,1},... | collective-permute-start | bytes 294920 | tf_op jit(solution)/shard_map/ppermute | solution.py:14
  13.7 7.2 %collective-permute-start.3 = (bf16[128,768]{1,0:T(8,128)(2,1)S(1)}, bf16[128,768]{1,0:T(8,128)(2,1)S(1)}, u32[]{:S(2)}, u32[]{:S(2)}) collective-permute-start(bf16[128,768]{1,0:T(8,128)(2,1)S(1)} %divide_convert_fusion.refs_1_), channel_id=1, source_target_pairs={{0,4},{1,5},{2,6},{3,7},{4,0},{5,1},{6,2},{7,3},{8,12},{9,13},{10,... | collective-permute-start | bytes 589832 | tf_op jit(solution)/shard_map/ppermute | solution.py:14
  17.6 3.3 %collective-permute-start.9 = (bf16[128,768]{1,0:T(8,128)(2,1)S(1)}, bf16[128,768]{1,0:T(8,128)(2,1)S(1)}, u32[]{:S(2)}, u32[]{:S(2)}) collective-permute-start(bf16[128,768]{1,0:T(8,128)(2,1)S(1)} %pad_maximum_fusion), channel_id=1, source_target_pairs={{0,2},{1,3},{2,0},{3,1},{4,6},{5,7},{6,4},{7,5},{8,10},{9,11},{10,... | collective-permute-start | bytes 589832 | tf_op jit(solution)/shard_map/ppermute | solution.py:14
  17.7 2.7 %collective-permute-start.5 = (bf16[64,768]{1,0:T(8,128)(2,1)S(1)}, bf16[64,768]{1,0:T(8,128)(2,1)S(1)}, u32[]{:S(2)}, u32[]{:S(2)}) collective-permute-start(bf16[64,768]{1,0:T(8,128)(2,1)S(1)} %collective-permute-done.4.refs_5_), channel_id=1, source_target_pairs={{0,2},{1,3},{2,0},{3,1},{4,6},{5,7},{6,4},{7,5},{8,10},{9,11},{10,... | collective-permute-start | bytes 294920 | tf_op jit(solution)/shard_map/ppermute | solution.py:14
  19.6 1.3 %collective-permute-start.7 = (bf16[64,768]{1,0:T(8,128)(2,1)S(1)}, bf16[64,768]{1,0:T(8,128)(2,1)S(1)}, u32[]{:S(2)}, u32[]{:S(2)}) collective-permute-start(bf16[64,768]{1,0:T(8,128)(2,1)S(1)} %collective-permute-done.6.refs_7_), channel_id=1, source_target_pairs={{0,2},{1,3},{2,0},{3,1},{4,6},{5,7},{6,4},{7,5},{8,10},{9,11},{10,... | collective-permute-start | bytes 294920 | tf_op jit(solution)/shard_map/ppermute | solution.py:14
  21.6 1.5 %collective-permute-start.10 = (f32[2,256]{1,0:T(2,128)S(1)}, f32[2,256]{1,0:T(2,128)S(1)}, u32[]{:S(2)}, u32[]{:S(2)}) collective-permute-start(f32[2,256]{1,0:T(2,128)S(1)} %get-tuple-element.19), channel_id=1, source_target_pairs={{0,2},{1,3},{2,0},{3,1},{4,6},{5,7},{6,4},{7,5},{8,10},{9,11},{10,... | collective-permute-start | bytes 6152 | tf_op jit(solution)/shard_map/ppermute | solution.py:14
  21.8 3.6 %collective-permute-start.13 = (f32[2,128]{1,0:T(2,128)S(1)}, f32[2,128]{1,0:T(2,128)S(1)}, u32[]{:S(2)}, u32[]{:S(2)}) collective-permute-start(f32[2,128]{1,0:T(2,128)S(1)} %get-tuple-element.25), channel_id=1, source_target_pairs={{0,4},{1,5},{2,6},{3,7},{4,0},{5,1},{6,2},{7,3},{8,12},{9,13},{10,... | collective-permute-start | bytes 3080 | tf_op jit(solution)/shard_map/ppermute | solution.py:14
  23.1 4.5 %collective-permute-start.11 = (f32[2,128]{1,0:T(2,128)S(1)}, f32[2,128]{1,0:T(2,128)S(1)}, u32[]{:S(2)}, u32[]{:S(2)}) collective-permute-start(f32[2,128]{1,0:T(2,128)S(1)} %get-tuple-element.21), channel_id=1, source_target_pairs={{0,16},{1,17},{2,18},{3,19},{4,20},{5,21},{6,22},{7,23},{8,24},{9,... | collective-permute-start | bytes 3080 | tf_op jit(solution)/shard_map/ppermute | solution.py:14
  25.4 3.6 %collective-permute-start.14 = (f32[2,128]{1,0:T(2,128)S(1)}, f32[2,128]{1,0:T(2,128)S(1)}, u32[]{:S(2)}, u32[]{:S(2)}) collective-permute-start(f32[2,128]{1,0:T(2,128)S(1)} %shard_map.80.refs_2_), channel_id=1, source_target_pairs={{0,1},{1,0},{2,3},{3,2},{4,5},{5,4},{6,7},{7,6},{8,9},{9,8},{10,11... | collective-permute-start | bytes 3080 | tf_op jit(solution)/shard_map/ppermute | solution.py:14
  27.7 3.6 %collective-permute-start.12 = (f32[2,64]{1,0:T(2,128)S(1)}, f32[2,64]{1,0:T(2,128)S(1)}, u32[]{:S(2)}, u32[]{:S(2)}) collective-permute-start(f32[2,64]{1,0:T(2,128)S(1)} %get-tuple-element.23), channel_id=1, source_target_pairs={{0,8},{1,9},{2,10},{3,11},{4,12},{5,13},{6,14},{7,15},{8,0},{9,1},... | collective-permute-start | bytes 1544 | tf_op jit(solution)/shard_map/ppermute | solution.py:14

commit v6 on v5

--- a/solution.py
+++ b/solution.py
@@ -17,12 +17,6 @@
 def normalize(raw):
     norm_sq = jnp.sum(raw * raw, axis=1, keepdims=True)
     return (raw / jnp.sqrt(norm_sq + 1e-06)).astype(jnp.bfloat16)
-
-
-def join(stats):
-    top = functools.reduce(jnp.maximum, [s[0] for s in stats])
-    total = sum(jnp.exp(s[0] - top) for s in stats)
-    return jnp.stack([top + jnp.log(total), sum(s[1] for s in stats)])
 
 
 def stats_kernel(n_image, places, n_col, scale_ref, id_ref, *refs):
@@ -140,7 +134,7 @@
     rows = image_feat.shape[0]
     half = rows // mp
     width = text_proj.shape[1]
-    z_order = list(reversed(range(1, far)))
+    far_order = list(reversed(range(1, far)))
 
     def text_rows(owner):
         mine = lax.dynamic_slice_in_dim(text_feat, owner * half, half, 0)
@@ -156,7 +150,7 @@
         image_raw = image_raw + exchange(sent, 0, step)
     text_emb = normalize(sum(got, lax.optimization_barrier(text_rows(mp_index))))
 
-    texts = {j: exchange(text_emb, near * j) for j in z_order}
+    texts = {j: exchange(text_emb, near * j) for j in far_order}
 
     pairs = [pair_index[None]]
     pairs += [exchange(pairs[0], stride) for stride in range(core, near, core)]
@@ -164,11 +158,10 @@
     images = [image_emb] + [exchange(image_emb, stride) for stride in range(core, near, core)]
 
     texts[0] = text_emb
-    z_names = sorted(z_order, key=lambda j: -j)
     shards = [(texts[0], [(0, 0)])]
-    for n, j in enumerate(z_names):
+    for n, j in enumerate(far_order):
         shards.append((texts[j], [(0, j)]))
-        held = [0, j] if n == len(z_names) - 1 else [j]
+        held = [0, j] if n == far - 2 else [j]
         joint = jnp.concatenate([texts[i] for i in held]) if len(held) > 1 else texts[j]
         shards += [(exchange(joint, c), [(c, i) for i in held]) for c in range(1, core)]
     owner = jnp.stack([dp_index ^ (near * j + c) for c in range(core) for j in range(far)])

time: 32 us -> 32 us (level)
  no operation moved by 1% of the time
where the time goes in v6:
time: 32 us; the launch traced here: 31.8 us
  starting transfers between devices  17.4 us (54%)
  waiting for transfers between devices  8.46 us (26%)
  matrix products  1.88 us (6%)
  between operations  1.42 us (4%)
  Pallas kernels  1.37 us (4%)
  local copies, waits for them, and re-layouts  0.75 us (2%)
  other arithmetic  0.57 us (2%)
    ppermute x15, starting transfers between devices, exchange(): return lax.ppermute(value, ('dp', 'mp'), pairs)  17.4 us
    ppermute x15, waiting for transfers between devices, exchange(): return lax.ppermute(value, ('dp', 'mp'), pairs)  8.46 us
    dot_general x2, matrix products, text_rows(): return jnp.dot(mine, text_proj, preferred_element_type=jnp.float32)  1.61 us
    pallas_call x1, Pallas kernels, block_stats(): pl.pallas_call(functools.partial(stats_kernel, len(images), places, len(c...  0.73 us
    pallas_call x4, Pallas kernels, join(): pl.pallas_call(functools.partial(join_kernel, [len(g) for g in groups], s...  0.64 us
  transfers between devices with their start and end apart: 15, of which 8 were waited for; matrix products, arithmetic and copies ran while one was open for 4% of the time, Pallas kernels for 0%

profile of v6, /device:TPU:0, one launch (start us, length us, event | category | flops | bytes accessed | tf_op | source)
XLA Modules:
  0.0 31.8 jit_solution(7925494144706273954)
XLA Ops:
  0.6 0.0 copy-start
  0.7 0.0 copy-start.3
  0.7 1.4 %convolution_convert_fusion = f16[64,768]{1,0:T(8,128)(2,1)S(1)} fusion(bf16[384,768]{1,0:T(8,128)(2,1)} %param.9, bf16[128,384]{1,0:T(8,128)(2,1)} %param.8, s32[]{:T(128)S(6)} %select_n.7), kind=kOutput, calls=%fused_computation | convolution fusion | flops 37797888 | bytes 737284 | tf_op jit(solution)/shard_map/dot_general | solution.py:141
  2.1 0.0 copy-start.2
  2.1 0.0 copy-start.4
  2.1 3.0 %collective-permute-start = (f16[64,768]{1,0:T(8,128)(2,1)S(1)}, f16[64,768]{1,0:T(8,128)(2,1)S(1)}, u32[]{:S(2)}, u32[]{:S(2)}) collective-permute-start(f16[64,768]{1,0:T(8,128)(2,1)S(1)} %convolution_convert_fusion), channel_id=1, source_target_pairs={{0,1},{1,0},{2,3},{3,2},{4,5},{5,4},{6,7},{7,6},{8,9},{9,8},{10,11... | collective-permute-start | bytes 294920 | tf_op jit(solution)/shard_map/ppermute | solution.py:14
  5.1 0.0 copy-done
  5.1 0.0 copy-done.3
  5.1 0.3 fusion.5
  5.4 0.0 copy-start.1
  5.4 0.1 collective-permute-start.1
  5.5 0.6 %copy-done.1 = s32[128]{0:T(128)S(1)} copy-done((s32[128]{0:T(128)S(1)}, s32[128]{0:T(128)}, u32[]{:S(2)}) %copy-start.1) | copy-done | bytes 536
  6.0 1.5 %collective-permute-start.2 = (s32[1,128]{1,0:T(1,128)S(1)}, s32[1,128]{1,0:T(1,128)S(1)}, u32[]{:S(2)}, u32[]{:S(2)}) collective-permute-start(s32[1,128]{1,0:T(1,128)S(1)} %bitcast.17), channel_id=1, source_target_pairs={{0,4},{1,5},{2,6},{3,7},{4,0},{5,1},{6,2},{7,3},{8,12},{9,13},{10,... | collective-permute-start | bytes 1544 | tf_op jit(solution)/shard_map/ppermute | solution.py:14
  7.6 0.0 copy-done.2
  7.6 0.0 copy-done.4
  7.6 0.2 fusion.1
  7.8 0.1 stack.35
  7.9 0.4 %collective-permute-done = f16[64,768]{1,0:T(8,128)(2,1)S(1)} collective-permute-done((f16[64,768]{1,0:T(8,128)(2,1)S(1)}, f16[64,768]{1,0:T(8,128)(2,1)S(1)}, u32[]{:S(2)}, u32[]{:S(2)}) %collective-permute-start) | collective-permute-done | bytes 98336 | tf_op jit(solution)/shard_map/ppermute | solution.py:14
  8.3 0.1 multiply_reduce_fusion.1
  8.4 0.1 divide_convert_fusion.1.refs_0_
  8.5 4.3 %collective-permute-start.4 = (bf16[64,768]{1,0:T(8,128)(2,1)S(1)}, bf16[64,768]{1,0:T(8,128)(2,1)S(1)}, u32[]{:S(2)}, u32[]{:S(2)}) collective-permute-start(bf16[64,768]{1,0:T(8,128)(2,1)S(1)} %divide_convert_fusion.1.refs_0_), channel_id=1, source_target_pairs={{0,24},{1,25},{2,26},{3,27},{4,28},{5,29},{6,30},{7,31},{8,16},{9,... | collective-permute-start | bytes 294920 | tf_op jit(solution)/shard_map/ppermute | solution.py:14
  12.8 0.0 collective-permute-start.6
  12.8 0.6 %collective-permute-start.8 = (bf16[64,768]{1,0:T(8,128)(2,1)S(1)}, bf16[64,768]{1,0:T(8,128)(2,1)S(1)}, u32[]{:S(2)}, u32[]{:S(2)}) collective-permute-start(bf16[64,768]{1,0:T(8,128)(2,1)S(1)} %divide_convert_fusion.1.refs_0_), channel_id=1, source_target_pairs={{0,8},{1,9},{2,10},{3,11},{4,12},{5,13},{6,14},{7,15},{8,0},{9,1},... | collective-permute-start | bytes 294920 | tf_op jit(solution)/shard_map/ppermute | solution.py:14
  13.5 0.0 collective-permute-done.1
  13.5 0.1 multiply_reduce_fusion
  13.6 0.1 divide_convert_fusion.refs_1_
  13.7 0.0 collective-permute-done.2.refs_4_
  13.7 1.7 %collective-permute-start.3 = (bf16[128,768]{1,0:T(8,128)(2,1)S(1)}, bf16[128,768]{1,0:T(8,128)(2,1)S(1)}, u32[]{:S(2)}, u32[]{:S(2)}) collective-permute-start(bf16[128,768]{1,0:T(8,128)(2,1)S(1)} %divide_convert_fusion.refs_1_), channel_id=1, source_target_pairs={{0,4},{1,5},{2,6},{3,7},{4,0},{5,1},{6,2},{7,3},{8,12},{9,13},{10,... | collective-permute-start | bytes 589832 | tf_op jit(solution)/shard_map/ppermute | solution.py:14
  15.5 2.1 %collective-permute-done.8.refs_9_ = bf16[64,768]{1,0:T(8,128)(2,1)S(1)} collective-permute-done((bf16[64,768]{1,0:T(8,128)(2,1)S(1)}, bf16[64,768]{1,0:T(8,128)(2,1)S(1)}, u32[]{:S(2)}, u32[]{:S(2)}) %collective-permute-start.8) | collective-permute-done | bytes 98336 | tf_op jit(solution)/shard_map/ppermute | solution.py:14
  17.6 0.1 collective-permute-start.9
  17.7 0.0 collective-permute-done.4.refs_5_
  17.7 0.5 %collective-permute-start.5 = (bf16[64,768]{1,0:T(8,128)(2,1)S(1)}, bf16[64,768]{1,0:T(8,128)(2,1)S(1)}, u32[]{:S(2)}, u32[]{:S(2)}) collective-permute-start(bf16[64,768]{1,0:T(8,128)(2,1)S(1)} %collective-permute-done.4.refs_5_), channel_id=1, source_target_pairs={{0,2},{1,3},{2,0},{3,1},{4,6},{5,7},{6,4},{7,5},{8,10},{9,11},{10,... | collective-permute-start | bytes 294920 | tf_op jit(solution)/shard_map/ppermute | solution.py:14
  18.2 1.4 %collective-permute-done.6.refs_7_ = bf16[64,768]{1,0:T(8,128)(2,1)S(1)} collective-permute-done((bf16[64,768]{1,0:T(8,128)(2,1)S(1)}, bf16[64,768]{1,0:T(8,128)(2,1)S(1)}, u32[]{:S(2)}, u32[]{:S(2)}) %collective-permute-start.6) | collective-permute-done | bytes 98336 | tf_op jit(solution)/shard_map/ppermute | solution.py:14
  19.6 0.0 collective-permute-start.7
  19.6 0.1 iota_add_fusion
  20.3 0.1 add.72.id_ref
  20.4 0.0 collective-permute-done.5.refs_6_
  20.4 0.5 %collective-permute-done.7.refs_8_ = bf16[64,768]{1,0:T(8,128)(2,1)S(1)} collective-permute-done((bf16[64,768]{1,0:T(8,128)(2,1)S(1)}, bf16[64,768]{1,0:T(8,128)(2,1)S(1)}, u32[]{:S(2)}, u32[]{:S(2)}) %collective-permute-start.7) | collective-permute-done | bytes 98336 | tf_op jit(solution)/shard_map/ppermute | solution.py:14
  20.9 0.0 collective-permute-done.3.refs_2_
  20.9 0.0 collective-permute-done.9.refs_10_
  20.9 0.7 %shard_map.77 = (f32[2,256]{1,0:T(2,128)S(1)}, f32[2,256]{1,0:T(2,128)S(1)}, f32[2,128]{1,0:T(2,128)S(1)}, f32[2,128]{1,0:T(2,128)S(1)}) custom-call(f32[1,128]{1,0:T(1,128)S(1)} %broadcast_in_dim.7.scale_ref, s32[1,512]{1,0:T(1,128)S(1)} %add.72.id_ref, bf16[64,768]{1,0:T(8,128)(2,1)S(1)} %divide_convert_fusion.1.refs_0_, ...), custom_call_target="tpu_custom_call" | custom-call | flops 201326592 | bytes 1183232 | tf_op jit(solution)/shard_map/pallas_call | solution.py:76
  21.6 0.2 collective-permute-start.10
  21.8 1.3 %collective-permute-start.13 = (f32[2,128]{1,0:T(2,128)S(1)}, f32[2,128]{1,0:T(2,128)S(1)}, u32[]{:S(2)}, u32[]{:S(2)}) collective-permute-start(f32[2,128]{1,0:T(2,128)S(1)} %get-tuple-element.25), channel_id=1, source_target_pairs={{0,4},{1,5},{2,6},{3,7},{4,0},{5,1},{6,2},{7,3},{8,12},{9,13},{10,... | collective-permute-start | bytes 3080 | tf_op jit(solution)/shard_map/ppermute | solution.py:14
  23.1 0.0 collective-permute-done.10.refs_1_
  23.1 1.7 %collective-permute-start.11 = (f32[2,128]{1,0:T(2,128)S(1)}, f32[2,128]{1,0:T(2,128)S(1)}, u32[]{:S(2)}, u32[]{:S(2)}) collective-permute-start(f32[2,128]{1,0:T(2,128)S(1)} %get-tuple-element.21), channel_id=1, source_target_pairs={{0,16},{1,17},{2,18},{3,19},{4,20},{5,21},{6,22},{7,23},{8,24},{9,... | collective-permute-start | bytes 3080 | tf_op jit(solution)/shard_map/ppermute | solution.py:14
  24.8 0.6 %collective-permute-done.13.refs_1_ = f32[2,128]{1,0:T(2,128)S(1)} collective-permute-done((f32[2,128]{1,0:T(2,128)S(1)}, f32[2,128]{1,0:T(2,128)S(1)}, u32[]{:S(2)}, u32[]{:S(2)}) %collective-permute-start.13) | collective-permute-done | bytes 1056 | tf_op jit(solution)/shard_map/ppermute | solution.py:14
  25.4 1.3 %collective-permute-start.14 = (f32[2,128]{1,0:T(2,128)S(1)}, f32[2,128]{1,0:T(2,128)S(1)}, u32[]{:S(2)}, u32[]{:S(2)}) collective-permute-start(f32[2,128]{1,0:T(2,128)S(1)} %shard_map.80.refs_2_), channel_id=1, source_target_pairs={{0,1},{1,0},{2,3},{3,2},{4,5},{5,4},{6,7},{7,6},{8,9},{9,8},{10,11... | collective-permute-start | bytes 3080 | tf_op jit(solution)/shard_map/ppermute | solution.py:14
  26.7 0.9 %collective-permute-done.11.refs_1_ = f32[2,128]{1,0:T(2,128)S(1)} collective-permute-done((f32[2,128]{1,0:T(2,128)S(1)}, f32[2,128]{1,0:T(2,128)S(1)}, u32[]{:S(2)}, u32[]{:S(2)}) %collective-permute-start.11) | collective-permute-done | bytes 1056 | tf_op jit(solution)/shard_map/ppermute | solution.py:14
  27.6 0.1 shard_map.79
  27.7 1.1 %collective-permute-start.12 = (f32[2,64]{1,0:T(2,128)S(1)}, f32[2,64]{1,0:T(2,128)S(1)}, u32[]{:S(2)}, u32[]{:S(2)}) collective-permute-start(f32[2,64]{1,0:T(2,128)S(1)} %get-tuple-element.23), channel_id=1, source_target_pairs={{0,8},{1,9},{2,10},{3,11},{4,12},{5,13},{6,14},{7,15},{8,0},{9,1},... | collective-permute-start | bytes 1544 | tf_op jit(solution)/shard_map/ppermute | solution.py:14
  28.8 0.2 collective-permute-done.14.refs_3_
  29.1 2.2 %collective-permute-done.12.refs_1_ = f32[2,64]{1,0:T(2,128)S(1)} collective-permute-done((f32[2,64]{1,0:T(2,128)S(1)}, f32[2,64]{1,0:T(2,128)S(1)}, u32[]{:S(2)}, u32[]{:S(2)}) %collective-permute-start.12) | collective-permute-done | bytes 544 | tf_op jit(solution)/shard_map/ppermute | solution.py:14
  31.3 0.5 %shard_map.81 = (f32[1,64]{1,0:T(1,128)}, f32[1,128]{1,0:T(1,128)}) custom-call(f32[2,64]{1,0:T(2,128)S(1)} %get-tuple-element.22.refs_0_, f32[2,64]{1,0:T(2,128)S(1)} %collective-permute-done.12.refs_1_, f32[2,128]{1,0:T(2,128)S(1)} %shard_map.80.refs_2_, f32[2,128]{1,0:T(2,128)S(1)} %collective-permute-done.14.refs_3_), custom_call_target="tpu_custom_call" | custom-call | tf_op jit(solution)/shard_map/pallas_call | solution.py:116
  (7 shorter events, 0.1 us)
Async XLA Ops:
  0.6 4.5 %copy-start = (bf16[512,768]{1,0:T(8,128)(2,1)S(1)}, bf16[512,768]{1,0:T(8,128)(2,1)}, u32[]{:S(2)}) copy-start(bf16[512,768]{1,0:T(8,128)(2,1)} %param.7) | copy-start | bytes 2359300
  0.7 4.4 %copy-start.3 = (bf16[128,512]{1,0:T(8,128)(2,1)S(1)}, bf16[128,512]{1,0:T(8,128)(2,1)}, u32[]{:S(2)}) copy-start(bf16[128,512]{1,0:T(8,128)(2,1)} %param.6) | copy-start | bytes 393220
  2.1 5.5 %copy-start.2 = (bf16[384,768]{1,0:T(8,128)(2,1)S(1)}, bf16[384,768]{1,0:T(8,128)(2,1)}, u32[]{:S(2)}) copy-start(bf16[384,768]{1,0:T(8,128)(2,1)} %param.9) | copy-start | bytes 1769476
  2.1 5.5 %copy-start.4 = (bf16[128,384]{1,0:T(8,128)(2,1)S(1)}, bf16[128,384]{1,0:T(8,128)(2,1)}, u32[]{:S(2)}) copy-start(bf16[128,384]{1,0:T(8,128)(2,1)} %param.8) | copy-start | bytes 294916
  2.1 6.2 %collective-permute-start = (f16[64,768]{1,0:T(8,128)(2,1)S(1)}, f16[64,768]{1,0:T(8,128)(2,1)S(1)}, u32[]{:S(2)}, u32[]{:S(2)}) collective-permute-start(f16[64,768]{1,0:T(8,128)(2,1)S(1)} %convolution_convert_fusion), channel_id=1, source_target_pairs={{0,1},{1,0},{2,3},{3,2},{4,5},{5,4},{6,7},{7,6},{8,9},{9,8},{10,11... | collective-permute-start | bytes 294920 | tf_op jit(solution)/shard_map/ppermute | solution.py:14
  5.4 0.7 %copy-start.1 = (s32[128]{0:T(128)S(1)}, s32[128]{0:T(128)}, u32[]{:S(2)}) copy-start(s32[128]{0:T(128)} %param.10) | copy-start | bytes 1540
  5.4 8.1 %collective-permute-start.1 = (f16[128,768]{1,0:T(8,128)(2,1)S(1)}, f16[128,768]{1,0:T(8,128)(2,1)S(1)}, u32[]{:S(2)}, u32[]{:S(2)}) collective-permute-start(f16[128,768]{1,0:T(8,128)(2,1)S(1)} %get-tuple-element.28), channel_id=1, source_target_pairs={{0,1},{1,0},{2,3},{3,2},{4,5},{5,4},{6,7},{7,6},{8,9},{9,8},{10,11... | collective-permute-start | bytes 589832 | tf_op jit(solution)/shard_map/ppermute | solution.py:14
  6.0 7.7 %collective-permute-start.2 = (s32[1,128]{1,0:T(1,128)S(1)}, s32[1,128]{1,0:T(1,128)S(1)}, u32[]{:S(2)}, u32[]{:S(2)}) collective-permute-start(s32[1,128]{1,0:T(1,128)S(1)} %bitcast.17), channel_id=1, source_target_pairs={{0,4},{1,5},{2,6},{3,7},{4,0},{5,1},{6,2},{7,3},{8,12},{9,13},{10,... | collective-permute-start | bytes 1544 | tf_op jit(solution)/shard_map/ppermute | solution.py:14
  8.5 9.2 %collective-permute-start.4 = (bf16[64,768]{1,0:T(8,128)(2,1)S(1)}, bf16[64,768]{1,0:T(8,128)(2,1)S(1)}, u32[]{:S(2)}, u32[]{:S(2)}) collective-permute-start(bf16[64,768]{1,0:T(8,128)(2,1)S(1)} %divide_convert_fusion.1.refs_0_), channel_id=1, source_target_pairs={{0,24},{1,25},{2,26},{3,27},{4,28},{5,29},{6,30},{7,31},{8,16},{9,... | collective-permute-start | bytes 294920 | tf_op jit(solution)/shard_map/ppermute | solution.py:14
  12.8 6.8 %collective-permute-start.6 = (bf16[64,768]{1,0:T(8,128)(2,1)S(1)}, bf16[64,768]{1,0:T(8,128)(2,1)S(1)}, u32[]{:S(2)}, u32[]{:S(2)}) collective-permute-start(bf16[64,768]{1,0:T(8,128)(2,1)S(1)} %divide_convert_fusion.1.refs_0_), channel_id=1, source_target_pairs={{0,16},{1,17},{2,18},{3,19},{4,20},{5,21},{6,22},{7,23},{8,24},{9,... | collective-permute-start | bytes 294920 | tf_op jit(solution)/shard_map/ppermute | solution.py:14
  12.8 4.8 %collective-permute-start.8 = (bf16[64,768]{1,0:T(8,128)(2,1)S(1)}, bf16[64,768]{1,0:T(8,128)(2,1)S(1)}, u32[]{:S(2)}, u32[]{:S(2)}) collective-permute-start(bf16[64,768]{1,0:T(8,128)(2,1)S(1)} %divide_convert_fusion.1.refs_0_), channel_id=1, source_target_pairs={{0,8},{1,9},{2,10},{3,11},{4,12},{5,13},{6,14},{7,15},{8,0},{9,1},... | collective-permute-start | bytes 294920 | tf_op jit(solution)/shard_map/ppermute | solution.py:14
  13.7 7.2 %collective-permute-start.3 = (bf16[128,768]{1,0:T(8,128)(2,1)S(1)}, bf16[128,768]{1,0:T(8,128)(2,1)S(1)}, u32[]{:S(2)}, u32[]{:S(2)}) collective-permute-start(bf16[128,768]{1,0:T(8,128)(2,1)S(1)} %divide_convert_fusion.refs_1_), channel_id=1, source_target_pairs={{0,4},{1,5},{2,6},{3,7},{4,0},{5,1},{6,2},{7,3},{8,12},{9,13},{10,... | collective-permute-start | bytes 589832 | tf_op jit(solution)/shard_map/ppermute | solution.py:14
  17.6 3.3 %collective-permute-start.9 = (bf16[128,768]{1,0:T(8,128)(2,1)S(1)}, bf16[128,768]{1,0:T(8,128)(2,1)S(1)}, u32[]{:S(2)}, u32[]{:S(2)}) collective-permute-start(bf16[128,768]{1,0:T(8,128)(2,1)S(1)} %pad_maximum_fusion), channel_id=1, source_target_pairs={{0,2},{1,3},{2,0},{3,1},{4,6},{5,7},{6,4},{7,5},{8,10},{9,11},{10,... | collective-permute-start | bytes 589832 | tf_op jit(solution)/shard_map/ppermute | solution.py:14
  17.7 2.7 %collective-permute-start.5 = (bf16[64,768]{1,0:T(8,128)(2,1)S(1)}, bf16[64,768]{1,0:T(8,128)(2,1)S(1)}, u32[]{:S(2)}, u32[]{:S(2)}) collective-permute-start(bf16[64,768]{1,0:T(8,128)(2,1)S(1)} %collective-permute-done.4.refs_5_), channel_id=1, source_target_pairs={{0,2},{1,3},{2,0},{3,1},{4,6},{5,7},{6,4},{7,5},{8,10},{9,11},{10,... | collective-permute-start | bytes 294920 | tf_op jit(solution)/shard_map/ppermute | solution.py:14
  19.6 1.3 %collective-permute-start.7 = (bf16[64,768]{1,0:T(8,128)(2,1)S(1)}, bf16[64,768]{1,0:T(8,128)(2,1)S(1)}, u32[]{:S(2)}, u32[]{:S(2)}) collective-permute-start(bf16[64,768]{1,0:T(8,128)(2,1)S(1)} %collective-permute-done.6.refs_7_), channel_id=1, source_target_pairs={{0,2},{1,3},{2,0},{3,1},{4,6},{5,7},{6,4},{7,5},{8,10},{9,11},{10,... | collective-permute-start | bytes 294920 | tf_op jit(solution)/shard_map/ppermute | solution.py:14
  21.6 1.5 %collective-permute-start.10 = (f32[2,256]{1,0:T(2,128)S(1)}, f32[2,256]{1,0:T(2,128)S(1)}, u32[]{:S(2)}, u32[]{:S(2)}) collective-permute-start(f32[2,256]{1,0:T(2,128)S(1)} %get-tuple-element.19), channel_id=1, source_target_pairs={{0,2},{1,3},{2,0},{3,1},{4,6},{5,7},{6,4},{7,5},{8,10},{9,11},{10,... | collective-permute-start | bytes 6152 | tf_op jit(solution)/shard_map/ppermute | solution.py:14
  21.8 3.6 %collective-permute-start.13 = (f32[2,128]{1,0:T(2,128)S(1)}, f32[2,128]{1,0:T(2,128)S(1)}, u32[]{:S(2)}, u32[]{:S(2)}) collective-permute-start(f32[2,128]{1,0:T(2,128)S(1)} %get-tuple-element.25), channel_id=1, source_target_pairs={{0,4},{1,5},{2,6},{3,7},{4,0},{5,1},{6,2},{7,3},{8,12},{9,13},{10,... | collective-permute-start | bytes 3080 | tf_op jit(solution)/shard_map/ppermute | solution.py:14
  23.1 4.5 %collective-permute-start.11 = (f32[2,128]{1,0:T(2,128)S(1)}, f32[2,128]{1,0:T(2,128)S(1)}, u32[]{:S(2)}, u32[]{:S(2)}) collective-permute-start(f32[2,128]{1,0:T(2,128)S(1)} %get-tuple-element.21), channel_id=1, source_target_pairs={{0,16},{1,17},{2,18},{3,19},{4,20},{5,21},{6,22},{7,23},{8,24},{9,... | collective-permute-start | bytes 3080 | tf_op jit(solution)/shard_map/ppermute | solution.py:14
  25.4 3.6 %collective-permute-start.14 = (f32[2,128]{1,0:T(2,128)S(1)}, f32[2,128]{1,0:T(2,128)S(1)}, u32[]{:S(2)}, u32[]{:S(2)}) collective-permute-start(f32[2,128]{1,0:T(2,128)S(1)} %shard_map.80.refs_2_), channel_id=1, source_target_pairs={{0,1},{1,0},{2,3},{3,2},{4,5},{5,4},{6,7},{7,6},{8,9},{9,8},{10,11... | collective-permute-start | bytes 3080 | tf_op jit(solution)/shard_map/ppermute | solution.py:14
  27.7 3.6 %collective-permute-start.12 = (f32[2,64]{1,0:T(2,128)S(1)}, f32[2,64]{1,0:T(2,128)S(1)}, u32[]{:S(2)}, u32[]{:S(2)}) collective-permute-start(f32[2,64]{1,0:T(2,128)S(1)} %get-tuple-element.23), channel_id=1, source_target_pairs={{0,8},{1,9},{2,10},{3,11},{4,12},{5,13},{6,14},{7,15},{8,0},{9,1},... | collective-permute-start | bytes 1544 | tf_op jit(solution)/shard_map/ppermute | solution.py:14

commit v7 on v5

--- a/solution.py
+++ b/solution.py
@@ -14,15 +14,21 @@
     return lax.ppermute(value, ("dp", "mp"), pairs)
 
 
+def normalize_kernel(raw_ref, out_ref):
+    raw = raw_ref[...]
+    norm_sq = jnp.sum(raw * raw, axis=1, keepdims=True)
+    out_ref[...] = (raw / jnp.sqrt(norm_sq + 1e-06)).astype(jnp.bfloat16)
+
+
 def normalize(raw):
-    norm_sq = jnp.sum(raw * raw, axis=1, keepdims=True)
-    return (raw / jnp.sqrt(norm_sq + 1e-06)).astype(jnp.bfloat16)
-
-
-def join(stats):
-    top = functools.reduce(jnp.maximum, [s[0] for s in stats])
-    total = sum(jnp.exp(s[0] - top) for s in stats)
-    return jnp.stack([top + jnp.log(total), sum(s[1] for s in stats)])
+    vmem = pl.BlockSpec(memory_space=pltpu.VMEM)
+    return pl.pallas_call(
+        normalize_kernel,
+        out_shape=jax.ShapeDtypeStruct(raw.shape, jnp.bfloat16),
+        in_specs=[vmem],
+        out_specs=vmem,
+        compiler_params=pltpu.CompilerParams(vmem_limit_bytes=8 * 2**20),
+    )(raw)
 
 
 def stats_kernel(n_image, places, n_col, scale_ref, id_ref, *refs):

time: 32 us -> 31.9 us (level)
  other arithmetic: 0.57 us -> 0.17 us
  transfers between devices with their start and end apart: 15 -> 15, of which waited for: 8 -> 8; matrix products, arithmetic and copies ran while one was open for 4% -> 3% of each run, Pallas kernels for 0% -> 1%
where the time goes in v7:
time: 31.9 us; the launch traced here: 31.7 us
  starting transfers between devices  17.4 us (55%)
  waiting for transfers between devices  8.52 us (27%)
  matrix products  1.88 us (6%)
  Pallas kernels  1.62 us (5%)
  between operations  1.41 us (4%)
  local copies, waits for them, and re-layouts  0.75 us (2%)
    ppermute x15, starting transfers between devices, exchange(): return lax.ppermute(value, ('dp', 'mp'), pairs)  17.4 us
    ppermute x15, waiting for transfers between devices, exchange(): return lax.ppermute(value, ('dp', 'mp'), pairs)  8.52 us
    dot_general x2, matrix products, text_rows(): return jnp.dot(mine, text_proj, preferred_element_type=jnp.float32)  1.6 us
    pallas_call x1, Pallas kernels, block_stats(): pl.pallas_call(functools.partial(stats_kernel, len(images), places, len(c...  0.73 us
    pallas_call x4, Pallas kernels, join(): pl.pallas_call(functools.partial(join_kernel, [len(g) for g in groups], s...  0.64 us
  transfers between devices with their start and end apart: 15, of which 8 were waited for; matrix products, arithmetic and copies ran while one was open for 3% of the time, Pallas kernels for 1%

profile of v7, /device:TPU:0, one launch (start us, length us, event | category | flops | bytes accessed | tf_op | source)
XLA Modules:
  0.0 31.7 jit_solution(542661588120039889)
XLA Ops:
  0.6 0.0 copy-start
  0.7 0.0 copy-start.3
  0.7 1.4 %convolution_convert_fusion = f16[64,768]{1,0:T(8,128)(2,1)S(1)} fusion(bf16[384,768]{1,0:T(8,128)(2,1)} %param.9, bf16[128,384]{1,0:T(8,128)(2,1)} %param.8, s32[]{:T(128)S(6)} %select_n.7), kind=kOutput, calls=%fused_computation | convolution fusion | flops 37797888 | bytes 737284 | tf_op jit(solution)/shard_map/dot_general | solution.py:153
  2.1 0.0 copy-start.2
  2.1 0.0 copy-start.4
  2.1 3.0 %collective-permute-start = (f16[64,768]{1,0:T(8,128)(2,1)S(1)}, f16[64,768]{1,0:T(8,128)(2,1)S(1)}, u32[]{:S(2)}, u32[]{:S(2)}) collective-permute-start(f16[64,768]{1,0:T(8,128)(2,1)S(1)} %convolution_convert_fusion), channel_id=1, source_target_pairs={{0,1},{1,0},{2,3},{3,2},{4,5},{5,4},{6,7},{7,6},{8,9},{9,8},{10,11... | collective-permute-start | bytes 294920 | tf_op jit(solution)/shard_map/ppermute | solution.py:14
  5.1 0.0 copy-done
  5.1 0.0 copy-done.3
  5.1 0.3 fusion.5
  5.4 0.0 copy-start.1
  5.4 0.1 collective-permute-start.1
  5.5 0.6 %copy-done.1 = s32[128]{0:T(128)S(1)} copy-done((s32[128]{0:T(128)S(1)}, s32[128]{0:T(128)}, u32[]{:S(2)}) %copy-start.1) | copy-done | bytes 536
  6.0 1.5 %collective-permute-start.2 = (s32[1,128]{1,0:T(1,128)S(1)}, s32[1,128]{1,0:T(1,128)S(1)}, u32[]{:S(2)}, u32[]{:S(2)}) collective-permute-start(s32[1,128]{1,0:T(1,128)S(1)} %bitcast.17), channel_id=1, source_target_pairs={{0,4},{1,5},{2,6},{3,7},{4,0},{5,1},{6,2},{7,3},{8,12},{9,13},{10,... | collective-permute-start | bytes 1544 | tf_op jit(solution)/shard_map/ppermute | solution.py:14
  7.6 0.0 copy-done.2
  7.6 0.0 copy-done.4
  7.6 0.2 fusion.1
  7.8 0.1 stack.35
  7.9 0.4 %collective-permute-done = f16[64,768]{1,0:T(8,128)(2,1)S(1)} collective-permute-done((f16[64,768]{1,0:T(8,128)(2,1)S(1)}, f16[64,768]{1,0:T(8,128)(2,1)S(1)}, u32[]{:S(2)}, u32[]{:S(2)}) %collective-permute-start) | collective-permute-done | bytes 98336 | tf_op jit(solution)/shard_map/ppermute | solution.py:14
  8.3 0.1 shard_map.77.refs_0_
  8.4 4.3 %collective-permute-start.4 = (bf16[64,768]{1,0:T(8,128)(2,1)S(1)}, bf16[64,768]{1,0:T(8,128)(2,1)S(1)}, u32[]{:S(2)}, u32[]{:S(2)}) collective-permute-start(bf16[64,768]{1,0:T(8,128)(2,1)S(1)} %shard_map.77.refs_0_), channel_id=1, source_target_pairs={{0,24},{1,25},{2,26},{3,27},{4,28},{5,29},{6,30},{7,31},{8,16},{9,... | collective-permute-start | bytes 294920 | tf_op jit(solution)/shard_map/ppermute | solution.py:14
  12.7 0.0 collective-permute-start.6
  12.7 0.6 %collective-permute-start.8 = (bf16[64,768]{1,0:T(8,128)(2,1)S(1)}, bf16[64,768]{1,0:T(8,128)(2,1)S(1)}, u32[]{:S(2)}, u32[]{:S(2)}) collective-permute-start(bf16[64,768]{1,0:T(8,128)(2,1)S(1)} %shard_map.77.refs_0_), channel_id=1, source_target_pairs={{0,8},{1,9},{2,10},{3,11},{4,12},{5,13},{6,14},{7,15},{8,0},{9,1},... | collective-permute-start | bytes 294920 | tf_op jit(solution)/shard_map/ppermute | solution.py:14
  13.4 0.0 collective-permute-done.1
  13.4 0.1 shard_map.78.refs_1_
  13.6 0.0 collective-permute-done.2.refs_4_
  13.6 1.7 %collective-permute-start.3 = (bf16[128,768]{1,0:T(8,128)(2,1)S(1)}, bf16[128,768]{1,0:T(8,128)(2,1)S(1)}, u32[]{:S(2)}, u32[]{:S(2)}) collective-permute-start(bf16[128,768]{1,0:T(8,128)(2,1)S(1)} %shard_map.78.refs_1_), channel_id=1, source_target_pairs={{0,4},{1,5},{2,6},{3,7},{4,0},{5,1},{6,2},{7,3},{8,12},{9,13},{10,... | collective-permute-start | bytes 589832 | tf_op jit(solution)/shard_map/ppermute | solution.py:14
  15.3 2.2 %collective-permute-done.8.refs_9_ = bf16[64,768]{1,0:T(8,128)(2,1)S(1)} collective-permute-done((bf16[64,768]{1,0:T(8,128)(2,1)S(1)}, bf16[64,768]{1,0:T(8,128)(2,1)S(1)}, u32[]{:S(2)}, u32[]{:S(2)}) %collective-permute-start.8) | collective-permute-done | bytes 98336 | tf_op jit(solution)/shard_map/ppermute | solution.py:14
  17.5 0.1 collective-permute-start.9
  17.6 0.0 collective-permute-done.4.refs_5_
  17.6 0.5 %collective-permute-start.5 = (bf16[64,768]{1,0:T(8,128)(2,1)S(1)}, bf16[64,768]{1,0:T(8,128)(2,1)S(1)}, u32[]{:S(2)}, u32[]{:S(2)}) collective-permute-start(bf16[64,768]{1,0:T(8,128)(2,1)S(1)} %collective-permute-done.4.refs_5_), channel_id=1, source_target_pairs={{0,2},{1,3},{2,0},{3,1},{4,6},{5,7},{6,4},{7,5},{8,10},{9,11},{10,... | collective-permute-start | bytes 294920 | tf_op jit(solution)/shard_map/ppermute | solution.py:14
  18.1 1.4 %collective-permute-done.6.refs_7_ = bf16[64,768]{1,0:T(8,128)(2,1)S(1)} collective-permute-done((bf16[64,768]{1,0:T(8,128)(2,1)S(1)}, bf16[64,768]{1,0:T(8,128)(2,1)S(1)}, u32[]{:S(2)}, u32[]{:S(2)}) %collective-permute-start.6) | collective-permute-done | bytes 98336 | tf_op jit(solution)/shard_map/ppermute | solution.py:14
  19.5 0.0 collective-permute-start.7
  19.5 0.1 iota_add_fusion
  20.2 0.1 add.50.id_ref
  20.3 0.0 collective-permute-done.5.refs_6_
  20.3 0.5 %collective-permute-done.7.refs_8_ = bf16[64,768]{1,0:T(8,128)(2,1)S(1)} collective-permute-done((bf16[64,768]{1,0:T(8,128)(2,1)S(1)}, bf16[64,768]{1,0:T(8,128)(2,1)S(1)}, u32[]{:S(2)}, u32[]{:S(2)}) %collective-permute-start.7) | collective-permute-done | bytes 98336 | tf_op jit(solution)/shard_map/ppermute | solution.py:14
  20.8 0.0 collective-permute-done.3.refs_2_
  20.8 0.0 collective-permute-done.9.refs_10_
  20.8 0.7 %shard_map.79 = (f32[2,256]{1,0:T(2,128)S(1)}, f32[2,256]{1,0:T(2,128)S(1)}, f32[2,128]{1,0:T(2,128)S(1)}, f32[2,128]{1,0:T(2,128)S(1)}) custom-call(f32[1,128]{1,0:T(1,128)S(1)} %broadcast_in_dim.14.scale_ref, s32[1,512]{1,0:T(1,128)S(1)} %add.50.id_ref, bf16[64,768]{1,0:T(8,128)(2,1)S(1)} %shard_map.77.refs_0_, bf16[128,768]{1,0:T(8,128)(2,1)S(1)} %shard_map.78.refs_1_, ...), custom_call_target="tpu_custom_call" | custom-call | flops 201326592 | bytes 1183232 | tf_op jit(solution)/shard_map/pallas_call | solution.py:88
  21.6 0.2 collective-permute-start.10
  21.7 1.3 %collective-permute-start.13 = (f32[2,128]{1,0:T(2,128)S(1)}, f32[2,128]{1,0:T(2,128)S(1)}, u32[]{:S(2)}, u32[]{:S(2)}) collective-permute-start(f32[2,128]{1,0:T(2,128)S(1)} %get-tuple-element.25), channel_id=1, source_target_pairs={{0,4},{1,5},{2,6},{3,7},{4,0},{5,1},{6,2},{7,3},{8,12},{9,13},{10,... | collective-permute-start | bytes 3080 | tf_op jit(solution)/shard_map/ppermute | solution.py:14
  23.0 0.0 collective-permute-done.10.refs_1_
  23.0 1.7 %collective-permute-start.11 = (f32[2,128]{1,0:T(2,128)S(1)}, f32[2,128]{1,0:T(2,128)S(1)}, u32[]{:S(2)}, u32[]{:S(2)}) collective-permute-start(f32[2,128]{1,0:T(2,128)S(1)} %get-tuple-element.21), channel_id=1, source_target_pairs={{0,16},{1,17},{2,18},{3,19},{4,20},{5,21},{6,22},{7,23},{8,24},{9,... | collective-permute-start | bytes 3080 | tf_op jit(solution)/shard_map/ppermute | solution.py:14
  24.7 0.6 %collective-permute-done.13.refs_1_ = f32[2,128]{1,0:T(2,128)S(1)} collective-permute-done((f32[2,128]{1,0:T(2,128)S(1)}, f32[2,128]{1,0:T(2,128)S(1)}, u32[]{:S(2)}, u32[]{:S(2)}) %collective-permute-start.13) | collective-permute-done | bytes 1056 | tf_op jit(solution)/shard_map/ppermute | solution.py:14
  25.3 1.3 %collective-permute-start.14 = (f32[2,128]{1,0:T(2,128)S(1)}, f32[2,128]{1,0:T(2,128)S(1)}, u32[]{:S(2)}, u32[]{:S(2)}) collective-permute-start(f32[2,128]{1,0:T(2,128)S(1)} %shard_map.82.refs_2_), channel_id=1, source_target_pairs={{0,1},{1,0},{2,3},{3,2},{4,5},{5,4},{6,7},{7,6},{8,9},{9,8},{10,11... | collective-permute-start | bytes 3080 | tf_op jit(solution)/shard_map/ppermute | solution.py:14
  26.7 0.9 %collective-permute-done.11.refs_1_ = f32[2,128]{1,0:T(2,128)S(1)} collective-permute-done((f32[2,128]{1,0:T(2,128)S(1)}, f32[2,128]{1,0:T(2,128)S(1)}, u32[]{:S(2)}, u32[]{:S(2)}) %collective-permute-start.11) | collective-permute-done | bytes 1056 | tf_op jit(solution)/shard_map/ppermute | solution.py:14
  27.6 0.1 shard_map.81
  27.6 1.1 %collective-permute-start.12 = (f32[2,64]{1,0:T(2,128)S(1)}, f32[2,64]{1,0:T(2,128)S(1)}, u32[]{:S(2)}, u32[]{:S(2)}) collective-permute-start(f32[2,64]{1,0:T(2,128)S(1)} %get-tuple-element.23), channel_id=1, source_target_pairs={{0,8},{1,9},{2,10},{3,11},{4,12},{5,13},{6,14},{7,15},{8,0},{9,1},... | collective-permute-start | bytes 1544 | tf_op jit(solution)/shard_map/ppermute | solution.py:14
  28.7 0.2 collective-permute-done.14.refs_3_
  29.0 2.2 %collective-permute-done.12.refs_1_ = f32[2,64]{1,0:T(2,128)S(1)} collective-permute-done((f32[2,64]{1,0:T(2,128)S(1)}, f32[2,64]{1,0:T(2,128)S(1)}, u32[]{:S(2)}, u32[]{:S(2)}) %collective-permute-start.12) | collective-permute-done | bytes 544 | tf_op jit(solution)/shard_map/ppermute | solution.py:14
  31.2 0.5 %shard_map.83 = (f32[1,64]{1,0:T(1,128)}, f32[1,128]{1,0:T(1,128)}) custom-call(f32[2,64]{1,0:T(2,128)S(1)} %get-tuple-element.22.refs_0_, f32[2,64]{1,0:T(2,128)S(1)} %collective-permute-done.12.refs_1_, f32[2,128]{1,0:T(2,128)S(1)} %shard_map.82.refs_2_, f32[2,128]{1,0:T(2,128)S(1)} %collective-permute-done.14.refs_3_), custom_call_target="tpu_custom_call" | custom-call | tf_op jit(solution)/shard_map/pallas_call | solution.py:128
  (7 shorter events, 0.1 us)
Async XLA Ops:
  0.6 4.5 %copy-start = (bf16[512,768]{1,0:T(8,128)(2,1)S(1)}, bf16[512,768]{1,0:T(8,128)(2,1)}, u32[]{:S(2)}) copy-start(bf16[512,768]{1,0:T(8,128)(2,1)} %param.7) | copy-start | bytes 2359300
  0.7 4.4 %copy-start.3 = (bf16[128,512]{1,0:T(8,128)(2,1)S(1)}, bf16[128,512]{1,0:T(8,128)(2,1)}, u32[]{:S(2)}) copy-start(bf16[128,512]{1,0:T(8,128)(2,1)} %param.6) | copy-start | bytes 393220
  2.1 5.5 %copy-start.2 = (bf16[384,768]{1,0:T(8,128)(2,1)S(1)}, bf16[384,768]{1,0:T(8,128)(2,1)}, u32[]{:S(2)}) copy-start(bf16[384,768]{1,0:T(8,128)(2,1)} %param.9) | copy-start | bytes 1769476
  2.1 5.5 %copy-start.4 = (bf16[128,384]{1,0:T(8,128)(2,1)S(1)}, bf16[128,384]{1,0:T(8,128)(2,1)}, u32[]{:S(2)}) copy-start(bf16[128,384]{1,0:T(8,128)(2,1)} %param.8) | copy-start | bytes 294916
  2.1 6.2 %collective-permute-start = (f16[64,768]{1,0:T(8,128)(2,1)S(1)}, f16[64,768]{1,0:T(8,128)(2,1)S(1)}, u32[]{:S(2)}, u32[]{:S(2)}) collective-permute-start(f16[64,768]{1,0:T(8,128)(2,1)S(1)} %convolution_convert_fusion), channel_id=1, source_target_pairs={{0,1},{1,0},{2,3},{3,2},{4,5},{5,4},{6,7},{7,6},{8,9},{9,8},{10,11... | collective-permute-start | bytes 294920 | tf_op jit(solution)/shard_map/ppermute | solution.py:14
  5.4 0.7 %copy-start.1 = (s32[128]{0:T(128)S(1)}, s32[128]{0:T(128)}, u32[]{:S(2)}) copy-start(s32[128]{0:T(128)} %param.10) | copy-start | bytes 1540
  5.4 8.0 %collective-permute-start.1 = (f16[128,768]{1,0:T(8,128)(2,1)S(1)}, f16[128,768]{1,0:T(8,128)(2,1)S(1)}, u32[]{:S(2)}, u32[]{:S(2)}) collective-permute-start(f16[128,768]{1,0:T(8,128)(2,1)S(1)} %get-tuple-element.28), channel_id=1, source_target_pairs={{0,1},{1,0},{2,3},{3,2},{4,5},{5,4},{6,7},{7,6},{8,9},{9,8},{10,11... | collective-permute-start | bytes 589832 | tf_op jit(solution)/shard_map/ppermute | solution.py:14
  6.0 7.5 %collective-permute-start.2 = (s32[1,128]{1,0:T(1,128)S(1)}, s32[1,128]{1,0:T(1,128)S(1)}, u32[]{:S(2)}, u32[]{:S(2)}) collective-permute-start(s32[1,128]{1,0:T(1,128)S(1)} %bitcast.17), channel_id=1, source_target_pairs={{0,4},{1,5},{2,6},{3,7},{4,0},{5,1},{6,2},{7,3},{8,12},{9,13},{10,... | collective-permute-start | bytes 1544 | tf_op jit(solution)/shard_map/ppermute | solution.py:14
  8.4 9.2 %collective-permute-start.4 = (bf16[64,768]{1,0:T(8,128)(2,1)S(1)}, bf16[64,768]{1,0:T(8,128)(2,1)S(1)}, u32[]{:S(2)}, u32[]{:S(2)}) collective-permute-start(bf16[64,768]{1,0:T(8,128)(2,1)S(1)} %shard_map.77.refs_0_), channel_id=1, source_target_pairs={{0,24},{1,25},{2,26},{3,27},{4,28},{5,29},{6,30},{7,31},{8,16},{9,... | collective-permute-start | bytes 294920 | tf_op jit(solution)/shard_map/ppermute | solution.py:14
  12.7 6.8 %collective-permute-start.6 = (bf16[64,768]{1,0:T(8,128)(2,1)S(1)}, bf16[64,768]{1,0:T(8,128)(2,1)S(1)}, u32[]{:S(2)}, u32[]{:S(2)}) collective-permute-start(bf16[64,768]{1,0:T(8,128)(2,1)S(1)} %shard_map.77.refs_0_), channel_id=1, source_target_pairs={{0,16},{1,17},{2,18},{3,19},{4,20},{5,21},{6,22},{7,23},{8,24},{9,... | collective-permute-start | bytes 294920 | tf_op jit(solution)/shard_map/ppermute | solution.py:14
  12.7 4.8 %collective-permute-start.8 = (bf16[64,768]{1,0:T(8,128)(2,1)S(1)}, bf16[64,768]{1,0:T(8,128)(2,1)S(1)}, u32[]{:S(2)}, u32[]{:S(2)}) collective-permute-start(bf16[64,768]{1,0:T(8,128)(2,1)S(1)} %shard_map.77.refs_0_), channel_id=1, source_target_pairs={{0,8},{1,9},{2,10},{3,11},{4,12},{5,13},{6,14},{7,15},{8,0},{9,1},... | collective-permute-start | bytes 294920 | tf_op jit(solution)/shard_map/ppermute | solution.py:14
  13.6 7.2 %collective-permute-start.3 = (bf16[128,768]{1,0:T(8,128)(2,1)S(1)}, bf16[128,768]{1,0:T(8,128)(2,1)S(1)}, u32[]{:S(2)}, u32[]{:S(2)}) collective-permute-start(bf16[128,768]{1,0:T(8,128)(2,1)S(1)} %shard_map.78.refs_1_), channel_id=1, source_target_pairs={{0,4},{1,5},{2,6},{3,7},{4,0},{5,1},{6,2},{7,3},{8,12},{9,13},{10,... | collective-permute-start | bytes 589832 | tf_op jit(solution)/shard_map/ppermute | solution.py:14
  17.5 3.3 %collective-permute-start.9 = (bf16[128,768]{1,0:T(8,128)(2,1)S(1)}, bf16[128,768]{1,0:T(8,128)(2,1)S(1)}, u32[]{:S(2)}, u32[]{:S(2)}) collective-permute-start(bf16[128,768]{1,0:T(8,128)(2,1)S(1)} %pad_maximum_fusion), channel_id=1, source_target_pairs={{0,2},{1,3},{2,0},{3,1},{4,6},{5,7},{6,4},{7,5},{8,10},{9,11},{10,... | collective-permute-start | bytes 589832 | tf_op jit(solution)/shard_map/ppermute | solution.py:14
  17.6 2.7 %collective-permute-start.5 = (bf16[64,768]{1,0:T(8,128)(2,1)S(1)}, bf16[64,768]{1,0:T(8,128)(2,1)S(1)}, u32[]{:S(2)}, u32[]{:S(2)}) collective-permute-start(bf16[64,768]{1,0:T(8,128)(2,1)S(1)} %collective-permute-done.4.refs_5_), channel_id=1, source_target_pairs={{0,2},{1,3},{2,0},{3,1},{4,6},{5,7},{6,4},{7,5},{8,10},{9,11},{10,... | collective-permute-start | bytes 294920 | tf_op jit(solution)/shard_map/ppermute | solution.py:14
  19.5 1.3 %collective-permute-start.7 = (bf16[64,768]{1,0:T(8,128)(2,1)S(1)}, bf16[64,768]{1,0:T(8,128)(2,1)S(1)}, u32[]{:S(2)}, u32[]{:S(2)}) collective-permute-start(bf16[64,768]{1,0:T(8,128)(2,1)S(1)} %collective-permute-done.6.refs_7_), channel_id=1, source_target_pairs={{0,2},{1,3},{2,0},{3,1},{4,6},{5,7},{6,4},{7,5},{8,10},{9,11},{10,... | collective-permute-start | bytes 294920 | tf_op jit(solution)/shard_map/ppermute | solution.py:14
  21.6 1.4 %collective-permute-start.10 = (f32[2,256]{1,0:T(2,128)S(1)}, f32[2,256]{1,0:T(2,128)S(1)}, u32[]{:S(2)}, u32[]{:S(2)}) collective-permute-start(f32[2,256]{1,0:T(2,128)S(1)} %get-tuple-element.19), channel_id=1, source_target_pairs={{0,2},{1,3},{2,0},{3,1},{4,6},{5,7},{6,4},{7,5},{8,10},{9,11},{10,... | collective-permute-start | bytes 6152 | tf_op jit(solution)/shard_map/ppermute | solution.py:14
  21.7 3.6 %collective-permute-start.13 = (f32[2,128]{1,0:T(2,128)S(1)}, f32[2,128]{1,0:T(2,128)S(1)}, u32[]{:S(2)}, u32[]{:S(2)}) collective-permute-start(f32[2,128]{1,0:T(2,128)S(1)} %get-tuple-element.25), channel_id=1, source_target_pairs={{0,4},{1,5},{2,6},{3,7},{4,0},{5,1},{6,2},{7,3},{8,12},{9,13},{10,... | collective-permute-start | bytes 3080 | tf_op jit(solution)/shard_map/ppermute | solution.py:14
  23.0 4.5 %collective-permute-start.11 = (f32[2,128]{1,0:T(2,128)S(1)}, f32[2,128]{1,0:T(2,128)S(1)}, u32[]{:S(2)}, u32[]{:S(2)}) collective-permute-start(f32[2,128]{1,0:T(2,128)S(1)} %get-tuple-element.21), channel_id=1, source_target_pairs={{0,16},{1,17},{2,18},{3,19},{4,20},{5,21},{6,22},{7,23},{8,24},{9,... | collective-permute-start | bytes 3080 | tf_op jit(solution)/shard_map/ppermute | solution.py:14
  25.3 3.6 %collective-permute-start.14 = (f32[2,128]{1,0:T(2,128)S(1)}, f32[2,128]{1,0:T(2,128)S(1)}, u32[]{:S(2)}, u32[]{:S(2)}) collective-permute-start(f32[2,128]{1,0:T(2,128)S(1)} %shard_map.82.refs_2_), channel_id=1, source_target_pairs={{0,1},{1,0},{2,3},{3,2},{4,5},{5,4},{6,7},{7,6},{8,9},{9,8},{10,11... | collective-permute-start | bytes 3080 | tf_op jit(solution)/shard_map/ppermute | solution.py:14
  27.6 3.6 %collective-permute-start.12 = (f32[2,64]{1,0:T(2,128)S(1)}, f32[2,64]{1,0:T(2,128)S(1)}, u32[]{:S(2)}, u32[]{:S(2)}) collective-permute-start(f32[2,64]{1,0:T(2,128)S(1)} %get-tuple-element.23), channel_id=1, source_target_pairs={{0,8},{1,9},{2,10},{3,11},{4,12},{5,13},{6,14},{7,15},{8,0},{9,1},... | collective-permute-start | bytes 1544 | tf_op jit(solution)/shard_map/ppermute | solution.py:14

commit v8 on v7

--- a/solution.py
+++ b/solution.py
@@ -6,6 +6,9 @@
 from jax.experimental import pallas as pl
 from jax.experimental.pallas import tpu as pltpu
 from jax.sharding import PartitionSpec as P
+
+
+LOG2_E = 1.4426950408889634
 
 
 def exchange(value, stride, step=0):
@@ -46,7 +49,7 @@
     rows = images[0].shape[0]
     image = jnp.concatenate([r[...] for r in images], axis=0)
     text = jnp.concatenate(texts, axis=0)
-    logits = scale_ref[0:1, 0:1] * lax.dot_general(
+    logits = (scale_ref[0:1, 0:1] * LOG2_E) * lax.dot_general(
         image, text, (((1,), (1,)), ((), ())), preferred_element_type=jnp.float32
     )
     ids = id_ref[...]
@@ -55,13 +58,13 @@
     picked = jnp.where(pair == ids, logits, 0.0)
 
     top = jnp.max(logits, axis=0, keepdims=True)
-    lse = top + jnp.log(jnp.sum(jnp.exp(logits - top), axis=0, keepdims=True))
-    positive = jnp.sum(picked, axis=0, keepdims=True)
+    lse = (top + jnp.log2(jnp.sum(jnp.exp2(logits - top), axis=0, keepdims=True))) / LOG2_E
+    positive = jnp.sum(picked, axis=0, keepdims=True) / LOG2_E
     write(col_out, lse, positive)
 
     top = jnp.max(logits, axis=1, keepdims=True)
-    lse = top + jnp.log(jnp.sum(jnp.exp(logits - top), axis=1, keepdims=True))
-    positive = jnp.sum(picked, axis=1, keepdims=True)
+    lse = (top + jnp.log2(jnp.sum(jnp.exp2(logits - top), axis=1, keepdims=True))) / LOG2_E
+    positive = jnp.sum(picked, axis=1, keepdims=True) / LOG2_E
     lane = lax.broadcasted_iota(jnp.int32, (image.shape[0], rows), 1)
     both = jnp.where(lane == 0, lse, positive).T
     write(row_out, both[0:1], both[1:2])

time: 31.9 us -> 31.9 us (level)
  no operation moved by 1% of the time
where the time goes in v8:
time: 31.9 us; the launch traced here: 31.7 us
  starting transfers between devices  17.4 us (55%)
  waiting for transfers between devices  8.52 us (27%)
  matrix products  1.88 us (6%)
  Pallas kernels  1.6 us (5%)
  between operations  1.41 us (4%)
  local copies, waits for them, and re-layouts  0.75 us (2%)
    ppermute x15, starting transfers between devices, exchange(): return lax.ppermute(value, ('dp', 'mp'), pairs)  17.4 us
    ppermute x15, waiting for transfers between devices, exchange(): return lax.ppermute(value, ('dp', 'mp'), pairs)  8.52 us
    dot_general x2, matrix products, text_rows(): return jnp.dot(mine, text_proj, preferred_element_type=jnp.float32)  1.6 us
    pallas_call x1, Pallas kernels, block_stats(): pl.pallas_call(functools.partial(stats_kernel, len(images), places, len(c...  0.71 us
    pallas_call x4, Pallas kernels, join(): pl.pallas_call(functools.partial(join_kernel, [len(g) for g in groups], s...  0.64 us
  transfers between devices with their start and end apart: 15, of which 8 were waited for; matrix products, arithmetic and copies ran while one was open for 3% of the time, Pallas kernels for 1%

profile of v8, /device:TPU:0, one launch (start us, length us, event | category | flops | bytes accessed | tf_op | source)
XLA Modules:
  0.0 31.7 jit_solution(6153918755481317923)
XLA Ops:
  0.6 0.0 copy-start
  0.7 0.0 copy-start.3
  0.7 1.4 %convolution_convert_fusion = f16[64,768]{1,0:T(8,128)(2,1)S(1)} fusion(bf16[384,768]{1,0:T(8,128)(2,1)} %param.9, bf16[128,384]{1,0:T(8,128)(2,1)} %param.8, s32[]{:T(128)S(6)} %select_n.7), kind=kOutput, calls=%fused_computation | convolution fusion | flops 37797888 | bytes 737284 | tf_op jit(solution)/shard_map/dot_general | solution.py:156
  2.1 0.0 copy-start.2
  2.1 0.0 copy-start.4
  2.1 3.0 %collective-permute-start = (f16[64,768]{1,0:T(8,128)(2,1)S(1)}, f16[64,768]{1,0:T(8,128)(2,1)S(1)}, u32[]{:S(2)}, u32[]{:S(2)}) collective-permute-start(f16[64,768]{1,0:T(8,128)(2,1)S(1)} %convolution_convert_fusion), channel_id=1, source_target_pairs={{0,1},{1,0},{2,3},{3,2},{4,5},{5,4},{6,7},{7,6},{8,9},{9,8},{10,11... | collective-permute-start | bytes 294920 | tf_op jit(solution)/shard_map/ppermute | solution.py:17
  5.1 0.0 copy-done
  5.1 0.0 copy-done.3
  5.1 0.3 fusion.5
  5.4 0.0 copy-start.1
  5.4 0.1 collective-permute-start.1
  5.5 0.6 %copy-done.1 = s32[128]{0:T(128)S(1)} copy-done((s32[128]{0:T(128)S(1)}, s32[128]{0:T(128)}, u32[]{:S(2)}) %copy-start.1) | copy-done | bytes 536
  6.0 1.5 %collective-permute-start.2 = (s32[1,128]{1,0:T(1,128)S(1)}, s32[1,128]{1,0:T(1,128)S(1)}, u32[]{:S(2)}, u32[]{:S(2)}) collective-permute-start(s32[1,128]{1,0:T(1,128)S(1)} %bitcast.17), channel_id=1, source_target_pairs={{0,4},{1,5},{2,6},{3,7},{4,0},{5,1},{6,2},{7,3},{8,12},{9,13},{10,... | collective-permute-start | bytes 1544 | tf_op jit(solution)/shard_map/ppermute | solution.py:17
  7.6 0.0 copy-done.2
  7.6 0.0 copy-done.4
  7.6 0.2 fusion.1
  7.8 0.1 stack.35
  7.9 0.4 %collective-permute-done = f16[64,768]{1,0:T(8,128)(2,1)S(1)} collective-permute-done((f16[64,768]{1,0:T(8,128)(2,1)S(1)}, f16[64,768]{1,0:T(8,128)(2,1)S(1)}, u32[]{:S(2)}, u32[]{:S(2)}) %collective-permute-start) | collective-permute-done | bytes 98336 | tf_op jit(solution)/shard_map/ppermute | solution.py:17
  8.3 0.1 shard_map.77.refs_0_
  8.4 4.3 %collective-permute-start.4 = (bf16[64,768]{1,0:T(8,128)(2,1)S(1)}, bf16[64,768]{1,0:T(8,128)(2,1)S(1)}, u32[]{:S(2)}, u32[]{:S(2)}) collective-permute-start(bf16[64,768]{1,0:T(8,128)(2,1)S(1)} %shard_map.77.refs_0_), channel_id=1, source_target_pairs={{0,24},{1,25},{2,26},{3,27},{4,28},{5,29},{6,30},{7,31},{8,16},{9,... | collective-permute-start | bytes 294920 | tf_op jit(solution)/shard_map/ppermute | solution.py:17
  12.7 0.0 collective-permute-start.6
  12.7 0.6 %collective-permute-start.8 = (bf16[64,768]{1,0:T(8,128)(2,1)S(1)}, bf16[64,768]{1,0:T(8,128)(2,1)S(1)}, u32[]{:S(2)}, u32[]{:S(2)}) collective-permute-start(bf16[64,768]{1,0:T(8,128)(2,1)S(1)} %shard_map.77.refs_0_), channel_id=1, source_target_pairs={{0,8},{1,9},{2,10},{3,11},{4,12},{5,13},{6,14},{7,15},{8,0},{9,1},... | collective-permute-start | bytes 294920 | tf_op jit(solution)/shard_map/ppermute | solution.py:17
  13.4 0.0 collective-permute-done.1
  13.4 0.1 shard_map.78.refs_1_
  13.6 0.0 collective-permute-done.2.refs_4_
  13.6 1.7 %collective-permute-start.3 = (bf16[128,768]{1,0:T(8,128)(2,1)S(1)}, bf16[128,768]{1,0:T(8,128)(2,1)S(1)}, u32[]{:S(2)}, u32[]{:S(2)}) collective-permute-start(bf16[128,768]{1,0:T(8,128)(2,1)S(1)} %shard_map.78.refs_1_), channel_id=1, source_target_pairs={{0,4},{1,5},{2,6},{3,7},{4,0},{5,1},{6,2},{7,3},{8,12},{9,13},{10,... | collective-permute-start | bytes 589832 | tf_op jit(solution)/shard_map/ppermute | solution.py:17
  15.3 2.2 %collective-permute-done.8.refs_9_ = bf16[64,768]{1,0:T(8,128)(2,1)S(1)} collective-permute-done((bf16[64,768]{1,0:T(8,128)(2,1)S(1)}, bf16[64,768]{1,0:T(8,128)(2,1)S(1)}, u32[]{:S(2)}, u32[]{:S(2)}) %collective-permute-start.8) | collective-permute-done | bytes 98336 | tf_op jit(solution)/shard_map/ppermute | solution.py:17
  17.5 0.1 collective-permute-start.9
  17.6 0.0 collective-permute-done.4.refs_5_
  17.6 0.5 %collective-permute-start.5 = (bf16[64,768]{1,0:T(8,128)(2,1)S(1)}, bf16[64,768]{1,0:T(8,128)(2,1)S(1)}, u32[]{:S(2)}, u32[]{:S(2)}) collective-permute-start(bf16[64,768]{1,0:T(8,128)(2,1)S(1)} %collective-permute-done.4.refs_5_), channel_id=1, source_target_pairs={{0,2},{1,3},{2,0},{3,1},{4,6},{5,7},{6,4},{7,5},{8,10},{9,11},{10,... | collective-permute-start | bytes 294920 | tf_op jit(solution)/shard_map/ppermute | solution.py:17
  18.1 1.4 %collective-permute-done.6.refs_7_ = bf16[64,768]{1,0:T(8,128)(2,1)S(1)} collective-permute-done((bf16[64,768]{1,0:T(8,128)(2,1)S(1)}, bf16[64,768]{1,0:T(8,128)(2,1)S(1)}, u32[]{:S(2)}, u32[]{:S(2)}) %collective-permute-start.6) | collective-permute-done | bytes 98336 | tf_op jit(solution)/shard_map/ppermute | solution.py:17
  19.5 0.0 collective-permute-start.7
  19.5 0.1 iota_add_fusion
  20.2 0.1 add.50.id_ref
  20.3 0.0 collective-permute-done.5.refs_6_
  20.3 0.5 %collective-permute-done.7.refs_8_ = bf16[64,768]{1,0:T(8,128)(2,1)S(1)} collective-permute-done((bf16[64,768]{1,0:T(8,128)(2,1)S(1)}, bf16[64,768]{1,0:T(8,128)(2,1)S(1)}, u32[]{:S(2)}, u32[]{:S(2)}) %collective-permute-start.7) | collective-permute-done | bytes 98336 | tf_op jit(solution)/shard_map/ppermute | solution.py:17
  20.8 0.0 collective-permute-done.3.refs_2_
  20.8 0.0 collective-permute-done.9.refs_10_
  20.8 0.7 %shard_map.79 = (f32[2,256]{1,0:T(2,128)S(1)}, f32[2,256]{1,0:T(2,128)S(1)}, f32[2,128]{1,0:T(2,128)S(1)}, f32[2,128]{1,0:T(2,128)S(1)}) custom-call(f32[1,128]{1,0:T(1,128)S(1)} %broadcast_in_dim.14.scale_ref, s32[1,512]{1,0:T(1,128)S(1)} %add.50.id_ref, bf16[64,768]{1,0:T(8,128)(2,1)S(1)} %shard_map.77.refs_0_, bf16[128,768]{1,0:T(8,128)(2,1)S(1)} %shard_map.78.refs_1_, ...), custom_call_target="tpu_custom_call" | custom-call | flops 201326592 | bytes 1183232 | tf_op jit(solution)/shard_map/pallas_call | solution.py:91
  21.5 0.2 collective-permute-start.10
  21.7 1.3 %collective-permute-start.13 = (f32[2,128]{1,0:T(2,128)S(1)}, f32[2,128]{1,0:T(2,128)S(1)}, u32[]{:S(2)}, u32[]{:S(2)}) collective-permute-start(f32[2,128]{1,0:T(2,128)S(1)} %get-tuple-element.25), channel_id=1, source_target_pairs={{0,4},{1,5},{2,6},{3,7},{4,0},{5,1},{6,2},{7,3},{8,12},{9,13},{10,... | collective-permute-start | bytes 3080 | tf_op jit(solution)/shard_map/ppermute | solution.py:17
  23.0 0.0 collective-permute-done.10.refs_1_
  23.0 1.7 %collective-permute-start.11 = (f32[2,128]{1,0:T(2,128)S(1)}, f32[2,128]{1,0:T(2,128)S(1)}, u32[]{:S(2)}, u32[]{:S(2)}) collective-permute-start(f32[2,128]{1,0:T(2,128)S(1)} %get-tuple-element.21), channel_id=1, source_target_pairs={{0,16},{1,17},{2,18},{3,19},{4,20},{5,21},{6,22},{7,23},{8,24},{9,... | collective-permute-start | bytes 3080 | tf_op jit(solution)/shard_map/ppermute | solution.py:17
  24.7 0.6 %collective-permute-done.13.refs_1_ = f32[2,128]{1,0:T(2,128)S(1)} collective-permute-done((f32[2,128]{1,0:T(2,128)S(1)}, f32[2,128]{1,0:T(2,128)S(1)}, u32[]{:S(2)}, u32[]{:S(2)}) %collective-permute-start.13) | collective-permute-done | bytes 1056 | tf_op jit(solution)/shard_map/ppermute | solution.py:17
  25.3 1.3 %collective-permute-start.14 = (f32[2,128]{1,0:T(2,128)S(1)}, f32[2,128]{1,0:T(2,128)S(1)}, u32[]{:S(2)}, u32[]{:S(2)}) collective-permute-start(f32[2,128]{1,0:T(2,128)S(1)} %shard_map.82.refs_2_), channel_id=1, source_target_pairs={{0,1},{1,0},{2,3},{3,2},{4,5},{5,4},{6,7},{7,6},{8,9},{9,8},{10,11... | collective-permute-start | bytes 3080 | tf_op jit(solution)/shard_map/ppermute | solution.py:17
  26.6 0.9 %collective-permute-done.11.refs_1_ = f32[2,128]{1,0:T(2,128)S(1)} collective-permute-done((f32[2,128]{1,0:T(2,128)S(1)}, f32[2,128]{1,0:T(2,128)S(1)}, u32[]{:S(2)}, u32[]{:S(2)}) %collective-permute-start.11) | collective-permute-done | bytes 1056 | tf_op jit(solution)/shard_map/ppermute | solution.py:17
  27.5 0.1 shard_map.81
  27.6 1.1 %collective-permute-start.12 = (f32[2,64]{1,0:T(2,128)S(1)}, f32[2,64]{1,0:T(2,128)S(1)}, u32[]{:S(2)}, u32[]{:S(2)}) collective-permute-start(f32[2,64]{1,0:T(2,128)S(1)} %get-tuple-element.23), channel_id=1, source_target_pairs={{0,8},{1,9},{2,10},{3,11},{4,12},{5,13},{6,14},{7,15},{8,0},{9,1},... | collective-permute-start | bytes 1544 | tf_op jit(solution)/shard_map/ppermute | solution.py:17
  28.7 0.2 collective-permute-done.14.refs_3_
  29.0 2.2 %collective-permute-done.12.refs_1_ = f32[2,64]{1,0:T(2,128)S(1)} collective-permute-done((f32[2,64]{1,0:T(2,128)S(1)}, f32[2,64]{1,0:T(2,128)S(1)}, u32[]{:S(2)}, u32[]{:S(2)}) %collective-permute-start.12) | collective-permute-done | bytes 544 | tf_op jit(solution)/shard_map/ppermute | solution.py:17
  31.2 0.5 %shard_map.83 = (f32[1,64]{1,0:T(1,128)}, f32[1,128]{1,0:T(1,128)}) custom-call(f32[2,64]{1,0:T(2,128)S(1)} %get-tuple-element.22.refs_0_, f32[2,64]{1,0:T(2,128)S(1)} %collective-permute-done.12.refs_1_, f32[2,128]{1,0:T(2,128)S(1)} %shard_map.82.refs_2_, f32[2,128]{1,0:T(2,128)S(1)} %collective-permute-done.14.refs_3_), custom_call_target="tpu_custom_call" | custom-call | tf_op jit(solution)/shard_map/pallas_call | solution.py:131
  (7 shorter events, 0.1 us)
Async XLA Ops:
  0.6 4.5 %copy-start = (bf16[512,768]{1,0:T(8,128)(2,1)S(1)}, bf16[512,768]{1,0:T(8,128)(2,1)}, u32[]{:S(2)}) copy-start(bf16[512,768]{1,0:T(8,128)(2,1)} %param.7) | copy-start | bytes 2359300
  0.7 4.4 %copy-start.3 = (bf16[128,512]{1,0:T(8,128)(2,1)S(1)}, bf16[128,512]{1,0:T(8,128)(2,1)}, u32[]{:S(2)}) copy-start(bf16[128,512]{1,0:T(8,128)(2,1)} %param.6) | copy-start | bytes 393220
  2.1 5.5 %copy-start.2 = (bf16[384,768]{1,0:T(8,128)(2,1)S(1)}, bf16[384,768]{1,0:T(8,128)(2,1)}, u32[]{:S(2)}) copy-start(bf16[384,768]{1,0:T(8,128)(2,1)} %param.9) | copy-start | bytes 1769476
  2.1 5.5 %copy-start.4 = (bf16[128,384]{1,0:T(8,128)(2,1)S(1)}, bf16[128,384]{1,0:T(8,128)(2,1)}, u32[]{:S(2)}) copy-start(bf16[128,384]{1,0:T(8,128)(2,1)} %param.8) | copy-start | bytes 294916
  2.1 6.2 %collective-permute-start = (f16[64,768]{1,0:T(8,128)(2,1)S(1)}, f16[64,768]{1,0:T(8,128)(2,1)S(1)}, u32[]{:S(2)}, u32[]{:S(2)}) collective-permute-start(f16[64,768]{1,0:T(8,128)(2,1)S(1)} %convolution_convert_fusion), channel_id=1, source_target_pairs={{0,1},{1,0},{2,3},{3,2},{4,5},{5,4},{6,7},{7,6},{8,9},{9,8},{10,11... | collective-permute-start | bytes 294920 | tf_op jit(solution)/shard_map/ppermute | solution.py:17
  5.4 0.7 %copy-start.1 = (s32[128]{0:T(128)S(1)}, s32[128]{0:T(128)}, u32[]{:S(2)}) copy-start(s32[128]{0:T(128)} %param.10) | copy-start | bytes 1540
  5.4 8.0 %collective-permute-start.1 = (f16[128,768]{1,0:T(8,128)(2,1)S(1)}, f16[128,768]{1,0:T(8,128)(2,1)S(1)}, u32[]{:S(2)}, u32[]{:S(2)}) collective-permute-start(f16[128,768]{1,0:T(8,128)(2,1)S(1)} %get-tuple-element.28), channel_id=1, source_target_pairs={{0,1},{1,0},{2,3},{3,2},{4,5},{5,4},{6,7},{7,6},{8,9},{9,8},{10,11... | collective-permute-start | bytes 589832 | tf_op jit(solution)/shard_map/ppermute | solution.py:17
  6.0 7.5 %collective-permute-start.2 = (s32[1,128]{1,0:T(1,128)S(1)}, s32[1,128]{1,0:T(1,128)S(1)}, u32[]{:S(2)}, u32[]{:S(2)}) collective-permute-start(s32[1,128]{1,0:T(1,128)S(1)} %bitcast.17), channel_id=1, source_target_pairs={{0,4},{1,5},{2,6},{3,7},{4,0},{5,1},{6,2},{7,3},{8,12},{9,13},{10,... | collective-permute-start | bytes 1544 | tf_op jit(solution)/shard_map/ppermute | solution.py:17
  8.4 9.2 %collective-permute-start.4 = (bf16[64,768]{1,0:T(8,128)(2,1)S(1)}, bf16[64,768]{1,0:T(8,128)(2,1)S(1)}, u32[]{:S(2)}, u32[]{:S(2)}) collective-permute-start(bf16[64,768]{1,0:T(8,128)(2,1)S(1)} %shard_map.77.refs_0_), channel_id=1, source_target_pairs={{0,24},{1,25},{2,26},{3,27},{4,28},{5,29},{6,30},{7,31},{8,16},{9,... | collective-permute-start | bytes 294920 | tf_op jit(solution)/shard_map/ppermute | solution.py:17
  12.7 6.8 %collective-permute-start.6 = (bf16[64,768]{1,0:T(8,128)(2,1)S(1)}, bf16[64,768]{1,0:T(8,128)(2,1)S(1)}, u32[]{:S(2)}, u32[]{:S(2)}) collective-permute-start(bf16[64,768]{1,0:T(8,128)(2,1)S(1)} %shard_map.77.refs_0_), channel_id=1, source_target_pairs={{0,16},{1,17},{2,18},{3,19},{4,20},{5,21},{6,22},{7,23},{8,24},{9,... | collective-permute-start | bytes 294920 | tf_op jit(solution)/shard_map/ppermute | solution.py:17
  12.7 4.8 %collective-permute-start.8 = (bf16[64,768]{1,0:T(8,128)(2,1)S(1)}, bf16[64,768]{1,0:T(8,128)(2,1)S(1)}, u32[]{:S(2)}, u32[]{:S(2)}) collective-permute-start(bf16[64,768]{1,0:T(8,128)(2,1)S(1)} %shard_map.77.refs_0_), channel_id=1, source_target_pairs={{0,8},{1,9},{2,10},{3,11},{4,12},{5,13},{6,14},{7,15},{8,0},{9,1},... | collective-permute-start | bytes 294920 | tf_op jit(solution)/shard_map/ppermute | solution.py:17
  13.6 7.2 %collective-permute-start.3 = (bf16[128,768]{1,0:T(8,128)(2,1)S(1)}, bf16[128,768]{1,0:T(8,128)(2,1)S(1)}, u32[]{:S(2)}, u32[]{:S(2)}) collective-permute-start(bf16[128,768]{1,0:T(8,128)(2,1)S(1)} %shard_map.78.refs_1_), channel_id=1, source_target_pairs={{0,4},{1,5},{2,6},{3,7},{4,0},{5,1},{6,2},{7,3},{8,12},{9,13},{10,... | collective-permute-start | bytes 589832 | tf_op jit(solution)/shard_map/ppermute | solution.py:17
  17.5 3.3 %collective-permute-start.9 = (bf16[128,768]{1,0:T(8,128)(2,1)S(1)}, bf16[128,768]{1,0:T(8,128)(2,1)S(1)}, u32[]{:S(2)}, u32[]{:S(2)}) collective-permute-start(bf16[128,768]{1,0:T(8,128)(2,1)S(1)} %pad_maximum_fusion), channel_id=1, source_target_pairs={{0,2},{1,3},{2,0},{3,1},{4,6},{5,7},{6,4},{7,5},{8,10},{9,11},{10,... | collective-permute-start | bytes 589832 | tf_op jit(solution)/shard_map/ppermute | solution.py:17
  17.6 2.7 %collective-permute-start.5 = (bf16[64,768]{1,0:T(8,128)(2,1)S(1)}, bf16[64,768]{1,0:T(8,128)(2,1)S(1)}, u32[]{:S(2)}, u32[]{:S(2)}) collective-permute-start(bf16[64,768]{1,0:T(8,128)(2,1)S(1)} %collective-permute-done.4.refs_5_), channel_id=1, source_target_pairs={{0,2},{1,3},{2,0},{3,1},{4,6},{5,7},{6,4},{7,5},{8,10},{9,11},{10,... | collective-permute-start | bytes 294920 | tf_op jit(solution)/shard_map/ppermute | solution.py:17
  19.5 1.3 %collective-permute-start.7 = (bf16[64,768]{1,0:T(8,128)(2,1)S(1)}, bf16[64,768]{1,0:T(8,128)(2,1)S(1)}, u32[]{:S(2)}, u32[]{:S(2)}) collective-permute-start(bf16[64,768]{1,0:T(8,128)(2,1)S(1)} %collective-permute-done.6.refs_7_), channel_id=1, source_target_pairs={{0,2},{1,3},{2,0},{3,1},{4,6},{5,7},{6,4},{7,5},{8,10},{9,11},{10,... | collective-permute-start | bytes 294920 | tf_op jit(solution)/shard_map/ppermute | solution.py:17
  21.5 1.4 %collective-permute-start.10 = (f32[2,256]{1,0:T(2,128)S(1)}, f32[2,256]{1,0:T(2,128)S(1)}, u32[]{:S(2)}, u32[]{:S(2)}) collective-permute-start(f32[2,256]{1,0:T(2,128)S(1)} %get-tuple-element.19), channel_id=1, source_target_pairs={{0,2},{1,3},{2,0},{3,1},{4,6},{5,7},{6,4},{7,5},{8,10},{9,11},{10,... | collective-permute-start | bytes 6152 | tf_op jit(solution)/shard_map/ppermute | solution.py:17
  21.7 3.6 %collective-permute-start.13 = (f32[2,128]{1,0:T(2,128)S(1)}, f32[2,128]{1,0:T(2,128)S(1)}, u32[]{:S(2)}, u32[]{:S(2)}) collective-permute-start(f32[2,128]{1,0:T(2,128)S(1)} %get-tuple-element.25), channel_id=1, source_target_pairs={{0,4},{1,5},{2,6},{3,7},{4,0},{5,1},{6,2},{7,3},{8,12},{9,13},{10,... | collective-permute-start | bytes 3080 | tf_op jit(solution)/shard_map/ppermute | solution.py:17
  23.0 4.5 %collective-permute-start.11 = (f32[2,128]{1,0:T(2,128)S(1)}, f32[2,128]{1,0:T(2,128)S(1)}, u32[]{:S(2)}, u32[]{:S(2)}) collective-permute-start(f32[2,128]{1,0:T(2,128)S(1)} %get-tuple-element.21), channel_id=1, source_target_pairs={{0,16},{1,17},{2,18},{3,19},{4,20},{5,21},{6,22},{7,23},{8,24},{9,... | collective-permute-start | bytes 3080 | tf_op jit(solution)/shard_map/ppermute | solution.py:17
  25.3 3.6 %collective-permute-start.14 = (f32[2,128]{1,0:T(2,128)S(1)}, f32[2,128]{1,0:T(2,128)S(1)}, u32[]{:S(2)}, u32[]{:S(2)}) collective-permute-start(f32[2,128]{1,0:T(2,128)S(1)} %shard_map.82.refs_2_), channel_id=1, source_target_pairs={{0,1},{1,0},{2,3},{3,2},{4,5},{5,4},{6,7},{7,6},{8,9},{9,8},{10,11... | collective-permute-start | bytes 3080 | tf_op jit(solution)/shard_map/ppermute | solution.py:17
  27.6 3.6 %collective-permute-start.12 = (f32[2,64]{1,0:T(2,128)S(1)}, f32[2,64]{1,0:T(2,128)S(1)}, u32[]{:S(2)}, u32[]{:S(2)}) collective-permute-start(f32[2,64]{1,0:T(2,128)S(1)} %get-tuple-element.23), channel_id=1, source_target_pairs={{0,8},{1,9},{2,10},{3,11},{4,12},{5,13},{6,14},{7,15},{8,0},{9,1},... | collective-permute-start | bytes 1544 | tf_op jit(solution)/shard_map/ppermute | solution.py:17
